TPU v7x, 768 devices: a whole 4x8x12 slice. The times are simulated.
768 devices in a mesh: dp: 48 (over x, z), tensor: 16 (over y, core).
Axes of the slice: x: 4, y: 8, z: 12, core: 2. Of those that a mesh axis runs over, the one named last changes fastest.
Arguments:
- lengths: int32 [144], replicated, may hold values from 0 to 1536, as said below
- queries: bfloat16 [18432, 8192], P('dp', 'tensor'), may hold values from -6 to 6
- keys: bfloat16 [18432, 1024], P('dp'), may hold values from -6 to 6
- values: bfloat16 [18432, 1024], P('dp'), may hold values from -6 to 6
- out_weight: bfloat16 [8192, 8192], P('tensor'), may hold values from -0.29882812 to 0.29882812
Outputs:
- projected: bfloat16 [18432, 8192], P('dp', 'tensor')
Inputs may be any that keep to these rules, and one draw needn't show every extreme that they name: `lengths`: entries are multiples of 128; the positive ones come first and sum to 18432, zeros follow; one entry equals 1536.
All inputs are finite; a program needn't handle non-finite values.
Results may differ from a plain program's by a relative error of at most 0.023.
Values may be sent and summed in bfloat16 or wider, within the bound.
No kernel may reach another device: no remote copies, remote signals or barrier semaphores. Data moves between devices by JAX's collectives and lax.ppermute only.
A program may use at most 64 MiB of HBM per device.

v0:
```python
import jax
import jax.numpy as jnp
from jax import lax
from jax.sharding import PartitionSpec as P

HQ = 64
KVH = 8
HD = 128
SPANCAP = 4


def from_behind(value, axis, steps):
    count = lax.axis_size(axis)
    first, last = (max(0, -steps), min(count, count - steps))
    return lax.ppermute(value, axis, [(source, source + steps) for source in range(first, last)])


def doc_index(positions, lengths):
    ends = jnp.cumsum(lengths)
    return jnp.sum((ends[None, :] <= positions[:, None]).astype(jnp.int32), axis=1)


def on_device(lengths, queries, keys, values, out_weight):
    tok_rows = queries.shape[0]
    dp_count = lax.axis_size("dp")
    heads_dev = queries.shape[1] // HD
    group = HQ // KVH
    kv_dev = max(1, heads_dev // group)
    span = min(SPANCAP, dp_count // 2)
    kv_start = lax.axis_index("tensor") * heads_dev // group
    own_keys = lax.dynamic_slice_in_dim(keys, kv_start * HD, kv_dev * HD, 1)
    own_vals = lax.dynamic_slice_in_dim(values, kv_start * HD, kv_dev * HD, 1)
    own_pair = jnp.stack([own_keys, own_vals])
    pieces = [own_pair]
    for step in range(1, span + 1):
        pieces.insert(0, from_behind(own_pair, "dp", step))
    window = jnp.stack(pieces)
    dp_index = lax.axis_index("dp")
    q_pos = dp_index * tok_rows + jnp.arange(tok_rows, dtype=jnp.int32)
    q_doc = doc_index(q_pos, lengths)
    q_heads = queries.reshape(tok_rows, heads_dev, HD)
    scale = 1.0 / HD**0.5
    repeat_by = heads_dev // kv_dev

    def absorb(carry, inputs):
        pair_block, offset = inputs
        k_pos = (dp_index - span + offset) * tok_rows + jnp.arange(tok_rows, dtype=jnp.int32)
        k_doc = doc_index(jnp.maximum(k_pos, 0), lengths)
        allowed = (
            (k_pos[None, :] <= q_pos[:, None])
            & (k_pos[None, :] >= 0)
            & (k_doc[None, :] == q_doc[:, None])
        )
        running, total, accum = carry
        k_heads = jnp.repeat(pair_block[0].reshape(tok_rows, kv_dev, HD), repeat_by, axis=1)
        v_heads = jnp.repeat(pair_block[1].reshape(tok_rows, kv_dev, HD), repeat_by, axis=1)
        scores = (
            jnp.einsum("qhd,khd->hqk", q_heads, k_heads, preferred_element_type=jnp.float32) * scale
        )
        masked = jnp.where(allowed[None], scores, -1e30)
        fresh = jnp.maximum(running, jnp.max(masked, axis=-1))
        factor = jnp.exp(running - fresh)
        weights = jnp.where(allowed[None], jnp.exp(scores - fresh[:, :, None]), 0.0)
        total = total * factor + jnp.sum(weights, axis=-1)
        update = jnp.einsum(
            "hqk,khd->qhd",
            weights.astype(jnp.bfloat16),
            v_heads,
            preferred_element_type=jnp.float32,
        )
        accum = accum * jnp.transpose(factor)[:, :, None] + update
        carry = (fresh, total, accum)
        return (carry, None)

    start_state = (
        jnp.full((heads_dev, tok_rows), -1e30, jnp.float32),
        jnp.zeros((heads_dev, tok_rows), jnp.float32),
        jnp.zeros((tok_rows, heads_dev, HD), jnp.float32),
    )
    final_state, unused = lax.scan(
        absorb, start_state, (window, jnp.arange(span + 1, dtype=jnp.int32))
    )
    attended = (final_state[2] / jnp.transpose(final_state[1])[:, :, None]).astype(jnp.bfloat16)
    partial_value = jnp.dot(
        attended.reshape(tok_rows, heads_dev * HD), out_weight, preferred_element_type=jnp.float32
    )
    return lax.psum_scatter(
        partial_value.astype(jnp.bfloat16), "tensor", scatter_dimension=1, tiled=True
    )


def solution(mesh):
    placed = (P(), P("dp", "tensor"), P("dp", None), P("dp", None), P("tensor", None))
    return jax.shard_map(
        on_device, mesh=mesh, in_specs=placed, out_specs=P("dp", "tensor"), check_vma=False
    )
```

profile of v0, /device:TPU:31, one launch (start us, length us, event | category | flops | bytes accessed | tf_op | source)
XLA Modules:
  0.0 174.3 jit_solution(16910051688030837536)
XLA Ops:
  6.5 1.0 constant_dynamic-slice_fusion
  7.8 4.0 %collective-permute-start.3 = (bf16[2,384,128]{1,2,0:T(8,128)(2,1)S(1)}, bf16[2,384,128]{1,2,0:T(8,128)(2,1)S(1)}, u32[]{:S(2)}, u32[]{:S(2)}) collective-permute-start(bf16[2,384,128]{1,2,0:T(8,128)(2,1)S(1)} %pad_maximum_fusion), channel_id=1, source_target_pairs={{0,16},{16,32},{32,48},{48,64},{64,80},{80,96},{96,112},{112,128},... | collective-permute-start | bytes 589832 | tf_op jit(solution)/shard_map/ppermute | solution.py:15
  11.8 5.8 %collective-permute-start.2 = (bf16[2,384,128]{1,2,0:T(8,128)(2,1)S(1)}, bf16[2,384,128]{1,2,0:T(8,128)(2,1)S(1)}, u32[]{:S(2)}, u32[]{:S(2)}) collective-permute-start(bf16[2,384,128]{1,2,0:T(8,128)(2,1)S(1)} %pad_maximum_fusion), channel_id=1, source_target_pairs={{0,32},{16,48},{32,64},{48,80},{64,96},{80,112},{96,128},{112,144}... | collective-permute-start | bytes 589832 | tf_op jit(solution)/shard_map/ppermute | solution.py:15
  17.6 8.8 %collective-permute-start.1 = (bf16[2,384,128]{1,2,0:T(8,128)(2,1)S(1)}, bf16[2,384,128]{1,2,0:T(8,128)(2,1)}, u32[]{:S(2)}, u32[]{:S(2)}) collective-permute-start(bf16[2,384,128]{1,2,0:T(8,128)(2,1)S(1)} %pad_maximum_fusion), channel_id=1, source_target_pairs={{0,48},{16,64},{32,80},{48,96},{64,112},{80,128},{96,144},{112,160... | collective-permute-start | bytes 589832 | tf_op jit(solution)/shard_map/ppermute | solution.py:15
  26.5 6.4 %collective-permute-start = (bf16[2,384,128]{1,2,0:T(8,128)(2,1)S(1)}, bf16[2,384,128]{1,2,0:T(8,128)(2,1)}, u32[]{:S(2)}, u32[]{:S(2)}) collective-permute-start(bf16[2,384,128]{1,2,0:T(8,128)(2,1)S(1)} %pad_maximum_fusion), channel_id=1, source_target_pairs={{0,64},{16,80},{32,96},{48,112},{64,128},{80,144},{96,160},{112,17... | collective-permute-start | bytes 589832 | tf_op jit(solution)/shard_map/ppermute | solution.py:15
  33.0 0.7 pad_bitcast_fusion.1
  34.3 1.2 copy.20
  35.8 16.7 %collective-permute-done = bf16[2,384,128]{1,2,0:T(8,128)(2,1)} collective-permute-done((bf16[2,384,128]{1,2,0:T(8,128)(2,1)S(1)}, bf16[2,384,128]{1,2,0:T(8,128)(2,1)}, u32[]{:S(2)}, u32[]{:S(2)}) %collective-permute-start) | collective-permute-done | bytes 196640 | tf_op jit(solution)/shard_map/ppermute | solution.py:15
  52.6 0.9 bitcast_dynamic-update-slice_fusion.4
  53.5 1.0 bitcast_dynamic-update-slice_fusion.3
  54.6 22.5 %while.17 = (s32[]{:T(128)}, f32[4,384]{1,0:T(4,128)S(1)}, f32[4,384]{1,0:T(4,128)S(1)}, f32[384,4,128]{0,2,1:T(8,128)S(1)}, s32[5]{0:T(128)S(1)}, /*index=5*/s3...) while((s32[]{:T(128)}, f32[4,384]{1,0:T(4,128)S(1)}, ...), condition=%wide.region_9.10_spmd.clone, body=%wide.region_3.0_spmd.clone.sunk | while | flops 309867008 | bytes 10539689 | solution.py:80
  54.7 0.7 dynamic_slice.25
  58.3 0.8 fusion.41
  59.2 0.7 dynamic_slice.25
  62.8 0.8 fusion.41
  63.7 0.7 dynamic_slice.25
  67.3 0.8 fusion.41
  68.1 0.7 dynamic_slice.25
  70.7 0.6 fusion.37
  71.8 0.8 fusion.41
  72.6 0.7 dynamic_slice.25
  76.3 0.8 fusion.41
  77.2 9.5 %convolution_convert_fusion = bf16[384,8192]{1,0:T(8,128)(2,1)} fusion(bf16[384,512]{0,1:T(8,128)(2,1)S(1)} %bitcast.76, bf16[512,8192]{1,0:T(8,128)(2,1)} %param.11), kind=kOutput, calls=%fused_computation.35 | convolution fusion | flops 3224371200 | bytes 15073280 | tf_op jit(solution)/shard_map/dot_general | solution.py:84
  86.7 80.7 %reduce-scatter.2.cloned.1.call-done = bf16[384,512]{1,0:T(8,128)(2,1)} async-done(((bf16[384,8192]{1,0:T(8,128)(2,1)}), bf16[384,512]{1,0:T(8,128)(2,1)}) %reduce-scatter.2.cloned.1.call-update) | async-done | bytes 393232 | tf_op jit(solution)/shard_map/reduce_scatter | solution.py:87
  (115 shorter events, 12.1 us)
Async XLA Ops:
  6.5 161.0 %reduce-scatter.2.cloned.1.call-start = ((), (), s32[]{:S(2)}) async-start(), calls=%async_computation.1 | async-start | bytes 6684672 | tf_op jit(solution)/shard_map/reduce_scatter | solution.py:87
  6.5 48.1 %copy-start = (s32[144]{0:T(256)S(1)}, s32[144]{0:T(256)}, u32[]{:S(2)}) copy-start(s32[144]{0:T(256)} %param.7) | copy-start | bytes 1732
  7.8 46.7 %collective-permute-start.3 = (bf16[2,384,128]{1,2,0:T(8,128)(2,1)S(1)}, bf16[2,384,128]{1,2,0:T(8,128)(2,1)S(1)}, u32[]{:S(2)}, u32[]{:S(2)}) collective-permute-start(bf16[2,384,128]{1,2,0:T(8,128)(2,1)S(1)} %pad_maximum_fusion), channel_id=1, source_target_pairs={{0,16},{16,32},{32,48},{48,64},{64,80},{80,96},{96,112},{112,128},... | collective-permute-start | bytes 589832 | tf_op jit(solution)/shard_map/ppermute | solution.py:15
  11.8 42.7 %collective-permute-start.2 = (bf16[2,384,128]{1,2,0:T(8,128)(2,1)S(1)}, bf16[2,384,128]{1,2,0:T(8,128)(2,1)S(1)}, u32[]{:S(2)}, u32[]{:S(2)}) collective-permute-start(bf16[2,384,128]{1,2,0:T(8,128)(2,1)S(1)} %pad_maximum_fusion), channel_id=1, source_target_pairs={{0,32},{16,48},{32,64},{48,80},{64,96},{80,112},{96,128},{112,144}... | collective-permute-start | bytes 589832 | tf_op jit(solution)/shard_map/ppermute | solution.py:15
  17.6 35.9 %collective-permute-start.1 = (bf16[2,384,128]{1,2,0:T(8,128)(2,1)S(1)}, bf16[2,384,128]{1,2,0:T(8,128)(2,1)}, u32[]{:S(2)}, u32[]{:S(2)}) collective-permute-start(bf16[2,384,128]{1,2,0:T(8,128)(2,1)S(1)} %pad_maximum_fusion), channel_id=1, source_target_pairs={{0,48},{16,64},{32,80},{48,96},{64,112},{80,128},{96,144},{112,160... | collective-permute-start | bytes 589832 | tf_op jit(solution)/shard_map/ppermute | solution.py:15
  26.5 26.1 %collective-permute-start = (bf16[2,384,128]{1,2,0:T(8,128)(2,1)S(1)}, bf16[2,384,128]{1,2,0:T(8,128)(2,1)}, u32[]{:S(2)}, u32[]{:S(2)}) collective-permute-start(bf16[2,384,128]{1,2,0:T(8,128)(2,1)S(1)} %pad_maximum_fusion), channel_id=1, source_target_pairs={{0,64},{16,80},{32,96},{48,112},{64,128},{80,144},{96,160},{112,17... | collective-permute-start | bytes 589832 | tf_op jit(solution)/shard_map/ppermute | solution.py:15
Sparse Core Ops, SparseCore 0:
  86.9 80.5 reduce-scatter.1
where the time goes:
time: 175 us; the launch traced here: 174 us
  waiting for transfers between devices  97.5 us (56%)
  starting transfers between devices  25.1 us (14%)
  matrix products  16.4 us (9%)
  between operations  13.6 us (8%)
  local copies, waits for them, and re-layouts  10.6 us (6%)
  other arithmetic  7.27 us (4%)
  loops' own time  3.92 us (2%)
    reduce_scatter x1, waiting for transfers between devices, on_device(): lax.psum_scatter(partial_value.astype(jnp.bfloat16), 'tensor', scatter_di...  80.7 us
    ppermute x4, starting transfers between devices, from_behind(): lax.ppermute(value, axis, [(source, source + steps) for source in range(f...  25.1 us
    ppermute x4, waiting for transfers between devices, from_behind(): lax.ppermute(value, axis, [(source, source + steps) for source in range(f...  16.8 us
    dot_general x1, matrix products, on_device(): jnp.dot(attended.reshape(tok_rows, heads_dev * HD), out_weight, preferred...  9.51 us
    dot_general x5, matrix products, absorb(): jnp.einsum('hqk,khd->qhd', weights.astype(jnp.bfloat16), v_heads, preferr...  3.94 us
    another operation x1, loops' own time, on_device(): lax.scan(absorb, start_state, (window, jnp.arange(span + 1, dtype=jnp.int...  3.92 us
  transfers between devices with their start and end apart: 5, of which 2 were waited for; matrix products, arithmetic and copies ran while one was open for 3% of the time, Pallas kernels for 0%

commit v1 on v0

v1 whole, which is shorter than its diff:
```python
import functools
import math

import jax
import jax.numpy as jnp
from jax import lax
from jax.experimental import pallas as pl
from jax.experimental.pallas import tpu as pltpu
from jax.sharding import Mesh, PartitionSpec as P

HD = 128
UNIT = 128
NEG = -1e30
EXP_SCALE = math.log2(math.e) / HD**0.5
ROW_PARTS = 1

FIRST_BACK = (1, 3)
SECOND_BACK = (2, 4)


def block_bias(allowed):
    return jnp.where(allowed, 0.0, NEG).astype(jnp.float32)


def head_pair(q_refs, pair, unit):
    q_ref = q_refs[pair // 2]
    rows = pl.ds(unit * UNIT, UNIT)
    first = (pair % 2) * 2 * HD
    return jnp.concatenate([q_ref[rows, first : first + HD], q_ref[rows, first + HD : first + 2 * HD]], axis=0)


def raw_scores(k_rows, q_pair):
    return lax.dot_general(k_rows, q_pair, (((1,), (1,)), ((), ())), preferred_element_type=jnp.float32)


def weighted(v_rows, weights):
    return lax.dot_general(
        v_rows, weights.astype(jnp.bfloat16), (((0,), (0,)), ((), ())), preferred_element_type=jnp.float32
    )


def store_state(out_ref, pair, unit, top, total, accum):
    heads = 8
    cols = pl.ds(unit * UNIT, UNIT)
    for side in range(2):
        head = 2 * pair + side
        part = slice(side * UNIT, (side + 1) * UNIT)
        out_ref[pl.ds(head * HD, HD), cols] = accum[:, part]
        out_ref[pl.ds(heads * HD + head, 1), cols] = top[:, part]
        out_ref[pl.ds(heads * HD + heads + head, 1), cols] = total[:, part]


def load_state(ref, pair, unit):
    heads = 8
    cols = pl.ds(unit * UNIT, UNIT)
    both = []
    for base, size in ((heads * HD, 1), (heads * HD + heads, 1), (0, HD)):
        halves = [ref[pl.ds(base + (2 * pair + side) * size, size), cols] for side in range(2)]
        both.append(jnp.concatenate(halves, axis=1))
    return both


def piece_bias(info_ref, unit, back, units):
    low = info_ref[unit]
    return [block_bias(low <= block - units * back) for block in range(units)]


def attend_first(info_ref, qm_ref, qo_ref, own_ref, piece_ref, out_ref):
    units = qm_ref.shape[0] // UNIT
    core = info_ref[units + 2]
    triangle = lax.broadcasted_iota(jnp.int32, (UNIT, 2 * UNIT), 0) <= (
        lax.broadcasted_iota(jnp.int32, (UNIT, 2 * UNIT), 1) % UNIT
    )
    for unit in range(units):
        bias = piece_bias(info_ref, unit, info_ref[units], units)
        low = info_ref[unit]
        own_bias = [block_bias((low <= block) & (core == 0)) for block in range(unit + 1)]
        for pair in range(4):
            q_pair = head_pair((qm_ref, qo_ref), pair, unit)
            s = raw_scores(piece_ref[:, :HD], q_pair)
            blocks = [s[b * UNIT : (b + 1) * UNIT] + bias[b] for b in range(units)]
            span = (unit + 1) * UNIT
            s = raw_scores(own_ref[:span, :HD], q_pair)
            for b in range(unit + 1):
                block = s[b * UNIT : (b + 1) * UNIT] + own_bias[b]
                blocks.append(jnp.where(triangle, block, NEG) if b == unit else block)
            scores = jnp.concatenate(blocks, axis=0)
            top = jnp.max(scores, axis=0, keepdims=True)
            weights = jnp.exp2((scores - top) * EXP_SCALE)
            total = jnp.sum(weights, axis=0, keepdims=True)
            rows = units * UNIT
            accum = weighted(piece_ref[:, HD:], weights[:rows]) + weighted(own_ref[:span, HD:], weights[rows:])
            store_state(out_ref, pair, unit, top, total, accum)


def attend_second(info_ref, qm_ref, qo_ref, piece_ref, state_ref, out_ref):
    units = qm_ref.shape[0] // UNIT
    for unit in range(units):
        bias = piece_bias(info_ref, unit, info_ref[units + 1], units)
        for pair in range(4):
            q_pair = head_pair((qm_ref, qo_ref), pair, unit)
            s = raw_scores(piece_ref[:, :HD], q_pair)
            scores = jnp.concatenate([s[b * UNIT : (b + 1) * UNIT] + bias[b] for b in range(units)], axis=0)
            old_top, old_total, old_accum = load_state(state_ref, pair, unit)
            top = jnp.maximum(old_top, jnp.max(scores, axis=0, keepdims=True))
            weights = jnp.exp2((scores - top) * EXP_SCALE)
            factor = jnp.exp2((old_top - top) * EXP_SCALE)
            total = old_total * factor + jnp.sum(weights, axis=0, keepdims=True)
            accum = old_accum * factor + weighted(piece_ref[:, HD:], weights)
            store_state(out_ref, pair, unit, top, total, accum)


def combine(here_ref, there_ref, out_ref):
    heads = 8
    for head in range(heads):
        other = (head + heads // 2) % heads
        top_a = here_ref[pl.ds(heads * HD + head, 1), :]
        top_b = there_ref[pl.ds(heads * HD + other, 1), :]
        top = jnp.maximum(top_a, top_b)
        share_a = jnp.exp2((top_a - top) * EXP_SCALE)
        share_b = jnp.exp2((top_b - top) * EXP_SCALE)
        total = (
            here_ref[pl.ds(heads * HD + heads + head, 1), :] * share_a
            + there_ref[pl.ds(heads * HD + heads + other, 1), :] * share_b
        )
        accum = here_ref[pl.ds(head * HD, HD), :] * share_a + there_ref[pl.ds(other * HD, HD), :] * share_b
        out_ref[:, head * HD : (head + 1) * HD] = jnp.transpose(accum / total).astype(jnp.bfloat16)


def project(columns_ref, att_ref, wm_ref, wo_ref, out_ref):
    del columns_ref
    depth = wm_ref.shape[0]
    summed = jnp.dot(att_ref[:, :depth], wm_ref[...], preferred_element_type=jnp.float32)
    summed += jnp.dot(att_ref[:, depth:], wo_ref[...], preferred_element_type=jnp.float32)
    out_ref[0] = summed.astype(jnp.bfloat16)


VM = pl.BlockSpec(memory_space=pltpu.VMEM)
SM = pl.BlockSpec(memory_space=pltpu.SMEM)
LIMIT = pltpu.CompilerParams(vmem_limit_bytes=32 * 1024 * 1024)


def on_device(lengths, queries, keys, values, out_weight):
    rows, wide = queries.shape
    units = rows // UNIT
    dp_count, y_count = lax.axis_size("dp"), lax.axis_size("y")
    dp, y, core = lax.axis_index("dp"), lax.axis_index("y"), lax.axis_index("core")
    swap = [(0, 1), (1, 0)]

    own = jnp.concatenate(
        [lax.dynamic_slice_in_dim(keys, y * HD, HD, 1), lax.dynamic_slice_in_dim(values, y * HD, HD, 1)], axis=1
    )
    first_pairs = [
        (2 * i + c, 2 * (i + FIRST_BACK[c]) + c) for c in range(2) for i in range(dp_count - FIRST_BACK[c])
    ]
    first = lax.ppermute(own, ("dp", "core"), first_pairs)
    q_other = lax.ppermute(queries, "core", swap)
    w_other = lax.ppermute(out_weight, "core", swap)
    second = lax.ppermute(first, "dp", [(i, i + 1) for i in range(dp_count - 1)])

    order = jnp.arange(lengths.shape[0], dtype=jnp.int32)
    ends = jnp.sum(jnp.where(order[None, :] <= order[:, None], lengths[None, :], 0), axis=1)
    q_starts = dp * rows + UNIT * jnp.arange(units, dtype=jnp.int32)
    doc_starts = jnp.max(jnp.where(ends[None, :] <= q_starts[:, None], ends[None, :], 0), axis=1)
    lows = doc_starts // UNIT - dp * units
    tail = jnp.stack([1 + 2 * core, 2 + 2 * core, core])
    info = jnp.concatenate([lows, tail]).astype(jnp.int32)

    state_shape = jax.ShapeDtypeStruct((2 * wide + 16, rows), jnp.float32)
    state = pl.pallas_call(
        attend_first,
        out_shape=state_shape,
        in_specs=[SM, VM, VM, VM, VM],
        out_specs=VM,
        compiler_params=LIMIT,
        cost_estimate=pl.CostEstimate(flops=1_200_000_000, bytes_accessed=4_000_000, transcendentals=2_000_000),
    )(info, queries, q_other, own, first)
    state = pl.pallas_call(
        attend_second,
        out_shape=state_shape,
        in_specs=[SM, VM, VM, VM, VM],
        out_specs=VM,
        compiler_params=LIMIT,
        cost_estimate=pl.CostEstimate(flops=600_000_000, bytes_accessed=4_000_000, transcendentals=1_000_000),
    )(info, queries, q_other, second, state)
    there = lax.ppermute(state, "core", swap)
    attended = pl.pallas_call(
        combine,
        out_shape=jax.ShapeDtypeStruct((rows, 2 * wide), jnp.bfloat16),
        in_specs=[VM, VM],
        out_specs=VM,
        compiler_params=LIMIT,
        cost_estimate=pl.CostEstimate(flops=2_000_000, bytes_accessed=4_000_000, transcendentals=10_000),
    )(state, there)

    def part(columns):
        count = columns.shape[0]
        return pl.pallas_call(
            project,
            out_shape=jax.ShapeDtypeStruct((count, rows, wide), jnp.bfloat16),
            grid_spec=pltpu.PrefetchScalarGridSpec(
                num_scalar_prefetch=1,
                grid=(count,),
                in_specs=[
                    pl.BlockSpec((rows, 2 * wide), lambda g, cols: (0, 0)),
                    pl.BlockSpec((wide, wide), lambda g, cols: (0, cols[g])),
                    pl.BlockSpec((wide, wide), lambda g, cols: (0, cols[g])),
                ],
                out_specs=pl.BlockSpec((1, rows, wide), lambda g, cols: (g, 0, 0)),
            ),
            compiler_params=LIMIT,
            cost_estimate=pl.CostEstimate(
                flops=4 * rows * wide * wide * count, bytes_accessed=3_000_000 * count, transcendentals=0
            ),
        )(columns, attended, out_weight, w_other)

    half = y_count // 2
    way = 1 - 2 * core

    def columns_at(distance):
        chunk = jnp.mod(y + way * distance, y_count)
        return jnp.stack([2 * chunk + core, 2 * chunk + 1 - core]).astype(jnp.int32)

    straight = [(2 * i + c, 2 * ((i + 1 - 2 * c) % y_count) + c) for i in range(y_count) for c in range(2)]
    cross = [(2 * i + c, 2 * ((i + 1 - 2 * c) % y_count) + 1 - c) for i in range(y_count) for c in range(2)]
    axes = ("y", "core")
    size = rows // ROW_PARTS

    def add(a, *others):
        total = a.astype(jnp.float32)
        for b in others:
            total = total + b.astype(jnp.float32)
        return total.astype(jnp.bfloat16)

    parts = {half: part(columns_at(half)[:1])}
    for distance in range(half - 1, 0, -1):
        parts[distance] = part(columns_at(distance))
    mine = part(columns_at(0)[:1])[0]
    outs = []
    for r in range(ROW_PARTS):
        at = slice(r * size, (r + 1) * size)
        got = lax.ppermute(parts[half][0, at], axes, straight)
        for distance in range(half - 1, 0, -1):
            now = parts[distance][:, at]
            if distance == half - 1:
                send = jnp.stack([add(now[0], got), now[1]])
            else:
                send = add(now, got)
            if distance > 1:
                got = lax.ppermute(send, axes, straight)
        near = lax.ppermute(send[0], axes, straight)
        far = lax.ppermute(send[1], axes, cross)
        outs.append(add(mine[at], near, far))
    return jnp.concatenate(outs, axis=0) if ROW_PARTS > 1 else outs[0]


def solution(mesh):
    dp_count, tensor_count = mesh.shape["dp"], mesh.shape["tensor"]
    split = Mesh(mesh.devices.reshape(dp_count, tensor_count // 2, 2), ("dp", "y", "core"))
    heads = ("y", "core")
    placed = (P(), P("dp", heads), P("dp", None), P("dp", None), P(heads, None))
    return jax.shard_map(on_device, mesh=split, in_specs=placed, out_specs=P("dp", heads), check_vma=False)
```

time: 175 us -> 113 us (0.65)
  the two profiles are of different devices: /device:TPU:31 before, /device:TPU:7 now
where the time goes in v1:
time: 113 us
  starting transfers between devices  46.6 us (41%)
  Pallas kernels  24.6 us (22%)
  waiting for transfers between devices  19.3 us (17%)
  local copies, waits for them, and re-layouts  18.9 us (17%)
  other arithmetic  2.81 us (2%)
    unnamed x12, local copies, waits for them, and re-layouts  17.9 us
    pallas_call x5, Pallas kernels, part(): pl.pallas_call(project, out_shape=jax.ShapeDtypeStruct((count, rows, wide...  11.7 us
    ppermute x1, starting transfers between devices, on_device(): lax.ppermute(first, 'dp', [(i, i + 1) for i in range(dp_count - 1)])  8.92 us
    ppermute x2, starting transfers between devices, on_device(): got = lax.ppermute(send, axes, straight)  7.65 us
    ppermute x1, starting transfers between devices, on_device(): first = lax.ppermute(own, ('dp', 'core'), first_pairs)  7.62 us
    ppermute x1, waiting for transfers between devices, on_device(): first = lax.ppermute(own, ('dp', 'core'), first_pairs)  7.44 us
    ppermute x2, waiting for transfers between devices, on_device(): got = lax.ppermute(send, axes, straight)  5.96 us
    pallas_call x1, Pallas kernels, on_device(): pl.pallas_call(attend_first, out_shape=state_shape, in_specs=[SM, VM, VM,...  5.92 us
  transfers between devices with their start and end apart: 10, of which 5 were waited for; matrix products, arithmetic and copies ran while one was open for 2% of the time, Pallas kernels for 20%

profile of v1, /device:TPU:7, one launch (start us, length us, event | category | flops | bytes accessed | tf_op | source)
XLA Modules:
  0.0 112.6 jit_solution(469425894176081407)
XLA Ops:
  0.0 2.6 %collective-permute-start.4 = (bf16[512,8192]{1,0:T(8,128)(2,1)}, bf16[512,8192]{1,0:T(8,128)(2,1)}, u32[]{:S(2)}, u32[]{:S(2)}) collective-permute-start(bf16[512,8192]{1,0:T(8,128)(2,1)} %wm_ref.9), channel_id=1, source_target_pairs={{0,1},{1,0},{2,3},{3,2},{4,5},{5,4},{6,7},{7,6},{8,9},{9,8},{10,11... | collective-permute-start | bytes 25165832 | tf_op jit(solution)/shard_map/ppermute | solution.py:158
  3.6 7.6 %collective-permute-start.1 = (bf16[384,256]{1,0:T(8,128)(2,1)S(1)}, bf16[384,256]{1,0:T(8,128)(2,1)S(1)}, u32[]{:S(2)}, u32[]{:S(2)}) collective-permute-start(bf16[384,256]{1,0:T(8,128)(2,1)S(1)} %pad_maximum_fusion.1.own_ref), channel_id=1, source_target_pairs={{0,16},{16,32},{32,48},{48,64},{64,80},{80,96},{96,112},{112,128},... | collective-permute-start | bytes 589832 | tf_op jit(solution)/shard_map/ppermute | solution.py:156
  14.2 7.4 %collective-permute-done.1.piece_ref = bf16[384,256]{1,0:T(8,128)(2,1)S(1)} collective-permute-done((bf16[384,256]{1,0:T(8,128)(2,1)S(1)}, bf16[384,256]{1,0:T(8,128)(2,1)S(1)}, u32[]{:S(2)}, u32[]{:S(2)}) %collective-permute-start.1) | collective-permute-done | bytes 196640 | tf_op jit(solution)/shard_map/ppermute | solution.py:156
  21.6 8.9 %collective-permute-start.2 = (bf16[384,256]{1,0:T(8,128)(2,1)S(1)}, bf16[384,256]{1,0:T(8,128)(2,1)S(1)}, u32[]{:S(2)}, u32[]{:S(2)}) collective-permute-start(bf16[384,256]{1,0:T(8,128)(2,1)S(1)} %collective-permute-done.1.piece_ref), channel_id=1, source_target_pairs={{0,16},{16,32},{32,48},{48,64},{64,80},{80,96},{96,112},{112,128},... | collective-permute-start | bytes 589832 | tf_op jit(solution)/shard_map/ppermute | solution.py:159
  31.6 5.9 %shard_map.55.state_ref = f32[1040,384]{1,0:T(8,128)S(1)} custom-call(s32[6]{0:T(128)S(1)} %pad_add_fusion.info_ref, bf16[384,512]{1,0:T(8,128)(2,1)S(1)} %copy-done.5, bf16[384,512]{1,0:T(8,128)(2,1)S(1)} %collective-permute-done.qo_ref, bf16[384,256]{1,0:T(8,128)(2,1)S(1)} %pad_maximum_fusion.1.own_ref, bf16[384,256]{1,0:T(8,128)(2,1)S(1)} %collective-permute-done.1.piece_ref), custom_call_target="tpu_custom_call" | custom-call | flops 1200000000 | bytes 4000000 | tf_op jit(solution)/shard_map/pallas_call | solution.py:170
  37.6 5.1 %shard_map.56.here_ref = f32[1040,384]{1,0:T(8,128)S(1)} custom-call(s32[6]{0:T(128)S(1)} %pad_add_fusion.info_ref, bf16[384,512]{1,0:T(8,128)(2,1)S(1)} %copy-done.5, bf16[384,512]{1,0:T(8,128)(2,1)S(1)} %collective-permute-done.qo_ref, bf16[384,256]{1,0:T(8,128)(2,1)S(1)} %collective-permute-done.2.piece_ref, f32[1040,384]{1,0:T(8,128)S(1)} %shard_map.55.state_ref), custom_call_target="tpu_custom_call" | custom-call | flops 600000000 | bytes 4000000 | tf_op jit(solution)/shard_map/pallas_call | solution.py:178
  42.7 2.2 %collective-permute-start.3 = (f32[1040,384]{1,0:T(8,128)S(1)}, f32[1040,384]{1,0:T(8,128)}, u32[]{:S(2)}, u32[]{:S(2)}) collective-permute-start(f32[1040,384]{1,0:T(8,128)S(1)} %shard_map.56.here_ref), channel_id=1, source_target_pairs={{0,1},{1,0},{2,3},{3,2},{4,5},{5,4},{6,7},{7,6},{8,9},{9,8},{10,11... | collective-permute-start | bytes 4792328 | tf_op jit(solution)/shard_map/ppermute | solution.py:186
  44.9 3.2 %collective-permute-done.3.there_ref = f32[1040,384]{1,0:T(8,128)} collective-permute-done((f32[1040,384]{1,0:T(8,128)S(1)}, f32[1040,384]{1,0:T(8,128)}, u32[]{:S(2)}, u32[]{:S(2)}) %collective-permute-start.3) | collective-permute-done | bytes 1597472 | tf_op jit(solution)/shard_map/ppermute | solution.py:186
  50.0 3.4 %copy-done = bf16[512,8192]{1,0:T(8,128)(2,1)S(1)} copy-done((bf16[512,8192]{1,0:T(8,128)(2,1)S(1)}, bf16[512,8192]{1,0:T(8,128)(2,1)}, u32[]{:S(2)}) %copy-start) | copy-done | bytes 8388632
  55.0 5.1 %collective-permute-start.5 = (bf16[384,512]{1,0:T(8,128)(2,1)S(1)}, bf16[384,512]{1,0:T(8,128)(2,1)S(1)}, u32[]{:S(2)}, u32[]{:S(2)}) collective-permute-start(bf16[384,512]{1,0:T(8,128)(2,1)S(1)} %bitcast.26), channel_id=1, source_target_pairs={{0,2},{1,15},{2,4},{3,1},{4,6},{5,3},{6,8},{7,5},{8,10},{9,7},{10,... | collective-permute-start | bytes 1179656 | tf_op jit(solution)/shard_map/ppermute | solution.py:242
  60.3 3.4 %copy-done.1 = bf16[512,8192]{1,0:T(8,128)(2,1)S(1)} copy-done((bf16[512,8192]{1,0:T(8,128)(2,1)S(1)}, bf16[512,8192]{1,0:T(8,128)(2,1)}, u32[]{:S(2)}) %copy-start.1) | copy-done | bytes 8388632
  63.6 2.8 %shard_map.61 = bf16[2,384,512]{2,1,0:T(8,128)(2,1)S(1)} custom-call(s32[2]{0:T(128)S(1)} %pad_add_fusion.3.columns_ref, bf16[384,1024]{1,0:T(8,128)(2,1)S(1)} %shard_map.57.att_ref, bf16[512,8192]{1,0:T(8,128)(2,1)S(1)} %copy-done.1, bf16[512,8192]{1,0:T(8,128)(2,1)} %collective-permute-done.4.wo_ref), custom_call_target="tpu_custom_call" | custom-call | flops 805306368 | bytes 6000000 | tf_op jit(solution)/shard_map/pallas_call | solution.py:198
  66.7 3.4 %collective-permute-start.6 = (bf16[2,384,512]{2,1,0:T(8,128)(2,1)S(1)}, bf16[2,384,512]{2,1,0:T(8,128)(2,1)S(1)}, u32[]{:S(2)}, u32[]{:S(2)}) collective-permute-start(bf16[2,384,512]{2,1,0:T(8,128)(2,1)S(1)} %pad_maximum_fusion), channel_id=1, source_target_pairs={{0,2},{1,15},{2,4},{3,1},{4,6},{5,3},{6,8},{7,5},{8,10},{9,7},{10,... | collective-permute-start | bytes 2359304 | tf_op jit(solution)/shard_map/ppermute | solution.py:250
  70.2 3.4 %copy-done.2 = bf16[512,8192]{1,0:T(8,128)(2,1)S(1)} copy-done((bf16[512,8192]{1,0:T(8,128)(2,1)S(1)}, bf16[512,8192]{1,0:T(8,128)(2,1)}, u32[]{:S(2)}) %copy-start.2) | copy-done | bytes 8388632
  73.5 2.8 %shard_map.60 = bf16[2,384,512]{2,1,0:T(8,128)(2,1)S(1)} custom-call(s32[2]{0:T(128)S(1)} %pad_add_fusion.2.columns_ref, bf16[384,1024]{1,0:T(8,128)(2,1)S(1)} %shard_map.57.att_ref, bf16[512,8192]{1,0:T(8,128)(2,1)S(1)} %copy-done.2, bf16[512,8192]{1,0:T(8,128)(2,1)} %collective-permute-done.4.wo_ref), custom_call_target="tpu_custom_call" | custom-call | flops 805306368 | bytes 6000000 | tf_op jit(solution)/shard_map/pallas_call | solution.py:198
  76.4 3.3 %collective-permute-done.6 = bf16[2,384,512]{2,1,0:T(8,128)(2,1)S(1)} collective-permute-done((bf16[2,384,512]{2,1,0:T(8,128)(2,1)S(1)}, bf16[2,384,512]{2,1,0:T(8,128)(2,1)S(1)}, u32[]{:S(2)}, u32[]{:S(2)}) %collective-permute-start.6) | collective-permute-done | bytes 786464 | tf_op jit(solution)/shard_map/ppermute | solution.py:250
  79.9 4.3 %collective-permute-start.7 = (bf16[2,384,512]{2,1,0:T(8,128)(2,1)S(1)}, bf16[2,384,512]{2,1,0:T(8,128)(2,1)S(1)}, u32[]{:S(2)}, u32[]{:S(2)}) collective-permute-start(bf16[2,384,512]{2,1,0:T(8,128)(2,1)S(1)} %add_convert_fusion.1), channel_id=1, source_target_pairs={{0,2},{1,15},{2,4},{3,1},{4,6},{5,3},{6,8},{7,5},{8,10},{9,7},{10,... | collective-permute-start | bytes 2359304 | tf_op jit(solution)/shard_map/ppermute | solution.py:250
  84.3 3.4 %copy-done.3 = bf16[512,8192]{1,0:T(8,128)(2,1)S(1)} copy-done((bf16[512,8192]{1,0:T(8,128)(2,1)S(1)}, bf16[512,8192]{1,0:T(8,128)(2,1)}, u32[]{:S(2)}) %copy-start.3) | copy-done | bytes 8388632
  87.7 2.8 %shard_map.59 = bf16[2,384,512]{2,1,0:T(8,128)(2,1)S(1)} custom-call(s32[2]{0:T(128)S(1)} %pad_add_fusion.1.columns_ref, bf16[384,1024]{1,0:T(8,128)(2,1)S(1)} %shard_map.57.att_ref, bf16[512,8192]{1,0:T(8,128)(2,1)S(1)} %copy-done.3, bf16[512,8192]{1,0:T(8,128)(2,1)} %collective-permute-done.4.wo_ref), custom_call_target="tpu_custom_call" | custom-call | flops 805306368 | bytes 6000000 | tf_op jit(solution)/shard_map/pallas_call | solution.py:198
  90.5 2.6 %collective-permute-done.7 = bf16[2,384,512]{2,1,0:T(8,128)(2,1)S(1)} collective-permute-done((bf16[2,384,512]{2,1,0:T(8,128)(2,1)S(1)}, bf16[2,384,512]{2,1,0:T(8,128)(2,1)S(1)}, u32[]{:S(2)}, u32[]{:S(2)}) %collective-permute-start.7) | collective-permute-done | bytes 786464 | tf_op jit(solution)/shard_map/ppermute | solution.py:250
  93.4 5.0 %collective-permute-start.8 = (bf16[384,512]{1,0:T(8,128)(2,1)S(1)}, bf16[384,512]{1,0:T(8,128)(2,1)S(1)}, u32[]{:S(2)}, u32[]{:S(2)}) collective-permute-start(bf16[384,512]{1,0:T(8,128)(2,1)S(1)} %get-tuple-element.5), channel_id=1, source_target_pairs={{0,2},{1,15},{2,4},{3,1},{4,6},{5,3},{6,8},{7,5},{8,10},{9,7},{10,... | collective-permute-start | bytes 1179656 | tf_op jit(solution)/shard_map/ppermute | solution.py:251
  98.4 5.5 %collective-permute-start.9 = (bf16[384,512]{1,0:T(8,128)(2,1)S(1)}, bf16[384,512]{1,0:T(8,128)(2,1)S(1)}, u32[]{:S(2)}, u32[]{:S(2)}) collective-permute-start(bf16[384,512]{1,0:T(8,128)(2,1)S(1)} %get-tuple-element.6), channel_id=1, source_target_pairs={{0,3},{1,14},{2,5},{3,0},{4,7},{5,2},{6,9},{7,4},{8,11},{9,6},{10,... | collective-permute-start | bytes 1179656 | tf_op jit(solution)/shard_map/ppermute | solution.py:252
  104.0 3.4 %copy-done.4 = bf16[512,8192]{1,0:T(8,128)(2,1)S(1)} copy-done((bf16[512,8192]{1,0:T(8,128)(2,1)S(1)}, bf16[512,8192]{1,0:T(8,128)(2,1)}, u32[]{:S(2)}) %copy-start.4) | copy-done | bytes 8388632
  109.1 2.7 %collective-permute-done.9 = bf16[384,512]{1,0:T(8,128)(2,1)S(1)} collective-permute-done((bf16[384,512]{1,0:T(8,128)(2,1)S(1)}, bf16[384,512]{1,0:T(8,128)(2,1)S(1)}, u32[]{:S(2)}, u32[]{:S(2)}) %collective-permute-start.9) | collective-permute-done | bytes 393248 | tf_op jit(solution)/shard_map/ppermute | solution.py:252
  (33 shorter events, 11.9 us)
Async XLA Ops:
  0.0 50.0 %collective-permute-start.4 = (bf16[512,8192]{1,0:T(8,128)(2,1)}, bf16[512,8192]{1,0:T(8,128)(2,1)}, u32[]{:S(2)}, u32[]{:S(2)}) collective-permute-start(bf16[512,8192]{1,0:T(8,128)(2,1)} %wm_ref.9), channel_id=1, source_target_pairs={{0,1},{1,0},{2,3},{3,2},{4,5},{5,4},{6,7},{7,6},{8,9},{9,8},{10,11... | collective-permute-start | bytes 25165832 | tf_op jit(solution)/shard_map/ppermute | solution.py:158
  3.6 18.0 %collective-permute-start.1 = (bf16[384,256]{1,0:T(8,128)(2,1)S(1)}, bf16[384,256]{1,0:T(8,128)(2,1)S(1)}, u32[]{:S(2)}, u32[]{:S(2)}) collective-permute-start(bf16[384,256]{1,0:T(8,128)(2,1)S(1)} %pad_maximum_fusion.1.own_ref), channel_id=1, source_target_pairs={{0,16},{16,32},{32,48},{48,64},{64,80},{80,96},{96,112},{112,128},... | collective-permute-start | bytes 589832 | tf_op jit(solution)/shard_map/ppermute | solution.py:156
  11.2 19.4 %collective-permute-start = (bf16[384,512]{1,0:T(8,128)(2,1)}, bf16[384,512]{1,0:T(8,128)(2,1)S(1)}, u32[]{:S(2)}, u32[]{:S(2)}) collective-permute-start(bf16[384,512]{1,0:T(8,128)(2,1)} %qm_ref.3), channel_id=1, source_target_pairs={{0,1},{1,0},{2,3},{3,2},{4,5},{5,4},{6,7},{7,6},{8,9},{9,8},{10,11... | collective-permute-start | bytes 1179656 | tf_op jit(solution)/shard_map/ppermute | solution.py:157
  21.6 15.9 %collective-permute-start.2 = (bf16[384,256]{1,0:T(8,128)(2,1)S(1)}, bf16[384,256]{1,0:T(8,128)(2,1)S(1)}, u32[]{:S(2)}, u32[]{:S(2)}) collective-permute-start(bf16[384,256]{1,0:T(8,128)(2,1)S(1)} %collective-permute-done.1.piece_ref), channel_id=1, source_target_pairs={{0,16},{16,32},{32,48},{48,64},{64,80},{80,96},{96,112},{112,128},... | collective-permute-start | bytes 589832 | tf_op jit(solution)/shard_map/ppermute | solution.py:159
  30.6 1.0 copy-start.5
  42.7 5.5 %collective-permute-start.3 = (f32[1040,384]{1,0:T(8,128)S(1)}, f32[1040,384]{1,0:T(8,128)}, u32[]{:S(2)}, u32[]{:S(2)}) collective-permute-start(f32[1040,384]{1,0:T(8,128)S(1)} %shard_map.56.here_ref), channel_id=1, source_target_pairs={{0,1},{1,0},{2,3},{3,2},{4,5},{5,4},{6,7},{7,6},{8,9},{9,8},{10,11... | collective-permute-start | bytes 4792328 | tf_op jit(solution)/shard_map/ppermute | solution.py:186
  50.0 3.4 %copy-start = (bf16[512,8192]{1,0:T(8,128)(2,1)S(1)}, bf16[512,8192]{1,0:T(8,128)(2,1)}, u32[]{:S(2)}) copy-start(bf16[512,8192]{1,0:T(8,128)(2,1)} %wm_ref.9) | copy-start | bytes 25165828
  55.0 11.4 %collective-permute-start.5 = (bf16[384,512]{1,0:T(8,128)(2,1)S(1)}, bf16[384,512]{1,0:T(8,128)(2,1)S(1)}, u32[]{:S(2)}, u32[]{:S(2)}) collective-permute-start(bf16[384,512]{1,0:T(8,128)(2,1)S(1)} %bitcast.26), channel_id=1, source_target_pairs={{0,2},{1,15},{2,4},{3,1},{4,6},{5,3},{6,8},{7,5},{8,10},{9,7},{10,... | collective-permute-start | bytes 1179656 | tf_op jit(solution)/shard_map/ppermute | solution.py:242
  60.2 3.4 %copy-start.1 = (bf16[512,8192]{1,0:T(8,128)(2,1)S(1)}, bf16[512,8192]{1,0:T(8,128)(2,1)}, u32[]{:S(2)}) copy-start(bf16[512,8192]{1,0:T(8,128)(2,1)} %wm_ref.9) | copy-start | bytes 25165828
  66.7 13.0 %collective-permute-start.6 = (bf16[2,384,512]{2,1,0:T(8,128)(2,1)S(1)}, bf16[2,384,512]{2,1,0:T(8,128)(2,1)S(1)}, u32[]{:S(2)}, u32[]{:S(2)}) collective-permute-start(bf16[2,384,512]{2,1,0:T(8,128)(2,1)S(1)} %pad_maximum_fusion), channel_id=1, source_target_pairs={{0,2},{1,15},{2,4},{3,1},{4,6},{5,3},{6,8},{7,5},{8,10},{9,7},{10,... | collective-permute-start | bytes 2359304 | tf_op jit(solution)/shard_map/ppermute | solution.py:250
  70.2 3.4 %copy-start.2 = (bf16[512,8192]{1,0:T(8,128)(2,1)S(1)}, bf16[512,8192]{1,0:T(8,128)(2,1)}, u32[]{:S(2)}) copy-start(bf16[512,8192]{1,0:T(8,128)(2,1)} %wm_ref.9) | copy-start | bytes 25165828
  79.9 13.2 %collective-permute-start.7 = (bf16[2,384,512]{2,1,0:T(8,128)(2,1)S(1)}, bf16[2,384,512]{2,1,0:T(8,128)(2,1)S(1)}, u32[]{:S(2)}, u32[]{:S(2)}) collective-permute-start(bf16[2,384,512]{2,1,0:T(8,128)(2,1)S(1)} %add_convert_fusion.1), channel_id=1, source_target_pairs={{0,2},{1,15},{2,4},{3,1},{4,6},{5,3},{6,8},{7,5},{8,10},{9,7},{10,... | collective-permute-start | bytes 2359304 | tf_op jit(solution)/shard_map/ppermute | solution.py:250
  84.3 3.4 %copy-start.3 = (bf16[512,8192]{1,0:T(8,128)(2,1)S(1)}, bf16[512,8192]{1,0:T(8,128)(2,1)}, u32[]{:S(2)}) copy-start(bf16[512,8192]{1,0:T(8,128)(2,1)} %wm_ref.9) | copy-start | bytes 25165828
  93.4 15.6 %collective-permute-start.8 = (bf16[384,512]{1,0:T(8,128)(2,1)S(1)}, bf16[384,512]{1,0:T(8,128)(2,1)S(1)}, u32[]{:S(2)}, u32[]{:S(2)}) collective-permute-start(bf16[384,512]{1,0:T(8,128)(2,1)S(1)} %get-tuple-element.5), channel_id=1, source_target_pairs={{0,2},{1,15},{2,4},{3,1},{4,6},{5,3},{6,8},{7,5},{8,10},{9,7},{10,... | collective-permute-start | bytes 1179656 | tf_op jit(solution)/shard_map/ppermute | solution.py:251
  98.4 13.3 %collective-permute-start.9 = (bf16[384,512]{1,0:T(8,128)(2,1)S(1)}, bf16[384,512]{1,0:T(8,128)(2,1)S(1)}, u32[]{:S(2)}, u32[]{:S(2)}) collective-permute-start(bf16[384,512]{1,0:T(8,128)(2,1)S(1)} %get-tuple-element.6), channel_id=1, source_target_pairs={{0,3},{1,14},{2,5},{3,0},{4,7},{5,2},{6,9},{7,4},{8,11},{9,6},{10,... | collective-permute-start | bytes 1179656 | tf_op jit(solution)/shard_map/ppermute | solution.py:252
  104.0 3.4 %copy-start.4 = (bf16[512,8192]{1,0:T(8,128)(2,1)S(1)}, bf16[512,8192]{1,0:T(8,128)(2,1)}, u32[]{:S(2)}) copy-start(bf16[512,8192]{1,0:T(8,128)(2,1)} %wm_ref.9) | copy-start | bytes 25165828

commit v2 on v1

v2 whole, which is shorter than its diff:
```python
import functools
import math

import jax
import jax.numpy as jnp
from jax import lax
from jax.experimental import pallas as pl
from jax.experimental.pallas import tpu as pltpu
from jax.sharding import Mesh, PartitionSpec as P

HD = 128
UNIT = 128
NEG = -1e30
EXP_SCALE = math.log2(math.e) / HD**0.5
ROW_PARTS = 2
AHEAD = 3

FIRST_BACK = (1, 3)
SECOND_BACK = (2, 4)


def block_bias(allowed):
    return jnp.where(allowed, 0.0, NEG).astype(jnp.float32)


def head_pair(q_refs, pair, unit):
    q_ref = q_refs[pair // 2]
    rows = pl.ds(unit * UNIT, UNIT)
    first = (pair % 2) * 2 * HD
    return jnp.concatenate([q_ref[rows, first : first + HD], q_ref[rows, first + HD : first + 2 * HD]], axis=0)


def raw_scores(k_rows, q_pair):
    return lax.dot_general(k_rows, q_pair, (((1,), (1,)), ((), ())), preferred_element_type=jnp.float32)


def weighted(v_columns, weights):
    return jnp.dot(v_columns, weights.astype(jnp.bfloat16), preferred_element_type=jnp.float32)


def ahead(steps, compute):
    pending = [compute(*step) for step in steps[:AHEAD]]
    for at, step in enumerate(steps):
        if at + AHEAD < len(steps):
            pending.append(compute(*steps[at + AHEAD]))
        yield step, pending.pop(0)


def store_state(out_ref, pair, unit, top, total, accum):
    heads = 8
    cols = pl.ds(unit * UNIT, UNIT)
    for side in range(2):
        head = 2 * pair + side
        part = slice(side * UNIT, (side + 1) * UNIT)
        out_ref[pl.ds(head * HD, HD), cols] = accum[:, part]
        out_ref[pl.ds(heads * HD + head, 1), cols] = top[:, part]
        out_ref[pl.ds(heads * HD + heads + head, 1), cols] = total[:, part]


def load_state(ref, pair, unit):
    heads = 8
    cols = pl.ds(unit * UNIT, UNIT)
    both = []
    for base, size in ((heads * HD, 1), (heads * HD + heads, 1), (0, HD)):
        halves = [ref[pl.ds(base + (2 * pair + side) * size, size), cols] for side in range(2)]
        both.append(jnp.concatenate(halves, axis=1))
    return both


def piece_bias(info_ref, unit, back, units):
    low = info_ref[unit]
    return [block_bias(low <= block - units * back) for block in range(units)]


def attend_own(info_ref, qm_ref, qo_ref, own_ref, out_ref):
    units = qm_ref.shape[0] // UNIT
    core = info_ref[units + 2]
    triangle = lax.broadcasted_iota(jnp.int32, (UNIT, 2 * UNIT), 0) <= (
        lax.broadcasted_iota(jnp.int32, (UNIT, 2 * UNIT), 1) % UNIT
    )
    v_own = jnp.transpose(own_ref[:, HD:])

    def scores_of(unit, pair):
        return raw_scores(own_ref[: (unit + 1) * UNIT, :HD], head_pair((qm_ref, qo_ref), pair, unit))

    steps = [(unit, pair) for unit in range(units) for pair in range(4)]
    for (unit, pair), raw in ahead(steps, scores_of):
        low = info_ref[unit]
        blocks = []
        for b in range(unit + 1):
            block = raw[b * UNIT : (b + 1) * UNIT] + block_bias((low <= b) & (core == 0))
            blocks.append(jnp.where(triangle, block, NEG) if b == unit else block)
        scores = jnp.concatenate(blocks, axis=0)
        top = jnp.max(scores, axis=0, keepdims=True)
        weights = jnp.exp2((scores - top) * EXP_SCALE)
        total = jnp.sum(weights, axis=0, keepdims=True)
        store_state(out_ref, pair, unit, top, total, weighted(v_own[:, : (unit + 1) * UNIT], weights))


def attend_piece(which, info_ref, qm_ref, qo_ref, piece_ref, state_ref, out_ref):
    units = qm_ref.shape[0] // UNIT
    v_piece = jnp.transpose(piece_ref[:, HD:])

    def scores_of(unit, pair):
        return raw_scores(piece_ref[:, :HD], head_pair((qm_ref, qo_ref), pair, unit))

    steps = [(unit, pair) for unit in range(units) for pair in range(4)]
    for (unit, pair), raw in ahead(steps, scores_of):
        bias = piece_bias(info_ref, unit, info_ref[units + which], units)
        scores = jnp.concatenate([raw[b * UNIT : (b + 1) * UNIT] + bias[b] for b in range(units)], axis=0)
        old_top, old_total, old_accum = load_state(state_ref, pair, unit)
        top = jnp.maximum(old_top, jnp.max(scores, axis=0, keepdims=True))
        weights = jnp.exp2((scores - top) * EXP_SCALE)
        factor = jnp.exp2((old_top - top) * EXP_SCALE)
        total = old_total * factor + jnp.sum(weights, axis=0, keepdims=True)
        accum = old_accum * factor + weighted(v_piece, weights)
        store_state(out_ref, pair, unit, top, total, accum)


def fetch(columns_ref, block, w_refs, w_buf, sems):
    wide = w_buf.shape[-1]
    at = pl.ds(pl.multiple_of(columns_ref[block] * wide, wide), wide)
    return [pltpu.make_async_copy(ref.at[:, at], w_buf.at[block, n], sems.at[block, n]) for n, ref in enumerate(w_refs)]


def product(att_ref, w_buf, block):
    depth = w_buf.shape[2]
    summed = jnp.dot(att_ref[:, :depth], w_buf[block, 0], preferred_element_type=jnp.float32)
    summed += jnp.dot(att_ref[:, depth:], w_buf[block, 1], preferred_element_type=jnp.float32)
    return summed.astype(jnp.bfloat16)


def combine(columns_ref, here_ref, there_ref, wm_ref, wo_ref, att_ref, out_ref, w_buf, sems):
    heads = 8
    copies = fetch(columns_ref, 0, (wm_ref, wo_ref), w_buf, sems)
    for copy in copies:
        copy.start()
    for head in range(heads):
        other = (head + heads // 2) % heads
        top_a = here_ref[pl.ds(heads * HD + head, 1), :]
        top_b = there_ref[pl.ds(heads * HD + other, 1), :]
        top = jnp.maximum(top_a, top_b)
        share_a = jnp.exp2((top_a - top) * EXP_SCALE)
        share_b = jnp.exp2((top_b - top) * EXP_SCALE)
        total = (
            here_ref[pl.ds(heads * HD + heads + head, 1), :] * share_a
            + there_ref[pl.ds(heads * HD + heads + other, 1), :] * share_b
        )
        accum = here_ref[pl.ds(head * HD, HD), :] * share_a + there_ref[pl.ds(other * HD, HD), :] * share_b
        att_ref[:, head * HD : (head + 1) * HD] = jnp.transpose(accum / total).astype(jnp.bfloat16)
    for copy in copies:
        copy.wait()
    out_ref[...] = product(att_ref, w_buf, 0)


def project(columns_ref, att_ref, wm_ref, wo_ref, out_ref, w_buf, sems):
    copies = [fetch(columns_ref, block, (wm_ref, wo_ref), w_buf, sems) for block in range(out_ref.shape[0])]
    for copy in sum(copies, []):
        copy.start()
    for block in range(out_ref.shape[0]):
        for copy in copies[block]:
            copy.wait()
        out_ref[block] = product(att_ref, w_buf, block)


VM = pl.BlockSpec(memory_space=pltpu.VMEM)
HBM = pl.BlockSpec(memory_space=pltpu.HBM)
SM = pl.BlockSpec(memory_space=pltpu.SMEM)
LIMIT = pltpu.CompilerParams(vmem_limit_bytes=32 * 1024 * 1024)
WIDE_LIMIT = pltpu.CompilerParams(vmem_limit_bytes=49 * 1024 * 1024)


def on_device(lengths, queries, keys, values, out_weight):
    rows, wide = queries.shape
    units = rows // UNIT
    dp_count, y_count = lax.axis_size("dp"), lax.axis_size("y")
    dp, y, core = lax.axis_index("dp"), lax.axis_index("y"), lax.axis_index("core")
    swap = [(0, 1), (1, 0)]

    own = jnp.concatenate(
        [lax.dynamic_slice_in_dim(keys, y * HD, HD, 1), lax.dynamic_slice_in_dim(values, y * HD, HD, 1)], axis=1
    )
    first_pairs = [
        (2 * i + c, 2 * (i + FIRST_BACK[c]) + c) for c in range(2) for i in range(dp_count - FIRST_BACK[c])
    ]
    first = lax.ppermute(own, ("dp", "core"), first_pairs)
    q_other = lax.ppermute(queries, "core", swap)
    second = lax.ppermute(first, "dp", [(i, i + 1) for i in range(dp_count - 1)])

    w_other = lax.ppermute(out_weight, "core", swap)

    order = jnp.arange(lengths.shape[0], dtype=jnp.int32)
    ends = jnp.sum(jnp.where(order[None, :] <= order[:, None], lengths[None, :], 0), axis=1)
    q_starts = dp * rows + UNIT * jnp.arange(units, dtype=jnp.int32)
    doc_starts = jnp.max(jnp.where(ends[None, :] <= q_starts[:, None], ends[None, :], 0), axis=1)
    lows = doc_starts // UNIT - dp * units
    tail = jnp.stack([1 + 2 * core, 2 + 2 * core, core])
    info = jnp.concatenate([lows, tail]).astype(jnp.int32)

    state_shape = jax.ShapeDtypeStruct((2 * wide + 16, rows), jnp.float32)
    state = pl.pallas_call(
        attend_own,
        out_shape=state_shape,
        in_specs=[SM, VM, VM, VM],
        out_specs=VM,
        compiler_params=LIMIT,
        cost_estimate=pl.CostEstimate(flops=60000000000, bytes_accessed=4_000_000, transcendentals=1_000_000),
    )(info, queries, q_other, own)
    for which, piece in enumerate((first, second)):
        state = pl.pallas_call(
            functools.partial(attend_piece, which),
            out_shape=state_shape,
            in_specs=[SM, VM, VM, VM, VM],
            out_specs=VM,
            compiler_params=LIMIT,
            cost_estimate=pl.CostEstimate(flops=60000000000, bytes_accessed=6_000_000, transcendentals=1_000_000),
        )(info, queries, q_other, piece, state)
    there = lax.ppermute(state, "core", swap)
    half = y_count // 2
    way = 1 - 2 * core

    def columns_at(distance):
        chunk = jnp.mod(y + way * distance, y_count)
        return jnp.stack([2 * chunk + core, 2 * chunk + 1 - core]).astype(jnp.int32)

    def w_scratch(count):
        return [pltpu.VMEM((count, 2, wide, wide), jnp.bfloat16), pltpu.SemaphoreType.DMA((count, 2))]

    attended, farthest = pl.pallas_call(
        combine,
        out_shape=[
            jax.ShapeDtypeStruct((rows, 2 * wide), jnp.bfloat16),
            jax.ShapeDtypeStruct((rows, wide), jnp.bfloat16),
        ],
        in_specs=[SM, VM, VM, HBM, HBM],
        out_specs=[VM, VM],
        scratch_shapes=w_scratch(1),
        compiler_params=WIDE_LIMIT,
        cost_estimate=pl.CostEstimate(flops=400_000_000, bytes_accessed=5_000_000, transcendentals=10_000),
    )(columns_at(half)[:1], state, there, out_weight, w_other)

    def part(columns):
        count = columns.shape[0]
        return pl.pallas_call(
            project,
            out_shape=jax.ShapeDtypeStruct((count, rows, wide), jnp.bfloat16),
            in_specs=[SM, VM, HBM, HBM],
            out_specs=VM,
            scratch_shapes=w_scratch(count),
            compiler_params=WIDE_LIMIT,
            cost_estimate=pl.CostEstimate(
                flops=4 * rows * wide * wide * count, bytes_accessed=3_000_000 * count, transcendentals=0
            ),
        )(columns, attended, out_weight, w_other)

    straight = [(2 * i + c, 2 * ((i + 1 - 2 * c) % y_count) + c) for i in range(y_count) for c in range(2)]
    cross = [(2 * i + c, 2 * ((i + 1 - 2 * c) % y_count) + 1 - c) for i in range(y_count) for c in range(2)]
    axes = ("y", "core")
    size = rows // ROW_PARTS

    def add(a, *others):
        total = a.astype(jnp.float32)
        for b in others:
            total = total + b.astype(jnp.float32)
        return total.astype(jnp.bfloat16)

    parts = {distance: part(columns_at(distance)) for distance in range(half - 1, 0, -1)}
    mine = part(columns_at(0)[:1])[0]
    spots = [slice(r * size, (r + 1) * size) for r in range(ROW_PARTS)]
    got = []
    for at in spots:
        value = lax.ppermute(farthest[at], axes, straight)
        got.append(lax.pad(value[None], jnp.zeros((), value.dtype), ((0, 1, 0), (0, 0, 0), (0, 0, 0))))
    token = None
    for distance in range(half - 1, 0, -1):
        for r, at in enumerate(spots):
            now = parts[distance][:, at]
            if token is not None:
                now, token = lax.optimization_barrier((now, token))
            if distance > 1:
                token = add(now, got[r])
                got[r] = lax.ppermute(token, axes, straight)
            else:
                near, far = add(now[0], got[r][0]), add(now[1], got[r][1])
                token = near
                got[r] = (lax.ppermute(near, axes, straight), lax.ppermute(far, axes, cross))
    outs = [add(mine[at], *got[r]) for r, at in enumerate(spots)]
    return jnp.concatenate(outs, axis=0) if ROW_PARTS > 1 else outs[0]


def solution(mesh):
    dp_count, tensor_count = mesh.shape["dp"], mesh.shape["tensor"]
    split = Mesh(mesh.devices.reshape(dp_count, tensor_count // 2, 2), ("dp", "y", "core"))
    heads = ("y", "core")
    placed = (P(), P("dp", heads), P("dp", None), P("dp", None), P(heads, None))
    return jax.shard_map(on_device, mesh=split, in_specs=placed, out_specs=P("dp", heads), check_vma=False)
```

time: 113 us -> 105 us (0.929)
  local copies, waits for them, and re-layouts: 18.9 us -> 2.12 us
  starting transfers between devices: 46.6 us -> 62.4 us
  Pallas kernels: 24.6 us -> 20.9 us
  waiting for transfers between devices: 19.3 us -> 15.8 us
    unnamed x12 -> x2, local copies, waits for them, and re-layouts: 17.9 us -> 0.99 us
    ppermute x5 -> x10, starting transfers between devices: 23.3 us -> 37.8 us  [the longest x4 13.5 us: on_device(): got[r] = lax.ppermute(token, axes, straight)]
    ppermute x5 -> x10, waiting for transfers between devices: 8.64 us -> 5.53 us  [the longest x2 4.42 us: on_device(): lax.ppermute(far, axes, cross)]
    pallas_call x3 -> x4, Pallas kernels: 12.9 us -> 10.3 us  [the longest x2 4.92 us: on_device(): pl.pallas_call(functools.partial(attend_piece, which), out_shape=state_sh...]
    ppermute x1, starting transfers between devices: 2.21 us -> 3.62 us  [on_device(): there = lax.ppermute(state, 'core', swap)]
    pallas_call x5 -> x4, Pallas kernels: 11.7 us -> 10.6 us  [part(): pl.pallas_call(project, out_shape=jax.ShapeDtypeStruct((count, rows, wide...]
  transfers between devices with their start and end apart: 10 -> 15, of which waited for: 5 -> 5; matrix products, arithmetic and copies ran while one was open for 2% -> 3% of each run, Pallas kernels for 20% -> 17%
where the time goes in v2:
time: 105 us; the launch traced here: 104 us
  starting transfers between devices  62.4 us (59%)
  Pallas kernels  20.9 us (20%)
  waiting for transfers between devices  15.8 us (15%)
  other arithmetic  2.75 us (3%)
  local copies, waits for them, and re-layouts  2.12 us (2%)
    ppermute x4, starting transfers between devices, on_device(): got[r] = lax.ppermute(token, axes, straight)  13.5 us
    pallas_call x4, Pallas kernels, part(): pl.pallas_call(project, out_shape=jax.ShapeDtypeStruct((count, rows, wide...  10.6 us
    ppermute x1, starting transfers between devices, on_device(): lax.ppermute(first, 'dp', [(i, i + 1) for i in range(dp_count - 1)])  8.92 us
    ppermute x2, starting transfers between devices, on_device(): lax.ppermute(near, axes, straight)  8.66 us
    ppermute x2, starting transfers between devices, on_device(): value = lax.ppermute(farthest[at], axes, straight)  8.07 us
    ppermute x1, starting transfers between devices, on_device(): first = lax.ppermute(own, ('dp', 'core'), first_pairs)  7.62 us
    ppermute x2, starting transfers between devices, on_device(): lax.ppermute(far, axes, cross)  7.56 us
    ppermute x1, waiting for transfers between devices, on_device(): first = lax.ppermute(own, ('dp', 'core'), first_pairs)  7.36 us
  transfers between devices with their start and end apart: 15, of which 5 were waited for; matrix products, arithmetic and copies ran while one was open for 3% of the time, Pallas kernels for 17%

profile of v2, /device:TPU:7, one launch (start us, length us, event | category | flops | bytes accessed | tf_op | source)
XLA Modules:
  0.0 104.5 jit_solution(10190793244519903529)
XLA Ops:
  0.0 2.6 %collective-permute-start = (bf16[384,512]{1,0:T(8,128)(2,1)}, bf16[384,512]{1,0:T(8,128)(2,1)S(1)}, u32[]{:S(2)}, u32[]{:S(2)}) collective-permute-start(bf16[384,512]{1,0:T(8,128)(2,1)} %qm_ref.5), channel_id=1, source_target_pairs={{0,1},{1,0},{2,3},{3,2},{4,5},{5,4},{6,7},{7,6},{8,9},{9,8},{10,11... | collective-permute-start | bytes 1179656 | tf_op jit(solution)/shard_map/ppermute | solution.py:187
  3.6 7.6 %collective-permute-start.1 = (bf16[384,256]{1,0:T(8,128)(2,1)S(1)}, bf16[384,256]{1,0:T(8,128)(2,1)S(1)}, u32[]{:S(2)}, u32[]{:S(2)}) collective-permute-start(bf16[384,256]{1,0:T(8,128)(2,1)S(1)} %pad_maximum_fusion.1.own_ref), channel_id=1, source_target_pairs={{0,16},{16,32},{32,48},{48,64},{64,80},{80,96},{96,112},{112,128},... | collective-permute-start | bytes 589832 | tf_op jit(solution)/shard_map/ppermute | solution.py:186
  11.2 1.9 %collective-permute-start.4 = (bf16[512,8192]{1,0:T(8,128)(2,1)}, bf16[512,8192]{1,0:T(8,128)(2,1)}, u32[]{:S(2)}, u32[]{:S(2)}) collective-permute-start(bf16[512,8192]{1,0:T(8,128)(2,1)} %wm_ref.9), channel_id=1, source_target_pairs={{0,1},{1,0},{2,3},{3,2},{4,5},{5,4},{6,7},{7,6},{8,9},{9,8},{10,11... | collective-permute-start | bytes 25165832 | tf_op jit(solution)/shard_map/ppermute | solution.py:190
  14.3 7.4 %collective-permute-done.1.piece_ref = bf16[384,256]{1,0:T(8,128)(2,1)S(1)} collective-permute-done((bf16[384,256]{1,0:T(8,128)(2,1)S(1)}, bf16[384,256]{1,0:T(8,128)(2,1)S(1)}, u32[]{:S(2)}, u32[]{:S(2)}) %collective-permute-start.1) | collective-permute-done | bytes 196640 | tf_op jit(solution)/shard_map/ppermute | solution.py:186
  21.6 8.9 %collective-permute-start.2 = (bf16[384,256]{1,0:T(8,128)(2,1)S(1)}, bf16[384,256]{1,0:T(8,128)(2,1)S(1)}, u32[]{:S(2)}, u32[]{:S(2)}) collective-permute-start(bf16[384,256]{1,0:T(8,128)(2,1)S(1)} %collective-permute-done.1.piece_ref), channel_id=1, source_target_pairs={{0,16},{16,32},{32,48},{48,64},{64,80},{80,96},{96,112},{112,128},... | collective-permute-start | bytes 589832 | tf_op jit(solution)/shard_map/ppermute | solution.py:188
  31.5 2.1 %shard_map.55.state_ref = f32[1040,384]{1,0:T(8,128)S(1)} custom-call(s32[6]{0:T(128)S(1)} %pad_add_fusion.info_ref, bf16[384,512]{1,0:T(8,128)(2,1)S(1)} %copy-done, bf16[384,512]{1,0:T(8,128)(2,1)S(1)} %collective-permute-done.qo_ref, bf16[384,256]{1,0:T(8,128)(2,1)S(1)} %pad_maximum_fusion.1.own_ref), custom_call_target="tpu_custom_call" | custom-call | flops 60000002048 | bytes 4000000 | tf_op jit(solution)/shard_map/pallas_call | solution.py:201
  33.7 2.4 %shard_map.56.state_ref = f32[1040,384]{1,0:T(8,128)S(1)} custom-call(s32[6]{0:T(128)S(1)} %pad_add_fusion.info_ref, bf16[384,512]{1,0:T(8,128)(2,1)S(1)} %copy-done, bf16[384,512]{1,0:T(8,128)(2,1)S(1)} %collective-permute-done.qo_ref, bf16[384,256]{1,0:T(8,128)(2,1)S(1)} %collective-permute-done.1.piece_ref, f32[1040,384]{1,0:T(8,128)S(1)} %shard_map.55.state_ref), custom_call_target="tpu_custom_call" | custom-call | flops 60000002048 | bytes 6000000 | tf_op jit(solution)/shard_map/pallas_call | solution.py:210
  36.1 2.5 %shard_map.57.here_ref = f32[1040,384]{1,0:T(8,128)S(1)} custom-call(s32[6]{0:T(128)S(1)} %pad_add_fusion.info_ref, bf16[384,512]{1,0:T(8,128)(2,1)S(1)} %copy-done, bf16[384,512]{1,0:T(8,128)(2,1)S(1)} %collective-permute-done.qo_ref, bf16[384,256]{1,0:T(8,128)(2,1)S(1)} %collective-permute-done.2.piece_ref, f32[1040,384]{1,0:T(8,128)S(1)} %shard_map.56.state_ref), custom_call_target="tpu_custom_call" | custom-call | flops 60000002048 | bytes 6000000 | tf_op jit(solution)/shard_map/pallas_call | solution.py:210
  38.6 3.6 %collective-permute-start.3 = (f32[1040,384]{1,0:T(8,128)S(1)}, f32[1040,384]{1,0:T(8,128)}, u32[]{:S(2)}, u32[]{:S(2)}) collective-permute-start(f32[1040,384]{1,0:T(8,128)S(1)} %shard_map.57.here_ref), channel_id=1, source_target_pairs={{0,1},{1,0},{2,3},{3,2},{4,5},{5,4},{6,7},{7,6},{8,9},{9,8},{10,11... | collective-permute-start | bytes 4792328 | tf_op jit(solution)/shard_map/ppermute | solution.py:218
  42.5 2.9 %collective-permute-done.3.there_ref = f32[1040,384]{1,0:T(8,128)} collective-permute-done((f32[1040,384]{1,0:T(8,128)S(1)}, f32[1040,384]{1,0:T(8,128)}, u32[]{:S(2)}, u32[]{:S(2)}) %collective-permute-start.3) | collective-permute-done | bytes 1597472 | tf_op jit(solution)/shard_map/ppermute | solution.py:218
  45.4 3.2 %shard_map.58 = (bf16[384,1024]{1,0:T(8,128)(2,1)S(1)}, bf16[384,512]{1,0:T(8,128)(2,1)S(1)}) custom-call(s32[1]{0:T(128)} %bitcast.1.columns_ref, f32[1040,384]{1,0:T(8,128)S(1)} %shard_map.57.here_ref, f32[1040,384]{1,0:T(8,128)} %collective-permute-done.3.there_ref, bf16[512,8192]{1,0:T(8,128)(2,1)} %wm_ref.9, bf16[512,8192]{1,0:T(8,128)(2,1)} %collective-permute-done.4.wo_ref), custom_call_target="tpu_custom_call" | custom-call | flops 400000000 | bytes 5000000 | tf_op jit(solution)/shard_map/pallas_call | solution.py:229
  48.7 5.1 %collective-permute-start.5 = (bf16[192,512]{1,0:T(8,128)(2,1)S(1)}, bf16[192,512]{1,0:T(8,128)(2,1)S(1)}, u32[]{:S(2)}, u32[]{:S(2)}) collective-permute-start(bf16[192,512]{1,0:T(8,128)(2,1)S(1)} %get-tuple-element.30), channel_id=1, source_target_pairs={{0,2},{1,15},{2,4},{3,1},{4,6},{5,3},{6,8},{7,5},{8,10},{9,7},{10,... | collective-permute-start | bytes 589832 | tf_op jit(solution)/shard_map/ppermute | solution.py:272
  53.9 2.9 %shard_map.62 = bf16[2,384,512]{2,1,0:T(8,128)(2,1)S(1)} custom-call(s32[2]{0:T(128)S(1)} %pad_add_fusion.3.columns_ref, bf16[384,1024]{1,0:T(8,128)(2,1)S(1)} %get-tuple-element.12.att_ref, bf16[512,8192]{1,0:T(8,128)(2,1)} %wm_ref.9, bf16[512,8192]{1,0:T(8,128)(2,1)} %collective-permute-done.4.wo_ref), custom_call_target="tpu_custom_call" | custom-call | flops 805306368 | bytes 6000000 | tf_op jit(solution)/shard_map/pallas_call | solution.py:244
  56.9 3.0 %collective-permute-start.6 = (bf16[192,512]{1,0:T(8,128)(2,1)S(1)}, bf16[192,512]{1,0:T(8,128)(2,1)S(1)}, u32[]{:S(2)}, u32[]{:S(2)}) collective-permute-start(bf16[192,512]{1,0:T(8,128)(2,1)S(1)} %get-tuple-element.29), channel_id=1, source_target_pairs={{0,2},{1,15},{2,4},{3,1},{4,6},{5,3},{6,8},{7,5},{8,10},{9,7},{10,... | collective-permute-start | bytes 589832 | tf_op jit(solution)/shard_map/ppermute | solution.py:272
  59.8 2.9 %shard_map.61 = bf16[2,384,512]{2,1,0:T(8,128)(2,1)S(1)} custom-call(s32[2]{0:T(128)S(1)} %pad_add_fusion.2.columns_ref, bf16[384,1024]{1,0:T(8,128)(2,1)S(1)} %get-tuple-element.12.att_ref, bf16[512,8192]{1,0:T(8,128)(2,1)} %wm_ref.9, bf16[512,8192]{1,0:T(8,128)(2,1)} %collective-permute-done.4.wo_ref), custom_call_target="tpu_custom_call" | custom-call | flops 805306368 | bytes 6000000 | tf_op jit(solution)/shard_map/pallas_call | solution.py:244
  62.9 3.0 %collective-permute-start.7 = (bf16[2,192,512]{2,1,0:T(8,128)(2,1)S(1)}, bf16[2,192,512]{2,1,0:T(8,128)(2,1)S(1)}, u32[]{:S(2)}, u32[]{:S(2)}) collective-permute-start(bf16[2,192,512]{2,1,0:T(8,128)(2,1)S(1)} %add_convert_fusion.3), channel_id=1, source_target_pairs={{0,2},{1,15},{2,4},{3,1},{4,6},{5,3},{6,8},{7,5},{8,10},{9,7},{10,... | collective-permute-start | bytes 1179656 | tf_op jit(solution)/shard_map/ppermute | solution.py:282
  65.9 3.0 %collective-permute-start.8 = (bf16[2,192,512]{2,1,0:T(8,128)(2,1)S(1)}, bf16[2,192,512]{2,1,0:T(8,128)(2,1)S(1)}, u32[]{:S(2)}, u32[]{:S(2)}) collective-permute-start(bf16[2,192,512]{2,1,0:T(8,128)(2,1)S(1)} %add_convert_fusion.2), channel_id=1, source_target_pairs={{0,2},{1,15},{2,4},{3,1},{4,6},{5,3},{6,8},{7,5},{8,10},{9,7},{10,... | collective-permute-start | bytes 1179656 | tf_op jit(solution)/shard_map/ppermute | solution.py:282
  68.9 2.9 %shard_map.60 = bf16[2,384,512]{2,1,0:T(8,128)(2,1)S(1)} custom-call(s32[2]{0:T(128)S(1)} %pad_add_fusion.1.columns_ref, bf16[384,1024]{1,0:T(8,128)(2,1)S(1)} %get-tuple-element.12.att_ref, bf16[512,8192]{1,0:T(8,128)(2,1)} %wm_ref.9, bf16[512,8192]{1,0:T(8,128)(2,1)} %collective-permute-done.4.wo_ref), custom_call_target="tpu_custom_call" | custom-call | flops 805306368 | bytes 6000000 | tf_op jit(solution)/shard_map/pallas_call | solution.py:244
  72.0 3.7 %collective-permute-start.9 = (bf16[2,192,512]{2,1,0:T(8,128)(2,1)S(1)}, bf16[2,192,512]{2,1,0:T(8,128)(2,1)S(1)}, u32[]{:S(2)}, u32[]{:S(2)}) collective-permute-start(bf16[2,192,512]{2,1,0:T(8,128)(2,1)S(1)} %add_convert_fusion.1), channel_id=1, source_target_pairs={{0,2},{1,15},{2,4},{3,1},{4,6},{5,3},{6,8},{7,5},{8,10},{9,7},{10,... | collective-permute-start | bytes 1179656 | tf_op jit(solution)/shard_map/ppermute | solution.py:282
  76.0 3.9 %collective-permute-start.12 = (bf16[2,192,512]{2,1,0:T(8,128)(2,1)S(1)}, bf16[2,192,512]{2,1,0:T(8,128)(2,1)S(1)}, u32[]{:S(2)}, u32[]{:S(2)}) collective-permute-start(bf16[2,192,512]{2,1,0:T(8,128)(2,1)S(1)} %add_convert_fusion), channel_id=1, source_target_pairs={{0,2},{1,15},{2,4},{3,1},{4,6},{5,3},{6,8},{7,5},{8,10},{9,7},{10,... | collective-permute-start | bytes 1179656 | tf_op jit(solution)/shard_map/ppermute | solution.py:282
  80.9 4.6 %collective-permute-start.10 = (bf16[192,512]{1,0:T(8,128)(2,1)S(1)}, bf16[192,512]{1,0:T(8,128)(2,1)S(1)}, u32[]{:S(2)}, u32[]{:S(2)}) collective-permute-start(bf16[192,512]{1,0:T(8,128)(2,1)S(1)} %get-tuple-element.20), channel_id=1, source_target_pairs={{0,2},{1,15},{2,4},{3,1},{4,6},{5,3},{6,8},{7,5},{8,10},{9,7},{10,... | collective-permute-start | bytes 589832 | tf_op jit(solution)/shard_map/ppermute | solution.py:286
  85.6 4.1 %collective-permute-start.13 = (bf16[192,512]{1,0:T(8,128)(2,1)S(1)}, bf16[192,512]{1,0:T(8,128)(2,1)S(1)}, u32[]{:S(2)}, u32[]{:S(2)}) collective-permute-start(bf16[192,512]{1,0:T(8,128)(2,1)S(1)} %get-tuple-element.21), channel_id=1, source_target_pairs={{0,2},{1,15},{2,4},{3,1},{4,6},{5,3},{6,8},{7,5},{8,10},{9,7},{10,... | collective-permute-start | bytes 589832 | tf_op jit(solution)/shard_map/ppermute | solution.py:286
  89.7 5.6 %collective-permute-start.14 = (bf16[192,512]{1,0:T(8,128)(2,1)S(1)}, bf16[192,512]{1,0:T(8,128)(2,1)S(1)}, u32[]{:S(2)}, u32[]{:S(2)}) collective-permute-start(bf16[192,512]{1,0:T(8,128)(2,1)S(1)} %get-tuple-element.22), channel_id=1, source_target_pairs={{0,3},{1,14},{2,5},{3,0},{4,7},{5,2},{6,9},{7,4},{8,11},{9,6},{10,... | collective-permute-start | bytes 589832 | tf_op jit(solution)/shard_map/ppermute | solution.py:286
  99.1 4.4 %collective-permute-done.11 = bf16[192,512]{1,0:T(8,128)(2,1)S(1)} collective-permute-done((bf16[192,512]{1,0:T(8,128)(2,1)S(1)}, bf16[192,512]{1,0:T(8,128)(2,1)S(1)}, u32[]{:S(2)}, u32[]{:S(2)}) %collective-permute-start.11) | collective-permute-done | bytes 196640 | tf_op jit(solution)/shard_map/ppermute | solution.py:286
  (38 shorter events, 9.7 us)
Async XLA Ops:
  0.0 30.5 %collective-permute-start = (bf16[384,512]{1,0:T(8,128)(2,1)}, bf16[384,512]{1,0:T(8,128)(2,1)S(1)}, u32[]{:S(2)}, u32[]{:S(2)}) collective-permute-start(bf16[384,512]{1,0:T(8,128)(2,1)} %qm_ref.5), channel_id=1, source_target_pairs={{0,1},{1,0},{2,3},{3,2},{4,5},{5,4},{6,7},{7,6},{8,9},{9,8},{10,11... | collective-permute-start | bytes 1179656 | tf_op jit(solution)/shard_map/ppermute | solution.py:187
  3.6 18.0 %collective-permute-start.1 = (bf16[384,256]{1,0:T(8,128)(2,1)S(1)}, bf16[384,256]{1,0:T(8,128)(2,1)S(1)}, u32[]{:S(2)}, u32[]{:S(2)}) collective-permute-start(bf16[384,256]{1,0:T(8,128)(2,1)S(1)} %pad_maximum_fusion.1.own_ref), channel_id=1, source_target_pairs={{0,16},{16,32},{32,48},{48,64},{64,80},{80,96},{96,112},{112,128},... | collective-permute-start | bytes 589832 | tf_op jit(solution)/shard_map/ppermute | solution.py:186
  11.2 34.2 %collective-permute-start.4 = (bf16[512,8192]{1,0:T(8,128)(2,1)}, bf16[512,8192]{1,0:T(8,128)(2,1)}, u32[]{:S(2)}, u32[]{:S(2)}) collective-permute-start(bf16[512,8192]{1,0:T(8,128)(2,1)} %wm_ref.9), channel_id=1, source_target_pairs={{0,1},{1,0},{2,3},{3,2},{4,5},{5,4},{6,7},{7,6},{8,9},{9,8},{10,11... | collective-permute-start | bytes 25165832 | tf_op jit(solution)/shard_map/ppermute | solution.py:190
  21.6 14.5 %collective-permute-start.2 = (bf16[384,256]{1,0:T(8,128)(2,1)S(1)}, bf16[384,256]{1,0:T(8,128)(2,1)S(1)}, u32[]{:S(2)}, u32[]{:S(2)}) collective-permute-start(bf16[384,256]{1,0:T(8,128)(2,1)S(1)} %collective-permute-done.1.piece_ref), channel_id=1, source_target_pairs={{0,16},{16,32},{32,48},{48,64},{64,80},{80,96},{96,112},{112,128},... | collective-permute-start | bytes 589832 | tf_op jit(solution)/shard_map/ppermute | solution.py:188
  30.5 1.0 copy-start
  38.6 6.8 %collective-permute-start.3 = (f32[1040,384]{1,0:T(8,128)S(1)}, f32[1040,384]{1,0:T(8,128)}, u32[]{:S(2)}, u32[]{:S(2)}) collective-permute-start(f32[1040,384]{1,0:T(8,128)S(1)} %shard_map.57.here_ref), channel_id=1, source_target_pairs={{0,1},{1,0},{2,3},{3,2},{4,5},{5,4},{6,7},{7,6},{8,9},{9,8},{10,11... | collective-permute-start | bytes 4792328 | tf_op jit(solution)/shard_map/ppermute | solution.py:218
  48.7 14.1 %collective-permute-start.5 = (bf16[192,512]{1,0:T(8,128)(2,1)S(1)}, bf16[192,512]{1,0:T(8,128)(2,1)S(1)}, u32[]{:S(2)}, u32[]{:S(2)}) collective-permute-start(bf16[192,512]{1,0:T(8,128)(2,1)S(1)} %get-tuple-element.30), channel_id=1, source_target_pairs={{0,2},{1,15},{2,4},{3,1},{4,6},{5,3},{6,8},{7,5},{8,10},{9,7},{10,... | collective-permute-start | bytes 589832 | tf_op jit(solution)/shard_map/ppermute | solution.py:272
  56.9 9.0 %collective-permute-start.6 = (bf16[192,512]{1,0:T(8,128)(2,1)S(1)}, bf16[192,512]{1,0:T(8,128)(2,1)S(1)}, u32[]{:S(2)}, u32[]{:S(2)}) collective-permute-start(bf16[192,512]{1,0:T(8,128)(2,1)S(1)} %get-tuple-element.29), channel_id=1, source_target_pairs={{0,2},{1,15},{2,4},{3,1},{4,6},{5,3},{6,8},{7,5},{8,10},{9,7},{10,... | collective-permute-start | bytes 589832 | tf_op jit(solution)/shard_map/ppermute | solution.py:272
  62.9 9.0 %collective-permute-start.7 = (bf16[2,192,512]{2,1,0:T(8,128)(2,1)S(1)}, bf16[2,192,512]{2,1,0:T(8,128)(2,1)S(1)}, u32[]{:S(2)}, u32[]{:S(2)}) collective-permute-start(bf16[2,192,512]{2,1,0:T(8,128)(2,1)S(1)} %add_convert_fusion.3), channel_id=1, source_target_pairs={{0,2},{1,15},{2,4},{3,1},{4,6},{5,3},{6,8},{7,5},{8,10},{9,7},{10,... | collective-permute-start | bytes 1179656 | tf_op jit(solution)/shard_map/ppermute | solution.py:282
  65.9 10.0 %collective-permute-start.8 = (bf16[2,192,512]{2,1,0:T(8,128)(2,1)S(1)}, bf16[2,192,512]{2,1,0:T(8,128)(2,1)S(1)}, u32[]{:S(2)}, u32[]{:S(2)}) collective-permute-start(bf16[2,192,512]{2,1,0:T(8,128)(2,1)S(1)} %add_convert_fusion.2), channel_id=1, source_target_pairs={{0,2},{1,15},{2,4},{3,1},{4,6},{5,3},{6,8},{7,5},{8,10},{9,7},{10,... | collective-permute-start | bytes 1179656 | tf_op jit(solution)/shard_map/ppermute | solution.py:282
  72.0 8.8 %collective-permute-start.9 = (bf16[2,192,512]{2,1,0:T(8,128)(2,1)S(1)}, bf16[2,192,512]{2,1,0:T(8,128)(2,1)S(1)}, u32[]{:S(2)}, u32[]{:S(2)}) collective-permute-start(bf16[2,192,512]{2,1,0:T(8,128)(2,1)S(1)} %add_convert_fusion.1), channel_id=1, source_target_pairs={{0,2},{1,15},{2,4},{3,1},{4,6},{5,3},{6,8},{7,5},{8,10},{9,7},{10,... | collective-permute-start | bytes 1179656 | tf_op jit(solution)/shard_map/ppermute | solution.py:282
  76.0 9.5 %collective-permute-start.12 = (bf16[2,192,512]{2,1,0:T(8,128)(2,1)S(1)}, bf16[2,192,512]{2,1,0:T(8,128)(2,1)S(1)}, u32[]{:S(2)}, u32[]{:S(2)}) collective-permute-start(bf16[2,192,512]{2,1,0:T(8,128)(2,1)S(1)} %add_convert_fusion), channel_id=1, source_target_pairs={{0,2},{1,15},{2,4},{3,1},{4,6},{5,3},{6,8},{7,5},{8,10},{9,7},{10,... | collective-permute-start | bytes 1179656 | tf_op jit(solution)/shard_map/ppermute | solution.py:282
  80.9 18.2 %collective-permute-start.10 = (bf16[192,512]{1,0:T(8,128)(2,1)S(1)}, bf16[192,512]{1,0:T(8,128)(2,1)S(1)}, u32[]{:S(2)}, u32[]{:S(2)}) collective-permute-start(bf16[192,512]{1,0:T(8,128)(2,1)S(1)} %get-tuple-element.20), channel_id=1, source_target_pairs={{0,2},{1,15},{2,4},{3,1},{4,6},{5,3},{6,8},{7,5},{8,10},{9,7},{10,... | collective-permute-start | bytes 589832 | tf_op jit(solution)/shard_map/ppermute | solution.py:286
  85.6 13.5 %collective-permute-start.13 = (bf16[192,512]{1,0:T(8,128)(2,1)S(1)}, bf16[192,512]{1,0:T(8,128)(2,1)S(1)}, u32[]{:S(2)}, u32[]{:S(2)}) collective-permute-start(bf16[192,512]{1,0:T(8,128)(2,1)S(1)} %get-tuple-element.21), channel_id=1, source_target_pairs={{0,2},{1,15},{2,4},{3,1},{4,6},{5,3},{6,8},{7,5},{8,10},{9,7},{10,... | collective-permute-start | bytes 589832 | tf_op jit(solution)/shard_map/ppermute | solution.py:286
  89.7 9.4 %collective-permute-start.14 = (bf16[192,512]{1,0:T(8,128)(2,1)S(1)}, bf16[192,512]{1,0:T(8,128)(2,1)S(1)}, u32[]{:S(2)}, u32[]{:S(2)}) collective-permute-start(bf16[192,512]{1,0:T(8,128)(2,1)S(1)} %get-tuple-element.22), channel_id=1, source_target_pairs={{0,3},{1,14},{2,5},{3,0},{4,7},{5,2},{6,9},{7,4},{8,11},{9,6},{10,... | collective-permute-start | bytes 589832 | tf_op jit(solution)/shard_map/ppermute | solution.py:286
  95.4 8.2 %collective-permute-start.11 = (bf16[192,512]{1,0:T(8,128)(2,1)S(1)}, bf16[192,512]{1,0:T(8,128)(2,1)S(1)}, u32[]{:S(2)}, u32[]{:S(2)}) collective-permute-start(bf16[192,512]{1,0:T(8,128)(2,1)S(1)} %get-tuple-element.19), channel_id=1, source_target_pairs={{0,3},{1,14},{2,5},{3,0},{4,7},{5,2},{6,9},{7,4},{8,11},{9,6},{10,... | collective-permute-start | bytes 589832 | tf_op jit(solution)/shard_map/ppermute | solution.py:286

commit v3 on v2

--- a/solution.py
+++ b/solution.py
@@ -14,6 +14,10 @@
 EXP_SCALE = math.log2(math.e) / HD**0.5
 ROW_PARTS = 2
 AHEAD = 3
+OWN_FLOPS = 60_000_000_000
+PIECE_FLOPS = (60_000_000_000, 60_000_000_000)
+PROJECT_FLOPS = 60_000_000_000
+STATS = 8 * HD
 
 FIRST_BACK = (1, 3)
 SECOND_BACK = (2, 4)
@@ -97,7 +101,7 @@
         store_state(out_ref, pair, unit, top, total, weighted(v_own[:, : (unit + 1) * UNIT], weights))
 
 
-def attend_piece(which, info_ref, qm_ref, qo_ref, piece_ref, state_ref, out_ref):
+def attend_piece(which, info_ref, qm_ref, qo_ref, piece_ref, state_ref, out_ref, message_ref=None):
     units = qm_ref.shape[0] // UNIT
     v_piece = jnp.transpose(piece_ref[:, HD:])
 
@@ -115,19 +119,29 @@
         total = old_total * factor + jnp.sum(weights, axis=0, keepdims=True)
         accum = old_accum * factor + weighted(v_piece, weights)
         store_state(out_ref, pair, unit, top, total, accum)
+        if message_ref is not None:
+            for side in range(2):
+                at = pl.ds((2 * pair + side) * HD, HD), pl.ds(unit * UNIT, UNIT)
+                message_ref[at] = accum[:, side * UNIT : (side + 1) * UNIT].astype(jnp.bfloat16)
+    if message_ref is not None:
+        rest = out_ref[STATS:, :]
+        for term in range(3):
+            rounded = rest.astype(jnp.bfloat16)
+            message_ref[pl.ds(STATS + 16 * term, 16), :] = rounded
+            rest = rest - rounded.astype(jnp.float32)
 
 
 def fetch(columns_ref, block, w_refs, w_buf, sems):
-    wide = w_buf.shape[-1]
+    depth, wide = w_buf.shape[1] // 2, w_buf.shape[2]
     at = pl.ds(pl.multiple_of(columns_ref[block] * wide, wide), wide)
-    return [pltpu.make_async_copy(ref.at[:, at], w_buf.at[block, n], sems.at[block, n]) for n, ref in enumerate(w_refs)]
+    return [
+        pltpu.make_async_copy(ref.at[:, at], w_buf.at[block, pl.ds(n * depth, depth)], sems.at[block, n])
+        for n, ref in enumerate(w_refs)
+    ]
 
 
 def product(att_ref, w_buf, block):
-    depth = w_buf.shape[2]
-    summed = jnp.dot(att_ref[:, :depth], w_buf[block, 0], preferred_element_type=jnp.float32)
-    summed += jnp.dot(att_ref[:, depth:], w_buf[block, 1], preferred_element_type=jnp.float32)
-    return summed.astype(jnp.bfloat16)
+    return jnp.dot(att_ref[...], w_buf[block], preferred_element_type=jnp.float32).astype(jnp.bfloat16)
 
 
 def combine(columns_ref, here_ref, there_ref, wm_ref, wo_ref, att_ref, out_ref, w_buf, sems):
@@ -135,18 +149,17 @@
     copies = fetch(columns_ref, 0, (wm_ref, wo_ref), w_buf, sems)
     for copy in copies:
         copy.start()
+    here = here_ref[STATS:, :]
+    there = sum(there_ref[pl.ds(STATS + 16 * term, 16), :].astype(jnp.float32) for term in (2, 1, 0))
     for head in range(heads):
         other = (head + heads // 2) % heads
-        top_a = here_ref[pl.ds(heads * HD + head, 1), :]
-        top_b = there_ref[pl.ds(heads * HD + other, 1), :]
+        top_a, top_b = here[head : head + 1], there[other : other + 1]
         top = jnp.maximum(top_a, top_b)
         share_a = jnp.exp2((top_a - top) * EXP_SCALE)
         share_b = jnp.exp2((top_b - top) * EXP_SCALE)
-        total = (
-            here_ref[pl.ds(heads * HD + heads + head, 1), :] * share_a
-            + there_ref[pl.ds(heads * HD + heads + other, 1), :] * share_b
-        )
-        accum = here_ref[pl.ds(head * HD, HD), :] * share_a + there_ref[pl.ds(other * HD, HD), :] * share_b
+        total = here[heads + head : heads + head + 1] * share_a + there[heads + other : heads + other + 1] * share_b
+        accum = here_ref[pl.ds(head * HD, HD), :] * share_a
+        accum += there_ref[pl.ds(other * HD, HD), :].astype(jnp.float32) * share_b
         att_ref[:, head * HD : (head + 1) * HD] = jnp.transpose(accum / total).astype(jnp.bfloat16)
     for copy in copies:
         copy.wait()
@@ -154,10 +167,11 @@
 
 
 def project(columns_ref, att_ref, wm_ref, wo_ref, out_ref, w_buf, sems):
-    copies = [fetch(columns_ref, block, (wm_ref, wo_ref), w_buf, sems) for block in range(out_ref.shape[0])]
+    blocks = range(out_ref.shape[0])
+    copies = [fetch(columns_ref, block, (wm_ref, wo_ref), w_buf, sems) for block in blocks]
     for copy in sum(copies, []):
         copy.start()
-    for block in range(out_ref.shape[0]):
+    for block in blocks:
         for copy in copies[block]:
             copy.wait()
         out_ref[block] = product(att_ref, w_buf, block)
@@ -200,22 +214,24 @@
     state_shape = jax.ShapeDtypeStruct((2 * wide + 16, rows), jnp.float32)
     state = pl.pallas_call(
         attend_own,
-        out_shape=state_shape,
+        out_shape=[state_shape],
         in_specs=[SM, VM, VM, VM],
-        out_specs=VM,
+        out_specs=[VM],
         compiler_params=LIMIT,
-        cost_estimate=pl.CostEstimate(flops=60000000000, bytes_accessed=4_000_000, transcendentals=1_000_000),
+        cost_estimate=pl.CostEstimate(flops=OWN_FLOPS, bytes_accessed=4_000_000, transcendentals=1_000_000),
     )(info, queries, q_other, own)
+    message_shape = jax.ShapeDtypeStruct((2 * wide + 48, rows), jnp.bfloat16)
     for which, piece in enumerate((first, second)):
         state = pl.pallas_call(
             functools.partial(attend_piece, which),
-            out_shape=state_shape,
+            out_shape=[state_shape, message_shape][: which + 1],
             in_specs=[SM, VM, VM, VM, VM],
-            out_specs=VM,
+            out_specs=[VM, VM][: which + 1],
             compiler_params=LIMIT,
-            cost_estimate=pl.CostEstimate(flops=60000000000, bytes_accessed=6_000_000, transcendentals=1_000_000),
-        )(info, queries, q_other, piece, state)
-    there = lax.ppermute(state, "core", swap)
+            cost_estimate=pl.CostEstimate(flops=PIECE_FLOPS[which], bytes_accessed=6_000_000, transcendentals=1_000_000),
+        )(info, queries, q_other, piece, state[0])
+    state, message = state
+    there = lax.ppermute(message, "core", swap)
     half = y_count // 2
     way = 1 - 2 * core
 
@@ -224,7 +240,7 @@
         return jnp.stack([2 * chunk + core, 2 * chunk + 1 - core]).astype(jnp.int32)
 
     def w_scratch(count):
-        return [pltpu.VMEM((count, 2, wide, wide), jnp.bfloat16), pltpu.SemaphoreType.DMA((count, 2))]
+        return [pltpu.VMEM((count, 2 * wide, wide), jnp.bfloat16), pltpu.SemaphoreType.DMA((count, 2))]
 
     attended, farthest = pl.pallas_call(
         combine,
@@ -239,19 +255,17 @@
         cost_estimate=pl.CostEstimate(flops=400_000_000, bytes_accessed=5_000_000, transcendentals=10_000),
     )(columns_at(half)[:1], state, there, out_weight, w_other)
 
-    def part(columns):
-        count = columns.shape[0]
-        return pl.pallas_call(
-            project,
-            out_shape=jax.ShapeDtypeStruct((count, rows, wide), jnp.bfloat16),
-            in_specs=[SM, VM, HBM, HBM],
-            out_specs=VM,
-            scratch_shapes=w_scratch(count),
-            compiler_params=WIDE_LIMIT,
-            cost_estimate=pl.CostEstimate(
-                flops=4 * rows * wide * wide * count, bytes_accessed=3_000_000 * count, transcendentals=0
-            ),
-        )(columns, attended, out_weight, w_other)
+    others = jnp.concatenate([*(columns_at(distance) for distance in range(half - 1, 0, -1)), columns_at(0)[:1]])
+    count = 2 * half - 1
+    parts = pl.pallas_call(
+        project,
+        out_shape=jax.ShapeDtypeStruct((count, rows, wide), jnp.bfloat16),
+        in_specs=[SM, VM, HBM, HBM],
+        out_specs=VM,
+        scratch_shapes=w_scratch(count),
+        compiler_params=WIDE_LIMIT,
+        cost_estimate=pl.CostEstimate(flops=PROJECT_FLOPS, bytes_accessed=10_000_000, transcendentals=0),
+    )(others, attended, out_weight, w_other)
 
     straight = [(2 * i + c, 2 * ((i + 1 - 2 * c) % y_count) + c) for i in range(y_count) for c in range(2)]
     cross = [(2 * i + c, 2 * ((i + 1 - 2 * c) % y_count) + 1 - c) for i in range(y_count) for c in range(2)]
@@ -264,8 +278,6 @@
             total = total + b.astype(jnp.float32)
         return total.astype(jnp.bfloat16)
 
-    parts = {distance: part(columns_at(distance)) for distance in range(half - 1, 0, -1)}
-    mine = part(columns_at(0)[:1])[0]
     spots = [slice(r * size, (r + 1) * size) for r in range(ROW_PARTS)]
     got = []
     for at in spots:
@@ -273,10 +285,11 @@
         got.append(lax.pad(value[None], jnp.zeros((), value.dtype), ((0, 1, 0), (0, 0, 0), (0, 0, 0))))
     token = None
     for distance in range(half - 1, 0, -1):
+        first_at = 2 * (half - 1 - distance)
         for r, at in enumerate(spots):
-            now = parts[distance][:, at]
             if token is not None:
-                now, token = lax.optimization_barrier((now, token))
+                parts, token = lax.optimization_barrier((parts, token))
+            now = parts[first_at : first_at + 2, at]
             if distance > 1:
                 token = add(now, got[r])
                 got[r] = lax.ppermute(token, axes, straight)
@@ -284,7 +297,11 @@
                 near, far = add(now[0], got[r][0]), add(now[1], got[r][1])
                 token = near
                 got[r] = (lax.ppermute(near, axes, straight), lax.ppermute(far, axes, cross))
-    outs = [add(mine[at], *got[r]) for r, at in enumerate(spots)]
+    outs = []
+    for r, at in enumerate(spots):
+        if r > 0:
+            parts, outs[-1] = lax.optimization_barrier((parts, outs[-1]))
+        outs.append(add(parts[count - 1, at], *got[r]))
     return jnp.concatenate(outs, axis=0) if ROW_PARTS > 1 else outs[0]
 
 

time: 105 us -> 97.6 us (0.930)
  Pallas kernels: 20.9 us -> 15.2 us
  starting transfers between devices: 62.4 us -> 60.7 us
    pallas_call x7 -> x4, Pallas kernels: 17.6 us -> 13 us  [the longest x1 5.94 us: on_device(): pl.pallas_call(project, out_shape=jax.ShapeDtypeStruct((count, rows, wide...]
    ppermute x1, waiting for transfers between devices: 7.36 us -> 4.72 us  [on_device(): first = lax.ppermute(own, ('dp', 'core'), first_pairs)]
    ppermute x4, waiting for transfers between devices: 1.09 us -> 3.69 us  [on_device(): got[r] = lax.ppermute(token, axes, straight)]
    ppermute x2, waiting for transfers between devices: 0.01 us -> 2.22 us  [on_device(): lax.ppermute(near, axes, straight)]
    ppermute x2, starting transfers between devices: 8.66 us -> 6.73 us  [on_device(): lax.ppermute(near, axes, straight)]
    ppermute x1, waiting for transfers between devices: 2.94 us -> 1.77 us  [on_device(): there = lax.ppermute(message, 'core', swap)]
  transfers between devices with their start and end apart: 15 -> 15, of which waited for: 5 -> 7; matrix products, arithmetic and copies ran while one was open for 3% -> 2% of each run, Pallas kernels for 17% -> 13%
where the time goes in v3:
time: 97.6 us; the launch traced here: 97 us
  starting transfers between devices  60.7 us (62%)
  waiting for transfers between devices  16.1 us (16%)
  Pallas kernels  15.2 us (16%)
  other arithmetic  2.52 us (3%)
  local copies, waits for them, and re-layouts  2.06 us (2%)
    ppermute x4, starting transfers between devices, on_device(): got[r] = lax.ppermute(token, axes, straight)  13.7 us
    ppermute x1, starting transfers between devices, on_device(): lax.ppermute(first, 'dp', [(i, i + 1) for i in range(dp_count - 1)])  8.54 us
    ppermute x2, starting transfers between devices, on_device(): value = lax.ppermute(farthest[at], axes, straight)  8.08 us
    ppermute x1, starting transfers between devices, on_device(): first = lax.ppermute(own, ('dp', 'core'), first_pairs)  7.62 us
    ppermute x2, starting transfers between devices, on_device(): lax.ppermute(far, axes, cross)  7.4 us
    ppermute x2, starting transfers between devices, on_device(): lax.ppermute(near, axes, straight)  6.73 us
    pallas_call x1, Pallas kernels, on_device(): pl.pallas_call(project, out_shape=jax.ShapeDtypeStruct((count, rows, wide...  5.94 us
    pallas_call x2, Pallas kernels, on_device(): pl.pallas_call(functools.partial(attend_piece, which), out_shape=[state_s...  4.9 us
  transfers between devices with their start and end apart: 15, of which 7 were waited for; matrix products, arithmetic and copies ran while one was open for 2% of the time, Pallas kernels for 13%

profile of v3, /device:TPU:7, one launch (start us, length us, event | category | flops | bytes accessed | tf_op | source)
XLA Modules:
  0.0 97.0 jit_solution(4137620571028827680)
XLA Ops:
  1.0 7.6 %collective-permute-start.1 = (bf16[384,256]{1,0:T(8,128)(2,1)S(1)}, bf16[384,256]{1,0:T(8,128)(2,1)S(1)}, u32[]{:S(2)}, u32[]{:S(2)}) collective-permute-start(bf16[384,256]{1,0:T(8,128)(2,1)S(1)} %pad_maximum_fusion.1.own_ref), channel_id=1, source_target_pairs={{0,16},{16,32},{32,48},{48,64},{64,80},{80,96},{96,112},{112,128},... | collective-permute-start | bytes 589832 | tf_op jit(solution)/shard_map/ppermute | solution.py:200
  8.6 1.9 %collective-permute-start = (bf16[384,512]{1,0:T(8,128)(2,1)}, bf16[384,512]{1,0:T(8,128)(2,1)S(1)}, u32[]{:S(2)}, u32[]{:S(2)}) collective-permute-start(bf16[384,512]{1,0:T(8,128)(2,1)} %qm_ref.5), channel_id=1, source_target_pairs={{0,1},{1,0},{2,3},{3,2},{4,5},{5,4},{6,7},{7,6},{8,9},{9,8},{10,11... | collective-permute-start | bytes 1179656 | tf_op jit(solution)/shard_map/ppermute | solution.py:201
  10.5 2.4 %collective-permute-start.4 = (bf16[512,8192]{1,0:T(8,128)(2,1)}, bf16[512,8192]{1,0:T(8,128)(2,1)}, u32[]{:S(2)}, u32[]{:S(2)}) collective-permute-start(bf16[512,8192]{1,0:T(8,128)(2,1)} %wm_ref.3), channel_id=1, source_target_pairs={{0,1},{1,0},{2,3},{3,2},{4,5},{5,4},{6,7},{7,6},{8,9},{9,8},{10,11... | collective-permute-start | bytes 25165832 | tf_op jit(solution)/shard_map/ppermute | solution.py:204
  14.1 4.7 %collective-permute-done.1.piece_ref = bf16[384,256]{1,0:T(8,128)(2,1)S(1)} collective-permute-done((bf16[384,256]{1,0:T(8,128)(2,1)S(1)}, bf16[384,256]{1,0:T(8,128)(2,1)S(1)}, u32[]{:S(2)}, u32[]{:S(2)}) %collective-permute-start.1) | collective-permute-done | bytes 196640 | tf_op jit(solution)/shard_map/ppermute | solution.py:200
  18.8 8.5 %collective-permute-start.2 = (bf16[384,256]{1,0:T(8,128)(2,1)S(1)}, bf16[384,256]{1,0:T(8,128)(2,1)S(1)}, u32[]{:S(2)}, u32[]{:S(2)}) collective-permute-start(bf16[384,256]{1,0:T(8,128)(2,1)S(1)} %collective-permute-done.1.piece_ref), channel_id=1, source_target_pairs={{0,16},{16,32},{32,48},{48,64},{64,80},{80,96},{96,112},{112,128},... | collective-permute-start | bytes 589832 | tf_op jit(solution)/shard_map/ppermute | solution.py:202
  28.4 2.1 %shard_map.55.state_ref = f32[1040,384]{1,0:T(8,128)S(1)} custom-call(s32[6]{0:T(128)S(1)} %pad_add_fusion.info_ref, bf16[384,512]{1,0:T(8,128)(2,1)S(1)} %copy-done, bf16[384,512]{1,0:T(8,128)(2,1)S(1)} %collective-permute-done.qo_ref, bf16[384,256]{1,0:T(8,128)(2,1)S(1)} %pad_maximum_fusion.1.own_ref), custom_call_target="tpu_custom_call" | custom-call | flops 60000002048 | bytes 4000000 | tf_op jit(solution)/shard_map/pallas_call | solution.py:215
  30.5 2.4 %shard_map.56.state_ref = f32[1040,384]{1,0:T(8,128)S(1)} custom-call(s32[6]{0:T(128)S(1)} %pad_add_fusion.info_ref, bf16[384,512]{1,0:T(8,128)(2,1)S(1)} %copy-done, bf16[384,512]{1,0:T(8,128)(2,1)S(1)} %collective-permute-done.qo_ref, bf16[384,256]{1,0:T(8,128)(2,1)S(1)} %collective-permute-done.1.piece_ref, f32[1040,384]{1,0:T(8,128)S(1)} %shard_map.55.state_ref), custom_call_target="tpu_custom_call" | custom-call | flops 60000002048 | bytes 6000000 | tf_op jit(solution)/shard_map/pallas_call | solution.py:225
  32.9 2.5 %shard_map.57 = (f32[1040,384]{1,0:T(8,128)S(1)}, bf16[1072,384]{1,0:T(8,128)(2,1)S(1)}) custom-call(s32[6]{0:T(128)S(1)} %pad_add_fusion.info_ref, bf16[384,512]{1,0:T(8,128)(2,1)S(1)} %copy-done, bf16[384,512]{1,0:T(8,128)(2,1)S(1)} %collective-permute-done.qo_ref, bf16[384,256]{1,0:T(8,128)(2,1)S(1)} %collective-permute-done.2.piece_ref, ...), custom_call_target="tpu_custom_call" | custom-call | flops 60000002048 | bytes 6000000 | tf_op jit(solution)/shard_map/pallas_call | solution.py:225
  35.4 4.2 %collective-permute-start.3 = (bf16[1072,384]{1,0:T(8,128)(2,1)S(1)}, bf16[1072,384]{1,0:T(8,128)(2,1)S(1)}, u32[]{:S(2)}, u32[]{:S(2)}) collective-permute-start(bf16[1072,384]{1,0:T(8,128)(2,1)S(1)} %get-tuple-element.17), channel_id=1, source_target_pairs={{0,1},{1,0},{2,3},{3,2},{4,5},{5,4},{6,7},{7,6},{8,9},{9,8},{10,11... | collective-permute-start | bytes 2469896 | tf_op jit(solution)/shard_map/ppermute | solution.py:234
  41.6 2.2 %shard_map.58 = (bf16[384,1024]{1,0:T(8,128)(2,1)S(1)}, bf16[384,512]{1,0:T(8,128)(2,1)S(1)}) custom-call(s32[1]{0:T(128)} %bitcast.7.columns_ref, f32[1040,384]{1,0:T(8,128)S(1)} %get-tuple-element.16.here_ref, bf16[1072,384]{1,0:T(8,128)(2,1)S(1)} %collective-permute-done.3.there_ref, bf16[512,8192]{1,0:T(8,128)(2,1)} %wm_ref.3, ...), custom_call_target="tpu_custom_call" | custom-call | flops 400000000 | bytes 5000000 | tf_op jit(solution)/shard_map/pallas_call | solution.py:245
  43.8 5.1 %collective-permute-start.5 = (bf16[192,512]{1,0:T(8,128)(2,1)S(1)}, bf16[192,512]{1,0:T(8,128)(2,1)S(1)}, u32[]{:S(2)}, u32[]{:S(2)}) collective-permute-start(bf16[192,512]{1,0:T(8,128)(2,1)S(1)} %get-tuple-element.31), channel_id=1, source_target_pairs={{0,2},{1,15},{2,4},{3,1},{4,6},{5,3},{6,8},{7,5},{8,10},{9,7},{10,... | collective-permute-start | bytes 589832 | tf_op jit(solution)/shard_map/ppermute | solution.py:284
  48.9 3.0 %collective-permute-start.6 = (bf16[192,512]{1,0:T(8,128)(2,1)S(1)}, bf16[192,512]{1,0:T(8,128)(2,1)S(1)}, u32[]{:S(2)}, u32[]{:S(2)}) collective-permute-start(bf16[192,512]{1,0:T(8,128)(2,1)S(1)} %get-tuple-element.32), channel_id=1, source_target_pairs={{0,2},{1,15},{2,4},{3,1},{4,6},{5,3},{6,8},{7,5},{8,10},{9,7},{10,... | collective-permute-start | bytes 589832 | tf_op jit(solution)/shard_map/ppermute | solution.py:284
  51.9 5.9 %shard_map.59 = bf16[7,384,512]{2,1,0:T(8,128)(2,1)S(1)} custom-call(s32[7]{0:T(128)S(1)} %concatenate.12.columns_ref, bf16[384,1024]{1,0:T(8,128)(2,1)S(1)} %get-tuple-element.18.att_ref, bf16[512,8192]{1,0:T(8,128)(2,1)} %wm_ref.3, bf16[512,8192]{1,0:T(8,128)(2,1)} %collective-permute-done.4.wo_ref), custom_call_target="tpu_custom_call" | custom-call | flops 60000002048 | bytes 10000000 | tf_op jit(solution)/shard_map/pallas_call | solution.py:260
  57.9 3.0 %collective-permute-start.7 = (bf16[2,192,512]{2,1,0:T(8,128)(2,1)S(1)}, bf16[2,192,512]{2,1,0:T(8,128)(2,1)S(1)}, u32[]{:S(2)}, u32[]{:S(2)}) collective-permute-start(bf16[2,192,512]{2,1,0:T(8,128)(2,1)S(1)} %add_convert_fusion.3), channel_id=1, source_target_pairs={{0,2},{1,15},{2,4},{3,1},{4,6},{5,3},{6,8},{7,5},{8,10},{9,7},{10,... | collective-permute-start | bytes 1179656 | tf_op jit(solution)/shard_map/ppermute | solution.py:295
  61.0 3.0 %collective-permute-start.8 = (bf16[2,192,512]{2,1,0:T(8,128)(2,1)S(1)}, bf16[2,192,512]{2,1,0:T(8,128)(2,1)S(1)}, u32[]{:S(2)}, u32[]{:S(2)}) collective-permute-start(bf16[2,192,512]{2,1,0:T(8,128)(2,1)S(1)} %add_convert_fusion.2), channel_id=1, source_target_pairs={{0,2},{1,15},{2,4},{3,1},{4,6},{5,3},{6,8},{7,5},{8,10},{9,7},{10,... | collective-permute-start | bytes 1179656 | tf_op jit(solution)/shard_map/ppermute | solution.py:295
  64.0 2.8 %collective-permute-done.7 = bf16[2,192,512]{2,1,0:T(8,128)(2,1)S(1)} collective-permute-done((bf16[2,192,512]{2,1,0:T(8,128)(2,1)S(1)}, bf16[2,192,512]{2,1,0:T(8,128)(2,1)S(1)}, u32[]{:S(2)}, u32[]{:S(2)}) %collective-permute-start.7) | collective-permute-done | bytes 393248 | tf_op jit(solution)/shard_map/ppermute | solution.py:295
  66.9 3.9 %collective-permute-start.9 = (bf16[2,192,512]{2,1,0:T(8,128)(2,1)S(1)}, bf16[2,192,512]{2,1,0:T(8,128)(2,1)S(1)}, u32[]{:S(2)}, u32[]{:S(2)}) collective-permute-start(bf16[2,192,512]{2,1,0:T(8,128)(2,1)S(1)} %add_convert_fusion.1), channel_id=1, source_target_pairs={{0,2},{1,15},{2,4},{3,1},{4,6},{5,3},{6,8},{7,5},{8,10},{9,7},{10,... | collective-permute-start | bytes 1179656 | tf_op jit(solution)/shard_map/ppermute | solution.py:295
  71.1 3.9 %collective-permute-start.12 = (bf16[2,192,512]{2,1,0:T(8,128)(2,1)S(1)}, bf16[2,192,512]{2,1,0:T(8,128)(2,1)S(1)}, u32[]{:S(2)}, u32[]{:S(2)}) collective-permute-start(bf16[2,192,512]{2,1,0:T(8,128)(2,1)S(1)} %add_convert_fusion), channel_id=1, source_target_pairs={{0,2},{1,15},{2,4},{3,1},{4,6},{5,3},{6,8},{7,5},{8,10},{9,7},{10,... | collective-permute-start | bytes 1179656 | tf_op jit(solution)/shard_map/ppermute | solution.py:295
  75.8 4.8 %collective-permute-start.10 = (bf16[192,512]{1,0:T(8,128)(2,1)S(1)}, bf16[192,512]{1,0:T(8,128)(2,1)S(1)}, u32[]{:S(2)}, u32[]{:S(2)}) collective-permute-start(bf16[192,512]{1,0:T(8,128)(2,1)S(1)} %get-tuple-element.28), channel_id=1, source_target_pairs={{0,2},{1,15},{2,4},{3,1},{4,6},{5,3},{6,8},{7,5},{8,10},{9,7},{10,... | collective-permute-start | bytes 589832 | tf_op jit(solution)/shard_map/ppermute | solution.py:299
  80.6 5.2 %collective-permute-start.11 = (bf16[192,512]{1,0:T(8,128)(2,1)S(1)}, bf16[192,512]{1,0:T(8,128)(2,1)S(1)}, u32[]{:S(2)}, u32[]{:S(2)}) collective-permute-start(bf16[192,512]{1,0:T(8,128)(2,1)S(1)} %get-tuple-element.27), channel_id=1, source_target_pairs={{0,3},{1,14},{2,5},{3,0},{4,7},{5,2},{6,9},{7,4},{8,11},{9,6},{10,... | collective-permute-start | bytes 589832 | tf_op jit(solution)/shard_map/ppermute | solution.py:299
  86.0 1.9 %collective-permute-start.13 = (bf16[192,512]{1,0:T(8,128)(2,1)S(1)}, bf16[192,512]{1,0:T(8,128)(2,1)S(1)}, u32[]{:S(2)}, u32[]{:S(2)}) collective-permute-start(bf16[192,512]{1,0:T(8,128)(2,1)S(1)} %get-tuple-element.29), channel_id=1, source_target_pairs={{0,2},{1,15},{2,4},{3,1},{4,6},{5,3},{6,8},{7,5},{8,10},{9,7},{10,... | collective-permute-start | bytes 589832 | tf_op jit(solution)/shard_map/ppermute | solution.py:299
  87.9 2.2 %collective-permute-start.14 = (bf16[192,512]{1,0:T(8,128)(2,1)S(1)}, bf16[192,512]{1,0:T(8,128)(2,1)S(1)}, u32[]{:S(2)}, u32[]{:S(2)}) collective-permute-start(bf16[192,512]{1,0:T(8,128)(2,1)S(1)} %get-tuple-element.30), channel_id=1, source_target_pairs={{0,3},{1,14},{2,5},{3,0},{4,7},{5,2},{6,9},{7,4},{8,11},{9,6},{10,... | collective-permute-start | bytes 589832 | tf_op jit(solution)/shard_map/ppermute | solution.py:299
  90.2 2.2 %collective-permute-done.13 = bf16[192,512]{1,0:T(8,128)(2,1)S(1)} collective-permute-done((bf16[192,512]{1,0:T(8,128)(2,1)S(1)}, bf16[192,512]{1,0:T(8,128)(2,1)S(1)}, u32[]{:S(2)}, u32[]{:S(2)}) %collective-permute-start.13) | collective-permute-done | bytes 196640 | tf_op jit(solution)/shard_map/ppermute | solution.py:299
  92.4 3.7 %collective-permute-done.14 = bf16[192,512]{1,0:T(8,128)(2,1)S(1)} collective-permute-done((bf16[192,512]{1,0:T(8,128)(2,1)S(1)}, bf16[192,512]{1,0:T(8,128)(2,1)S(1)}, u32[]{:S(2)}, u32[]{:S(2)}) %collective-permute-start.14) | collective-permute-done | bytes 196640 | tf_op jit(solution)/shard_map/ppermute | solution.py:299
  (31 shorter events, 7.3 us)
Async XLA Ops:
  1.0 17.8 %collective-permute-start.1 = (bf16[384,256]{1,0:T(8,128)(2,1)S(1)}, bf16[384,256]{1,0:T(8,128)(2,1)S(1)}, u32[]{:S(2)}, u32[]{:S(2)}) collective-permute-start(bf16[384,256]{1,0:T(8,128)(2,1)S(1)} %pad_maximum_fusion.1.own_ref), channel_id=1, source_target_pairs={{0,16},{16,32},{32,48},{48,64},{64,80},{80,96},{96,112},{112,128},... | collective-permute-start | bytes 589832 | tf_op jit(solution)/shard_map/ppermute | solution.py:200
  8.6 18.7 %collective-permute-start = (bf16[384,512]{1,0:T(8,128)(2,1)}, bf16[384,512]{1,0:T(8,128)(2,1)S(1)}, u32[]{:S(2)}, u32[]{:S(2)}) collective-permute-start(bf16[384,512]{1,0:T(8,128)(2,1)} %qm_ref.5), channel_id=1, source_target_pairs={{0,1},{1,0},{2,3},{3,2},{4,5},{5,4},{6,7},{7,6},{8,9},{9,8},{10,11... | collective-permute-start | bytes 1179656 | tf_op jit(solution)/shard_map/ppermute | solution.py:201
  10.5 31.1 %collective-permute-start.4 = (bf16[512,8192]{1,0:T(8,128)(2,1)}, bf16[512,8192]{1,0:T(8,128)(2,1)}, u32[]{:S(2)}, u32[]{:S(2)}) collective-permute-start(bf16[512,8192]{1,0:T(8,128)(2,1)} %wm_ref.3), channel_id=1, source_target_pairs={{0,1},{1,0},{2,3},{3,2},{4,5},{5,4},{6,7},{7,6},{8,9},{9,8},{10,11... | collective-permute-start | bytes 25165832 | tf_op jit(solution)/shard_map/ppermute | solution.py:204
  18.8 14.1 %collective-permute-start.2 = (bf16[384,256]{1,0:T(8,128)(2,1)S(1)}, bf16[384,256]{1,0:T(8,128)(2,1)S(1)}, u32[]{:S(2)}, u32[]{:S(2)}) collective-permute-start(bf16[384,256]{1,0:T(8,128)(2,1)S(1)} %collective-permute-done.1.piece_ref), channel_id=1, source_target_pairs={{0,16},{16,32},{32,48},{48,64},{64,80},{80,96},{96,112},{112,128},... | collective-permute-start | bytes 589832 | tf_op jit(solution)/shard_map/ppermute | solution.py:202
  27.4 1.0 %copy-start = (bf16[384,512]{1,0:T(8,128)(2,1)S(1)}, bf16[384,512]{1,0:T(8,128)(2,1)}, u32[]{:S(2)}) copy-start(bf16[384,512]{1,0:T(8,128)(2,1)} %qm_ref.5) | copy-start | bytes 1179652
  35.4 6.2 %collective-permute-start.3 = (bf16[1072,384]{1,0:T(8,128)(2,1)S(1)}, bf16[1072,384]{1,0:T(8,128)(2,1)S(1)}, u32[]{:S(2)}, u32[]{:S(2)}) collective-permute-start(bf16[1072,384]{1,0:T(8,128)(2,1)S(1)} %get-tuple-element.17), channel_id=1, source_target_pairs={{0,1},{1,0},{2,3},{3,2},{4,5},{5,4},{6,7},{7,6},{8,9},{9,8},{10,11... | collective-permute-start | bytes 2469896 | tf_op jit(solution)/shard_map/ppermute | solution.py:234
  43.8 14.0 %collective-permute-start.5 = (bf16[192,512]{1,0:T(8,128)(2,1)S(1)}, bf16[192,512]{1,0:T(8,128)(2,1)S(1)}, u32[]{:S(2)}, u32[]{:S(2)}) collective-permute-start(bf16[192,512]{1,0:T(8,128)(2,1)S(1)} %get-tuple-element.31), channel_id=1, source_target_pairs={{0,2},{1,15},{2,4},{3,1},{4,6},{5,3},{6,8},{7,5},{8,10},{9,7},{10,... | collective-permute-start | bytes 589832 | tf_op jit(solution)/shard_map/ppermute | solution.py:284
  48.9 12.0 %collective-permute-start.6 = (bf16[192,512]{1,0:T(8,128)(2,1)S(1)}, bf16[192,512]{1,0:T(8,128)(2,1)S(1)}, u32[]{:S(2)}, u32[]{:S(2)}) collective-permute-start(bf16[192,512]{1,0:T(8,128)(2,1)S(1)} %get-tuple-element.32), channel_id=1, source_target_pairs={{0,2},{1,15},{2,4},{3,1},{4,6},{5,3},{6,8},{7,5},{8,10},{9,7},{10,... | collective-permute-start | bytes 589832 | tf_op jit(solution)/shard_map/ppermute | solution.py:284
  57.9 8.8 %collective-permute-start.7 = (bf16[2,192,512]{2,1,0:T(8,128)(2,1)S(1)}, bf16[2,192,512]{2,1,0:T(8,128)(2,1)S(1)}, u32[]{:S(2)}, u32[]{:S(2)}) collective-permute-start(bf16[2,192,512]{2,1,0:T(8,128)(2,1)S(1)} %add_convert_fusion.3), channel_id=1, source_target_pairs={{0,2},{1,15},{2,4},{3,1},{4,6},{5,3},{6,8},{7,5},{8,10},{9,7},{10,... | collective-permute-start | bytes 1179656 | tf_op jit(solution)/shard_map/ppermute | solution.py:295
  61.0 10.0 %collective-permute-start.8 = (bf16[2,192,512]{2,1,0:T(8,128)(2,1)S(1)}, bf16[2,192,512]{2,1,0:T(8,128)(2,1)S(1)}, u32[]{:S(2)}, u32[]{:S(2)}) collective-permute-start(bf16[2,192,512]{2,1,0:T(8,128)(2,1)S(1)} %add_convert_fusion.2), channel_id=1, source_target_pairs={{0,2},{1,15},{2,4},{3,1},{4,6},{5,3},{6,8},{7,5},{8,10},{9,7},{10,... | collective-permute-start | bytes 1179656 | tf_op jit(solution)/shard_map/ppermute | solution.py:295
  66.9 8.8 %collective-permute-start.9 = (bf16[2,192,512]{2,1,0:T(8,128)(2,1)S(1)}, bf16[2,192,512]{2,1,0:T(8,128)(2,1)S(1)}, u32[]{:S(2)}, u32[]{:S(2)}) collective-permute-start(bf16[2,192,512]{2,1,0:T(8,128)(2,1)S(1)} %add_convert_fusion.1), channel_id=1, source_target_pairs={{0,2},{1,15},{2,4},{3,1},{4,6},{5,3},{6,8},{7,5},{8,10},{9,7},{10,... | collective-permute-start | bytes 1179656 | tf_op jit(solution)/shard_map/ppermute | solution.py:295
  71.1 14.8 %collective-permute-start.12 = (bf16[2,192,512]{2,1,0:T(8,128)(2,1)S(1)}, bf16[2,192,512]{2,1,0:T(8,128)(2,1)S(1)}, u32[]{:S(2)}, u32[]{:S(2)}) collective-permute-start(bf16[2,192,512]{2,1,0:T(8,128)(2,1)S(1)} %add_convert_fusion), channel_id=1, source_target_pairs={{0,2},{1,15},{2,4},{3,1},{4,6},{5,3},{6,8},{7,5},{8,10},{9,7},{10,... | collective-permute-start | bytes 1179656 | tf_op jit(solution)/shard_map/ppermute | solution.py:295
  75.8 14.3 %collective-permute-start.10 = (bf16[192,512]{1,0:T(8,128)(2,1)S(1)}, bf16[192,512]{1,0:T(8,128)(2,1)S(1)}, u32[]{:S(2)}, u32[]{:S(2)}) collective-permute-start(bf16[192,512]{1,0:T(8,128)(2,1)S(1)} %get-tuple-element.28), channel_id=1, source_target_pairs={{0,2},{1,15},{2,4},{3,1},{4,6},{5,3},{6,8},{7,5},{8,10},{9,7},{10,... | collective-permute-start | bytes 589832 | tf_op jit(solution)/shard_map/ppermute | solution.py:299
  80.6 9.5 %collective-permute-start.11 = (bf16[192,512]{1,0:T(8,128)(2,1)S(1)}, bf16[192,512]{1,0:T(8,128)(2,1)S(1)}, u32[]{:S(2)}, u32[]{:S(2)}) collective-permute-start(bf16[192,512]{1,0:T(8,128)(2,1)S(1)} %get-tuple-element.27), channel_id=1, source_target_pairs={{0,3},{1,14},{2,5},{3,0},{4,7},{5,2},{6,9},{7,4},{8,11},{9,6},{10,... | collective-permute-start | bytes 589832 | tf_op jit(solution)/shard_map/ppermute | solution.py:299
  86.0 6.4 %collective-permute-start.13 = (bf16[192,512]{1,0:T(8,128)(2,1)S(1)}, bf16[192,512]{1,0:T(8,128)(2,1)S(1)}, u32[]{:S(2)}, u32[]{:S(2)}) collective-permute-start(bf16[192,512]{1,0:T(8,128)(2,1)S(1)} %get-tuple-element.29), channel_id=1, source_target_pairs={{0,2},{1,15},{2,4},{3,1},{4,6},{5,3},{6,8},{7,5},{8,10},{9,7},{10,... | collective-permute-start | bytes 589832 | tf_op jit(solution)/shard_map/ppermute | solution.py:299
  87.9 8.2 %collective-permute-start.14 = (bf16[192,512]{1,0:T(8,128)(2,1)S(1)}, bf16[192,512]{1,0:T(8,128)(2,1)S(1)}, u32[]{:S(2)}, u32[]{:S(2)}) collective-permute-start(bf16[192,512]{1,0:T(8,128)(2,1)S(1)} %get-tuple-element.30), channel_id=1, source_target_pairs={{0,3},{1,14},{2,5},{3,0},{4,7},{5,2},{6,9},{7,4},{8,11},{9,6},{10,... | collective-permute-start | bytes 589832 | tf_op jit(solution)/shard_map/ppermute | solution.py:299

commit v4 on v3

--- a/solution.py
+++ b/solution.py
@@ -12,7 +12,6 @@
 UNIT = 128
 NEG = -1e30
 EXP_SCALE = math.log2(math.e) / HD**0.5
-ROW_PARTS = 2
 AHEAD = 3
 OWN_FLOPS = 60_000_000_000
 PIECE_FLOPS = (60_000_000_000, 60_000_000_000)
@@ -166,15 +165,15 @@
     out_ref[...] = product(att_ref, w_buf, 0)
 
 
-def project(columns_ref, att_ref, wm_ref, wo_ref, out_ref, w_buf, sems):
-    blocks = range(out_ref.shape[0])
-    copies = [fetch(columns_ref, block, (wm_ref, wo_ref), w_buf, sems) for block in blocks]
+def project(count, columns_ref, att_ref, wm_ref, wo_ref, *rest):
+    out_refs, (w_buf, sems) = rest[:count], rest[count:]
+    copies = [fetch(columns_ref, block, (wm_ref, wo_ref), w_buf, sems) for block in range(count)]
     for copy in sum(copies, []):
         copy.start()
-    for block in blocks:
+    for block in range(count):
         for copy in copies[block]:
             copy.wait()
-        out_ref[block] = product(att_ref, w_buf, block)
+        out_refs[block][...] = product(att_ref, w_buf, block)
 
 
 VM = pl.BlockSpec(memory_space=pltpu.VMEM)
@@ -255,22 +254,21 @@
         cost_estimate=pl.CostEstimate(flops=400_000_000, bytes_accessed=5_000_000, transcendentals=10_000),
     )(columns_at(half)[:1], state, there, out_weight, w_other)
 
-    others = jnp.concatenate([*(columns_at(distance) for distance in range(half - 1, 0, -1)), columns_at(0)[:1]])
-    count = 2 * half - 1
-    parts = pl.pallas_call(
-        project,
-        out_shape=jax.ShapeDtypeStruct((count, rows, wide), jnp.bfloat16),
-        in_specs=[SM, VM, HBM, HBM],
-        out_specs=VM,
-        scratch_shapes=w_scratch(count),
-        compiler_params=WIDE_LIMIT,
-        cost_estimate=pl.CostEstimate(flops=PROJECT_FLOPS, bytes_accessed=10_000_000, transcendentals=0),
-    )(others, attended, out_weight, w_other)
+    def part(columns):
+        count = columns.shape[0]
+        return pl.pallas_call(
+            functools.partial(project, count),
+            out_shape=[jax.ShapeDtypeStruct((rows, wide), jnp.bfloat16)] * count,
+            in_specs=[SM, VM, HBM, HBM],
+            out_specs=[VM] * count,
+            scratch_shapes=w_scratch(count),
+            compiler_params=WIDE_LIMIT,
+            cost_estimate=pl.CostEstimate(flops=PROJECT_FLOPS, bytes_accessed=10_000_000, transcendentals=0),
+        )(columns, attended, out_weight, w_other)
 
     straight = [(2 * i + c, 2 * ((i + 1 - 2 * c) % y_count) + c) for i in range(y_count) for c in range(2)]
     cross = [(2 * i + c, 2 * ((i + 1 - 2 * c) % y_count) + 1 - c) for i in range(y_count) for c in range(2)]
     axes = ("y", "core")
-    size = rows // ROW_PARTS
 
     def add(a, *others):
         total = a.astype(jnp.float32)
@@ -278,31 +276,20 @@
             total = total + b.astype(jnp.float32)
         return total.astype(jnp.bfloat16)
 
-    spots = [slice(r * size, (r + 1) * size) for r in range(ROW_PARTS)]
-    got = []
-    for at in spots:
-        value = lax.ppermute(farthest[at], axes, straight)
-        got.append(lax.pad(value[None], jnp.zeros((), value.dtype), ((0, 1, 0), (0, 0, 0), (0, 0, 0))))
-    token = None
+    near = lax.ppermute(farthest, axes, straight)
+    now = part(columns_at(half - 1))
+    far = lax.ppermute(now[1], axes, straight)
     for distance in range(half - 1, 0, -1):
-        first_at = 2 * (half - 1 - distance)
-        for r, at in enumerate(spots):
-            if token is not None:
-                parts, token = lax.optimization_barrier((parts, token))
-            now = parts[first_at : first_at + 2, at]
-            if distance > 1:
-                token = add(now, got[r])
-                got[r] = lax.ppermute(token, axes, straight)
-            else:
-                near, far = add(now[0], got[r][0]), add(now[1], got[r][1])
-                token = near
-                got[r] = (lax.ppermute(near, axes, straight), lax.ppermute(far, axes, cross))
-    outs = []
-    for r, at in enumerate(spots):
-        if r > 0:
-            parts, outs[-1] = lax.optimization_barrier((parts, outs[-1]))
-        outs.append(add(parts[count - 1, at], *got[r]))
-    return jnp.concatenate(outs, axis=0) if ROW_PARTS > 1 else outs[0]
+        send = add(now[0], near)
+        near = lax.ppermute(send, axes, straight)
+        if distance > 1:
+            now = part(columns_at(distance - 1))
+            now, send = lax.optimization_barrier((now, send))
+            send = add(now[1], far)
+            far = lax.ppermute(send, axes, straight if distance > 2 else cross)
+            now, send = lax.optimization_barrier((now, send))
+    mine = part(columns_at(0)[:1])[0]
+    return add(mine, near, far)
 
 
 def solution(mesh):

time: 97.6 us -> 91.9 us (0.942)
  the two profiles are of different devices: /device:TPU:7 before, /device:TPU:31 now
where the time goes in v4:
time: 91.9 us; the launch traced here: 91.3 us
  starting transfers between devices  43.9 us (48%)
  waiting for transfers between devices  22.5 us (24%)
  Pallas kernels  19.8 us (22%)
  other arithmetic  2.7 us (3%)
  local copies, waits for them, and re-layouts  1.95 us (2%)
    pallas_call x4, Pallas kernels, part(): pl.pallas_call(functools.partial(project, count), out_shape=[jax.ShapeDty...  10.6 us
    ppermute x3, waiting for transfers between devices, on_device(): near = lax.ppermute(send, axes, straight)  9.21 us
    ppermute x1, starting transfers between devices, on_device(): lax.ppermute(first, 'dp', [(i, i + 1) for i in range(dp_count - 1)])  8.92 us
    ppermute x2, starting transfers between devices, on_device(): far = lax.ppermute(send, axes, straight if distance > 2 else cross)  8.44 us
    ppermute x1, starting transfers between devices, on_device(): first = lax.ppermute(own, ('dp', 'core'), first_pairs)  7.62 us
    ppermute x1, waiting for transfers between devices, on_device(): first = lax.ppermute(own, ('dp', 'core'), first_pairs)  7.36 us
    ppermute x3, starting transfers between devices, on_device(): near = lax.ppermute(send, axes, straight)  6.64 us
    pallas_call x2, Pallas kernels, on_device(): pl.pallas_call(functools.partial(attend_piece, which), out_shape=[state_s...  4.91 us
  transfers between devices with their start and end apart: 12, of which 8 were waited for; matrix products, arithmetic and copies ran while one was open for 3% of the time, Pallas kernels for 19%

profile of v4, /device:TPU:31, one launch (start us, length us, event | category | flops | bytes accessed | tf_op | source)
XLA Modules:
  0.0 91.3 jit_solution(18327661254974619370)
XLA Ops:
  0.0 2.6 %collective-permute-start = (bf16[384,512]{1,0:T(8,128)(2,1)}, bf16[384,512]{1,0:T(8,128)(2,1)S(1)}, u32[]{:S(2)}, u32[]{:S(2)}) collective-permute-start(bf16[384,512]{1,0:T(8,128)(2,1)} %qm_ref.5), channel_id=1, source_target_pairs={{0,1},{1,0},{2,3},{3,2},{4,5},{5,4},{6,7},{7,6},{8,9},{9,8},{10,11... | collective-permute-start | bytes 1179656 | tf_op jit(solution)/shard_map/ppermute | solution.py:200
  3.6 7.6 %collective-permute-start.1 = (bf16[384,256]{1,0:T(8,128)(2,1)S(1)}, bf16[384,256]{1,0:T(8,128)(2,1)S(1)}, u32[]{:S(2)}, u32[]{:S(2)}) collective-permute-start(bf16[384,256]{1,0:T(8,128)(2,1)S(1)} %pad_maximum_fusion.own_ref), channel_id=1, source_target_pairs={{0,16},{16,32},{32,48},{48,64},{64,80},{80,96},{96,112},{112,128},... | collective-permute-start | bytes 589832 | tf_op jit(solution)/shard_map/ppermute | solution.py:199
  11.2 1.9 %collective-permute-start.4 = (bf16[512,8192]{1,0:T(8,128)(2,1)}, bf16[512,8192]{1,0:T(8,128)(2,1)}, u32[]{:S(2)}, u32[]{:S(2)}) collective-permute-start(bf16[512,8192]{1,0:T(8,128)(2,1)} %wm_ref.9), channel_id=1, source_target_pairs={{0,1},{1,0},{2,3},{3,2},{4,5},{5,4},{6,7},{7,6},{8,9},{9,8},{10,11... | collective-permute-start | bytes 25165832 | tf_op jit(solution)/shard_map/ppermute | solution.py:203
  14.3 7.4 %collective-permute-done.1.piece_ref = bf16[384,256]{1,0:T(8,128)(2,1)S(1)} collective-permute-done((bf16[384,256]{1,0:T(8,128)(2,1)S(1)}, bf16[384,256]{1,0:T(8,128)(2,1)S(1)}, u32[]{:S(2)}, u32[]{:S(2)}) %collective-permute-start.1) | collective-permute-done | bytes 196640 | tf_op jit(solution)/shard_map/ppermute | solution.py:199
  21.6 8.9 %collective-permute-start.2 = (bf16[384,256]{1,0:T(8,128)(2,1)S(1)}, bf16[384,256]{1,0:T(8,128)(2,1)S(1)}, u32[]{:S(2)}, u32[]{:S(2)}) collective-permute-start(bf16[384,256]{1,0:T(8,128)(2,1)S(1)} %collective-permute-done.1.piece_ref), channel_id=1, source_target_pairs={{0,16},{16,32},{32,48},{48,64},{64,80},{80,96},{96,112},{112,128},... | collective-permute-start | bytes 589832 | tf_op jit(solution)/shard_map/ppermute | solution.py:201
  31.5 2.1 %shard_map.55.state_ref = f32[1040,384]{1,0:T(8,128)S(1)} custom-call(s32[6]{0:T(128)S(1)} %pad_add_fusion.info_ref, bf16[384,512]{1,0:T(8,128)(2,1)S(1)} %copy-done, bf16[384,512]{1,0:T(8,128)(2,1)S(1)} %collective-permute-done.qo_ref, bf16[384,256]{1,0:T(8,128)(2,1)S(1)} %pad_maximum_fusion.own_ref), custom_call_target="tpu_custom_call" | custom-call | flops 60000002048 | bytes 4000000 | tf_op jit(solution)/shard_map/pallas_call | solution.py:214
  33.7 2.4 %shard_map.56.state_ref = f32[1040,384]{1,0:T(8,128)S(1)} custom-call(s32[6]{0:T(128)S(1)} %pad_add_fusion.info_ref, bf16[384,512]{1,0:T(8,128)(2,1)S(1)} %copy-done, bf16[384,512]{1,0:T(8,128)(2,1)S(1)} %collective-permute-done.qo_ref, bf16[384,256]{1,0:T(8,128)(2,1)S(1)} %collective-permute-done.1.piece_ref, f32[1040,384]{1,0:T(8,128)S(1)} %shard_map.55.state_ref), custom_call_target="tpu_custom_call" | custom-call | flops 60000002048 | bytes 6000000 | tf_op jit(solution)/shard_map/pallas_call | solution.py:224
  36.1 2.5 %shard_map.57 = (f32[1040,384]{1,0:T(8,128)S(1)}, bf16[1072,384]{1,0:T(8,128)(2,1)S(1)}) custom-call(s32[6]{0:T(128)S(1)} %pad_add_fusion.info_ref, bf16[384,512]{1,0:T(8,128)(2,1)S(1)} %copy-done, bf16[384,512]{1,0:T(8,128)(2,1)S(1)} %collective-permute-done.qo_ref, bf16[384,256]{1,0:T(8,128)(2,1)S(1)} %collective-permute-done.2.piece_ref, ...), custom_call_target="tpu_custom_call" | custom-call | flops 60000002048 | bytes 6000000 | tf_op jit(solution)/shard_map/pallas_call | solution.py:224
  38.6 3.7 %collective-permute-start.3 = (bf16[1072,384]{1,0:T(8,128)(2,1)S(1)}, bf16[1072,384]{1,0:T(8,128)(2,1)S(1)}, u32[]{:S(2)}, u32[]{:S(2)}) collective-permute-start(bf16[1072,384]{1,0:T(8,128)(2,1)S(1)} %get-tuple-element.22), channel_id=1, source_target_pairs={{0,1},{1,0},{2,3},{3,2},{4,5},{5,4},{6,7},{7,6},{8,9},{9,8},{10,11... | collective-permute-start | bytes 2469896 | tf_op jit(solution)/shard_map/ppermute | solution.py:233
  44.2 2.2 %shard_map.58 = (bf16[384,1024]{1,0:T(8,128)(2,1)S(1)}, bf16[384,512]{1,0:T(8,128)(2,1)S(1)}) custom-call(s32[1]{0:T(128)} %bitcast.1.columns_ref, f32[1040,384]{1,0:T(8,128)S(1)} %get-tuple-element.21.here_ref, bf16[1072,384]{1,0:T(8,128)(2,1)S(1)} %collective-permute-done.3.there_ref, bf16[512,8192]{1,0:T(8,128)(2,1)} %wm_ref.9, ...), custom_call_target="tpu_custom_call" | custom-call | flops 400000000 | bytes 5000000 | tf_op jit(solution)/shard_map/pallas_call | solution.py:244
  46.4 2.1 %collective-permute-start.5 = (bf16[384,512]{1,0:T(8,128)(2,1)S(1)}, bf16[384,512]{1,0:T(8,128)(2,1)S(1)}, u32[]{:S(2)}, u32[]{:S(2)}) collective-permute-start(bf16[384,512]{1,0:T(8,128)(2,1)S(1)} %get-tuple-element.29), channel_id=1, source_target_pairs={{0,2},{1,15},{2,4},{3,1},{4,6},{5,3},{6,8},{7,5},{8,10},{9,7},{10,... | collective-permute-start | bytes 1179656 | tf_op jit(solution)/shard_map/ppermute | solution.py:279
  48.5 2.9 %shard_map.62 = (bf16[384,512]{1,0:T(8,128)(2,1)S(1)}, bf16[384,512]{1,0:T(8,128)(2,1)S(1)}) custom-call(s32[2]{0:T(128)S(1)} %pad_add_fusion.3.columns_ref, bf16[384,1024]{1,0:T(8,128)(2,1)S(1)} %get-tuple-element.23.att_ref, bf16[512,8192]{1,0:T(8,128)(2,1)} %wm_ref.9, bf16[512,8192]{1,0:T(8,128)(2,1)} %collective-permute-done.4.wo_ref), custom_call_target="tpu_custom_call" | custom-call | flops 60000002048 | bytes 10000000 | tf_op jit(solution)/shard_map/pallas_call | solution.py:259
  51.4 2.1 %collective-permute-start.6 = (bf16[384,512]{1,0:T(8,128)(2,1)S(1)}, bf16[384,512]{1,0:T(8,128)(2,1)S(1)}, u32[]{:S(2)}, u32[]{:S(2)}) collective-permute-start(bf16[384,512]{1,0:T(8,128)(2,1)S(1)} %get-tuple-element.32), channel_id=1, source_target_pairs={{0,2},{1,15},{2,4},{3,1},{4,6},{5,3},{6,8},{7,5},{8,10},{9,7},{10,... | collective-permute-start | bytes 1179656 | tf_op jit(solution)/shard_map/ppermute | solution.py:281
  53.5 2.6 %collective-permute-done.5 = bf16[384,512]{1,0:T(8,128)(2,1)S(1)} collective-permute-done((bf16[384,512]{1,0:T(8,128)(2,1)S(1)}, bf16[384,512]{1,0:T(8,128)(2,1)S(1)}, u32[]{:S(2)}, u32[]{:S(2)}) %collective-permute-start.5) | collective-permute-done | bytes 393248 | tf_op jit(solution)/shard_map/ppermute | solution.py:279
  56.3 1.9 %collective-permute-start.7 = (bf16[384,512]{1,0:T(8,128)(2,1)S(1)}, bf16[384,512]{1,0:T(8,128)(2,1)S(1)}, u32[]{:S(2)}, u32[]{:S(2)}) collective-permute-start(bf16[384,512]{1,0:T(8,128)(2,1)S(1)} %add_convert_fusion.5), channel_id=1, source_target_pairs={{0,2},{1,15},{2,4},{3,1},{4,6},{5,3},{6,8},{7,5},{8,10},{9,7},{10,... | collective-permute-start | bytes 1179656 | tf_op jit(solution)/shard_map/ppermute | solution.py:284
  58.2 2.9 %shard_map.61 = (bf16[384,512]{1,0:T(8,128)(2,1)S(1)}, bf16[384,512]{1,0:T(8,128)(2,1)S(1)}) custom-call(s32[2]{0:T(128)S(1)} %pad_add_fusion.2.columns_ref, bf16[384,1024]{1,0:T(8,128)(2,1)S(1)} %get-tuple-element.23.att_ref, bf16[512,8192]{1,0:T(8,128)(2,1)} %wm_ref.9, bf16[512,8192]{1,0:T(8,128)(2,1)} %collective-permute-done.4.wo_ref), custom_call_target="tpu_custom_call" | custom-call | flops 60000002048 | bytes 10000000 | tf_op jit(solution)/shard_map/pallas_call | solution.py:259
  61.3 2.6 %collective-permute-start.8 = (bf16[384,512]{1,0:T(8,128)(2,1)S(1)}, bf16[384,512]{1,0:T(8,128)(2,1)S(1)}, u32[]{:S(2)}, u32[]{:S(2)}) collective-permute-start(bf16[384,512]{1,0:T(8,128)(2,1)S(1)} %add_convert_fusion.4), channel_id=1, source_target_pairs={{0,2},{1,15},{2,4},{3,1},{4,6},{5,3},{6,8},{7,5},{8,10},{9,7},{10,... | collective-permute-start | bytes 1179656 | tf_op jit(solution)/shard_map/ppermute | solution.py:289
  63.9 2.1 %collective-permute-done.7 = bf16[384,512]{1,0:T(8,128)(2,1)S(1)} collective-permute-done((bf16[384,512]{1,0:T(8,128)(2,1)S(1)}, bf16[384,512]{1,0:T(8,128)(2,1)S(1)}, u32[]{:S(2)}, u32[]{:S(2)}) %collective-permute-start.7) | collective-permute-done | bytes 393248 | tf_op jit(solution)/shard_map/ppermute | solution.py:284
  66.1 1.9 %collective-permute-start.9 = (bf16[384,512]{1,0:T(8,128)(2,1)S(1)}, bf16[384,512]{1,0:T(8,128)(2,1)S(1)}, u32[]{:S(2)}, u32[]{:S(2)}) collective-permute-start(bf16[384,512]{1,0:T(8,128)(2,1)S(1)} %add_convert_fusion.3), channel_id=1, source_target_pairs={{0,2},{1,15},{2,4},{3,1},{4,6},{5,3},{6,8},{7,5},{8,10},{9,7},{10,... | collective-permute-start | bytes 1179656 | tf_op jit(solution)/shard_map/ppermute | solution.py:284
  68.0 2.9 %shard_map.60 = (bf16[384,512]{1,0:T(8,128)(2,1)S(1)}, bf16[384,512]{1,0:T(8,128)(2,1)S(1)}) custom-call(s32[2]{0:T(128)S(1)} %pad_add_fusion.1.columns_ref, bf16[384,1024]{1,0:T(8,128)(2,1)S(1)} %get-tuple-element.23.att_ref, bf16[512,8192]{1,0:T(8,128)(2,1)} %wm_ref.9, bf16[512,8192]{1,0:T(8,128)(2,1)} %collective-permute-done.4.wo_ref), custom_call_target="tpu_custom_call" | custom-call | flops 60000002048 | bytes 10000000 | tf_op jit(solution)/shard_map/pallas_call | solution.py:259
  71.1 5.8 %collective-permute-start.11 = (bf16[384,512]{1,0:T(8,128)(2,1)S(1)}, bf16[384,512]{1,0:T(8,128)(2,1)S(1)}, u32[]{:S(2)}, u32[]{:S(2)}) collective-permute-start(bf16[384,512]{1,0:T(8,128)(2,1)S(1)} %add_convert_fusion.2), channel_id=1, source_target_pairs={{0,3},{1,14},{2,5},{3,0},{4,7},{5,2},{6,9},{7,4},{8,11},{9,6},{10,... | collective-permute-start | bytes 1179656 | tf_op jit(solution)/shard_map/ppermute | solution.py:289
  77.1 2.8 %collective-permute-start.10 = (bf16[384,512]{1,0:T(8,128)(2,1)S(1)}, bf16[384,512]{1,0:T(8,128)(2,1)S(1)}, u32[]{:S(2)}, u32[]{:S(2)}) collective-permute-start(bf16[384,512]{1,0:T(8,128)(2,1)S(1)} %add_convert_fusion.1), channel_id=1, source_target_pairs={{0,2},{1,15},{2,4},{3,1},{4,6},{5,3},{6,8},{7,5},{8,10},{9,7},{10,... | collective-permute-start | bytes 1179656 | tf_op jit(solution)/shard_map/ppermute | solution.py:284
  79.9 1.8 %shard_map.59 = bf16[384,512]{1,0:T(8,128)(2,1)S(1)} custom-call(s32[1]{0:T(128)} %bitcast.columns_ref, bf16[384,1024]{1,0:T(8,128)(2,1)S(1)} %get-tuple-element.23.att_ref, bf16[512,8192]{1,0:T(8,128)(2,1)} %wm_ref.9, bf16[512,8192]{1,0:T(8,128)(2,1)} %collective-permute-done.4.wo_ref), custom_call_target="tpu_custom_call" | custom-call | flops 60000002048 | bytes 10000000 | tf_op jit(solution)/shard_map/pallas_call | solution.py:259
  83.2 7.1 %collective-permute-done.10 = bf16[384,512]{1,0:T(8,128)(2,1)S(1)} collective-permute-done((bf16[384,512]{1,0:T(8,128)(2,1)S(1)}, bf16[384,512]{1,0:T(8,128)(2,1)S(1)}, u32[]{:S(2)}, u32[]{:S(2)}) %collective-permute-start.10) | collective-permute-done | bytes 393248 | tf_op jit(solution)/shard_map/ppermute | solution.py:284
  (26 shorter events, 8.0 us)
Async XLA Ops:
  0.0 30.5 %collective-permute-start = (bf16[384,512]{1,0:T(8,128)(2,1)}, bf16[384,512]{1,0:T(8,128)(2,1)S(1)}, u32[]{:S(2)}, u32[]{:S(2)}) collective-permute-start(bf16[384,512]{1,0:T(8,128)(2,1)} %qm_ref.5), channel_id=1, source_target_pairs={{0,1},{1,0},{2,3},{3,2},{4,5},{5,4},{6,7},{7,6},{8,9},{9,8},{10,11... | collective-permute-start | bytes 1179656 | tf_op jit(solution)/shard_map/ppermute | solution.py:200
  3.6 18.0 %collective-permute-start.1 = (bf16[384,256]{1,0:T(8,128)(2,1)S(1)}, bf16[384,256]{1,0:T(8,128)(2,1)S(1)}, u32[]{:S(2)}, u32[]{:S(2)}) collective-permute-start(bf16[384,256]{1,0:T(8,128)(2,1)S(1)} %pad_maximum_fusion.own_ref), channel_id=1, source_target_pairs={{0,16},{16,32},{32,48},{48,64},{64,80},{80,96},{96,112},{112,128},... | collective-permute-start | bytes 589832 | tf_op jit(solution)/shard_map/ppermute | solution.py:199
  11.2 33.0 %collective-permute-start.4 = (bf16[512,8192]{1,0:T(8,128)(2,1)}, bf16[512,8192]{1,0:T(8,128)(2,1)}, u32[]{:S(2)}, u32[]{:S(2)}) collective-permute-start(bf16[512,8192]{1,0:T(8,128)(2,1)} %wm_ref.9), channel_id=1, source_target_pairs={{0,1},{1,0},{2,3},{3,2},{4,5},{5,4},{6,7},{7,6},{8,9},{9,8},{10,11... | collective-permute-start | bytes 25165832 | tf_op jit(solution)/shard_map/ppermute | solution.py:203
  21.6 14.5 %collective-permute-start.2 = (bf16[384,256]{1,0:T(8,128)(2,1)S(1)}, bf16[384,256]{1,0:T(8,128)(2,1)S(1)}, u32[]{:S(2)}, u32[]{:S(2)}) collective-permute-start(bf16[384,256]{1,0:T(8,128)(2,1)S(1)} %collective-permute-done.1.piece_ref), channel_id=1, source_target_pairs={{0,16},{16,32},{32,48},{48,64},{64,80},{80,96},{96,112},{112,128},... | collective-permute-start | bytes 589832 | tf_op jit(solution)/shard_map/ppermute | solution.py:201
  30.5 1.0 %copy-start = (bf16[384,512]{1,0:T(8,128)(2,1)S(1)}, bf16[384,512]{1,0:T(8,128)(2,1)}, u32[]{:S(2)}) copy-start(bf16[384,512]{1,0:T(8,128)(2,1)} %qm_ref.5) | copy-start | bytes 1179652
  38.6 5.6 %collective-permute-start.3 = (bf16[1072,384]{1,0:T(8,128)(2,1)S(1)}, bf16[1072,384]{1,0:T(8,128)(2,1)S(1)}, u32[]{:S(2)}, u32[]{:S(2)}) collective-permute-start(bf16[1072,384]{1,0:T(8,128)(2,1)S(1)} %get-tuple-element.22), channel_id=1, source_target_pairs={{0,1},{1,0},{2,3},{3,2},{4,5},{5,4},{6,7},{7,6},{8,9},{9,8},{10,11... | collective-permute-start | bytes 2469896 | tf_op jit(solution)/shard_map/ppermute | solution.py:233
  46.4 9.7 %collective-permute-start.5 = (bf16[384,512]{1,0:T(8,128)(2,1)S(1)}, bf16[384,512]{1,0:T(8,128)(2,1)S(1)}, u32[]{:S(2)}, u32[]{:S(2)}) collective-permute-start(bf16[384,512]{1,0:T(8,128)(2,1)S(1)} %get-tuple-element.29), channel_id=1, source_target_pairs={{0,2},{1,15},{2,4},{3,1},{4,6},{5,3},{6,8},{7,5},{8,10},{9,7},{10,... | collective-permute-start | bytes 1179656 | tf_op jit(solution)/shard_map/ppermute | solution.py:279
  51.4 9.7 %collective-permute-start.6 = (bf16[384,512]{1,0:T(8,128)(2,1)S(1)}, bf16[384,512]{1,0:T(8,128)(2,1)S(1)}, u32[]{:S(2)}, u32[]{:S(2)}) collective-permute-start(bf16[384,512]{1,0:T(8,128)(2,1)S(1)} %get-tuple-element.32), channel_id=1, source_target_pairs={{0,2},{1,15},{2,4},{3,1},{4,6},{5,3},{6,8},{7,5},{8,10},{9,7},{10,... | collective-permute-start | bytes 1179656 | tf_op jit(solution)/shard_map/ppermute | solution.py:281
  56.3 9.7 %collective-permute-start.7 = (bf16[384,512]{1,0:T(8,128)(2,1)S(1)}, bf16[384,512]{1,0:T(8,128)(2,1)S(1)}, u32[]{:S(2)}, u32[]{:S(2)}) collective-permute-start(bf16[384,512]{1,0:T(8,128)(2,1)S(1)} %add_convert_fusion.5), channel_id=1, source_target_pairs={{0,2},{1,15},{2,4},{3,1},{4,6},{5,3},{6,8},{7,5},{8,10},{9,7},{10,... | collective-permute-start | bytes 1179656 | tf_op jit(solution)/shard_map/ppermute | solution.py:284
  61.3 9.7 %collective-permute-start.8 = (bf16[384,512]{1,0:T(8,128)(2,1)S(1)}, bf16[384,512]{1,0:T(8,128)(2,1)S(1)}, u32[]{:S(2)}, u32[]{:S(2)}) collective-permute-start(bf16[384,512]{1,0:T(8,128)(2,1)S(1)} %add_convert_fusion.4), channel_id=1, source_target_pairs={{0,2},{1,15},{2,4},{3,1},{4,6},{5,3},{6,8},{7,5},{8,10},{9,7},{10,... | collective-permute-start | bytes 1179656 | tf_op jit(solution)/shard_map/ppermute | solution.py:289
  66.1 10.9 %collective-permute-start.9 = (bf16[384,512]{1,0:T(8,128)(2,1)S(1)}, bf16[384,512]{1,0:T(8,128)(2,1)S(1)}, u32[]{:S(2)}, u32[]{:S(2)}) collective-permute-start(bf16[384,512]{1,0:T(8,128)(2,1)S(1)} %add_convert_fusion.3), channel_id=1, source_target_pairs={{0,2},{1,15},{2,4},{3,1},{4,6},{5,3},{6,8},{7,5},{8,10},{9,7},{10,... | collective-permute-start | bytes 1179656 | tf_op jit(solution)/shard_map/ppermute | solution.py:284
  71.1 12.1 %collective-permute-start.11 = (bf16[384,512]{1,0:T(8,128)(2,1)S(1)}, bf16[384,512]{1,0:T(8,128)(2,1)S(1)}, u32[]{:S(2)}, u32[]{:S(2)}) collective-permute-start(bf16[384,512]{1,0:T(8,128)(2,1)S(1)} %add_convert_fusion.2), channel_id=1, source_target_pairs={{0,3},{1,14},{2,5},{3,0},{4,7},{5,2},{6,9},{7,4},{8,11},{9,6},{10,... | collective-permute-start | bytes 1179656 | tf_op jit(solution)/shard_map/ppermute | solution.py:289
  77.1 13.3 %collective-permute-start.10 = (bf16[384,512]{1,0:T(8,128)(2,1)S(1)}, bf16[384,512]{1,0:T(8,128)(2,1)S(1)}, u32[]{:S(2)}, u32[]{:S(2)}) collective-permute-start(bf16[384,512]{1,0:T(8,128)(2,1)S(1)} %add_convert_fusion.1), channel_id=1, source_target_pairs={{0,2},{1,15},{2,4},{3,1},{4,6},{5,3},{6,8},{7,5},{8,10},{9,7},{10,... | collective-permute-start | bytes 1179656 | tf_op jit(solution)/shard_map/ppermute | solution.py:284

commit v5 on v4

--- a/solution.py
+++ b/solution.py
@@ -197,7 +197,8 @@
         (2 * i + c, 2 * (i + FIRST_BACK[c]) + c) for c in range(2) for i in range(dp_count - FIRST_BACK[c])
     ]
     first = lax.ppermute(own, ("dp", "core"), first_pairs)
-    q_other = lax.ppermute(queries, "core", swap)
+    own, q_sent = lax.optimization_barrier((own, queries))
+    q_other = lax.ppermute(q_sent, "core", swap)
     second = lax.ppermute(first, "dp", [(i, i + 1) for i in range(dp_count - 1)])
 
     w_other = lax.ppermute(out_weight, "core", swap)
@@ -279,17 +280,17 @@
     near = lax.ppermute(farthest, axes, straight)
     now = part(columns_at(half - 1))
     far = lax.ppermute(now[1], axes, straight)
+    rest = part(jnp.concatenate([*(columns_at(distance) for distance in range(half - 2, 0, -1)), columns_at(0)[:1]]))
     for distance in range(half - 1, 0, -1):
         send = add(now[0], near)
         near = lax.ppermute(send, axes, straight)
         if distance > 1:
-            now = part(columns_at(distance - 1))
-            now, send = lax.optimization_barrier((now, send))
+            rest, send = lax.optimization_barrier((rest, send))
+            now, rest = rest[:2], rest[2:]
             send = add(now[1], far)
             far = lax.ppermute(send, axes, straight if distance > 2 else cross)
             now, send = lax.optimization_barrier((now, send))
-    mine = part(columns_at(0)[:1])[0]
-    return add(mine, near, far)
+    return add(rest[0], near, far)
 
 
 def solution(mesh):

time: 91.9 us -> 90.1 us (0.980)
  the two profiles are of different devices: /device:TPU:31 before, /device:TPU:6 now
where the time goes in v5:
time: 90.1 us; the launch traced here: 89.6 us
  starting transfers between devices  36.5 us (41%)
  waiting for transfers between devices  31.1 us (35%)
  Pallas kernels  17.1 us (19%)
  other arithmetic  2.55 us (3%)
  local copies, waits for them, and re-layouts  2.03 us (2%)
    ppermute x1, waiting for transfers between devices, on_device(): first = lax.ppermute(own, ('dp', 'core'), first_pairs)  11.5 us
    ppermute x3, waiting for transfers between devices, on_device(): near = lax.ppermute(send, axes, straight)  9.4 us
    ppermute x3, starting transfers between devices, on_device(): near = lax.ppermute(send, axes, straight)  7.75 us
    pallas_call x2, Pallas kernels, part(): pl.pallas_call(functools.partial(project, count), out_shape=[jax.ShapeDty...  7.74 us
    ppermute x2, starting transfers between devices, on_device(): far = lax.ppermute(send, axes, straight if distance > 2 else cross)  6.62 us
    ppermute x1, starting transfers between devices, on_device(): q_other = lax.ppermute(q_sent, 'core', swap)  5.08 us
    pallas_call x2, Pallas kernels, on_device(): pl.pallas_call(functools.partial(attend_piece, which), out_shape=[state_s...  4.98 us
    ppermute x2, waiting for transfers between devices, on_device(): far = lax.ppermute(send, axes, straight if distance > 2 else cross)  4.86 us
  transfers between devices with their start and end apart: 12, of which 8 were waited for; matrix products, arithmetic and copies ran while one was open for 2% of the time, Pallas kernels for 17%

profile of v5, /device:TPU:6, one launch (start us, length us, event | category | flops | bytes accessed | tf_op | source)
XLA Modules:
  0.0 89.6 jit_solution(15591823731733728720)
XLA Ops:
  1.0 4.3 %collective-permute-start.1 = (bf16[384,256]{1,0:T(8,128)(2,1)S(1)}, bf16[384,256]{1,0:T(8,128)(2,1)S(1)}, u32[]{:S(2)}, u32[]{:S(2)}) collective-permute-start(bf16[384,256]{1,0:T(8,128)(2,1)S(1)} %pad_maximum_fusion.own_ref), channel_id=1, source_target_pairs={{0,16},{16,32},{32,48},{48,64},{64,80},{80,96},{96,112},{112,128},... | collective-permute-start | bytes 589832 | tf_op jit(solution)/shard_map/ppermute | solution.py:199
  5.3 5.1 %collective-permute-start = (bf16[384,512]{1,0:T(8,128)(2,1)}, bf16[384,512]{1,0:T(8,128)(2,1)S(1)}, u32[]{:S(2)}, u32[]{:S(2)}) collective-permute-start(bf16[384,512]{1,0:T(8,128)(2,1)} %qm_ref.5), channel_id=1, source_target_pairs={{0,1},{1,0},{2,3},{3,2},{4,5},{5,4},{6,7},{7,6},{8,9},{9,8},{10,11... | collective-permute-start | bytes 1179656 | tf_op jit(solution)/shard_map/ppermute | solution.py:201
  10.4 1.9 %collective-permute-start.4 = (bf16[512,8192]{1,0:T(8,128)(2,1)}, bf16[512,8192]{1,0:T(8,128)(2,1)}, u32[]{:S(2)}, u32[]{:S(2)}) collective-permute-start(bf16[512,8192]{1,0:T(8,128)(2,1)} %wm_ref.5), channel_id=1, source_target_pairs={{0,1},{1,0},{2,3},{3,2},{4,5},{5,4},{6,7},{7,6},{8,9},{9,8},{10,11... | collective-permute-start | bytes 25165832 | tf_op jit(solution)/shard_map/ppermute | solution.py:204
  13.4 11.5 %collective-permute-done.1.piece_ref = bf16[384,256]{1,0:T(8,128)(2,1)S(1)} collective-permute-done((bf16[384,256]{1,0:T(8,128)(2,1)S(1)}, bf16[384,256]{1,0:T(8,128)(2,1)S(1)}, u32[]{:S(2)}, u32[]{:S(2)}) %collective-permute-start.1) | collective-permute-done | bytes 196640 | tf_op jit(solution)/shard_map/ppermute | solution.py:199
  24.9 1.9 %collective-permute-start.2 = (bf16[384,256]{1,0:T(8,128)(2,1)S(1)}, bf16[384,256]{1,0:T(8,128)(2,1)S(1)}, u32[]{:S(2)}, u32[]{:S(2)}) collective-permute-start(bf16[384,256]{1,0:T(8,128)(2,1)S(1)} %collective-permute-done.1.piece_ref), channel_id=1, source_target_pairs={{0,16},{16,32},{32,48},{48,64},{64,80},{80,96},{96,112},{112,128},... | collective-permute-start | bytes 589832 | tf_op jit(solution)/shard_map/ppermute | solution.py:202
  27.9 2.2 %shard_map.55.state_ref = f32[1040,384]{1,0:T(8,128)S(1)} custom-call(s32[6]{0:T(128)S(1)} %pad_add_fusion.info_ref, bf16[384,512]{1,0:T(8,128)(2,1)S(1)} %copy-done, bf16[384,512]{1,0:T(8,128)(2,1)S(1)} %collective-permute-done.qo_ref, bf16[384,256]{1,0:T(8,128)(2,1)S(1)} %pad_maximum_fusion.own_ref), custom_call_target="tpu_custom_call" | custom-call | flops 60000002048 | bytes 4000000 | tf_op jit(solution)/shard_map/pallas_call | solution.py:215
  30.0 2.5 %shard_map.56.state_ref = f32[1040,384]{1,0:T(8,128)S(1)} custom-call(s32[6]{0:T(128)S(1)} %pad_add_fusion.info_ref, bf16[384,512]{1,0:T(8,128)(2,1)S(1)} %copy-done, bf16[384,512]{1,0:T(8,128)(2,1)S(1)} %collective-permute-done.qo_ref, bf16[384,256]{1,0:T(8,128)(2,1)S(1)} %collective-permute-done.1.piece_ref, f32[1040,384]{1,0:T(8,128)S(1)} %shard_map.55.state_ref), custom_call_target="tpu_custom_call" | custom-call | flops 60000002048 | bytes 6000000 | tf_op jit(solution)/shard_map/pallas_call | solution.py:225
  32.5 2.1 %collective-permute-done.2.piece_ref = bf16[384,256]{1,0:T(8,128)(2,1)S(1)} collective-permute-done((bf16[384,256]{1,0:T(8,128)(2,1)S(1)}, bf16[384,256]{1,0:T(8,128)(2,1)S(1)}, u32[]{:S(2)}, u32[]{:S(2)}) %collective-permute-start.2) | collective-permute-done | bytes 196640 | tf_op jit(solution)/shard_map/ppermute | solution.py:202
  34.6 2.5 %shard_map.57 = (f32[1040,384]{1,0:T(8,128)S(1)}, bf16[1072,384]{1,0:T(8,128)(2,1)S(1)}) custom-call(s32[6]{0:T(128)S(1)} %pad_add_fusion.info_ref, bf16[384,512]{1,0:T(8,128)(2,1)S(1)} %copy-done, bf16[384,512]{1,0:T(8,128)(2,1)S(1)} %collective-permute-done.qo_ref, bf16[384,256]{1,0:T(8,128)(2,1)S(1)} %collective-permute-done.2.piece_ref, ...), custom_call_target="tpu_custom_call" | custom-call | flops 60000002048 | bytes 6000000 | tf_op jit(solution)/shard_map/pallas_call | solution.py:225
  37.1 1.9 %collective-permute-start.3 = (bf16[1072,384]{1,0:T(8,128)(2,1)S(1)}, bf16[1072,384]{1,0:T(8,128)(2,1)S(1)}, u32[]{:S(2)}, u32[]{:S(2)}) collective-permute-start(bf16[1072,384]{1,0:T(8,128)(2,1)S(1)} %get-tuple-element.31), channel_id=1, source_target_pairs={{0,1},{1,0},{2,3},{3,2},{4,5},{5,4},{6,7},{7,6},{8,9},{9,8},{10,11... | collective-permute-start | bytes 2469896 | tf_op jit(solution)/shard_map/ppermute | solution.py:234
  39.3 2.0 %collective-permute-done.3.there_ref = bf16[1072,384]{1,0:T(8,128)(2,1)S(1)} collective-permute-done((bf16[1072,384]{1,0:T(8,128)(2,1)S(1)}, bf16[1072,384]{1,0:T(8,128)(2,1)S(1)}, u32[]{:S(2)}, u32[]{:S(2)}) %collective-permute-start.3) | collective-permute-done | bytes 823328 | tf_op jit(solution)/shard_map/ppermute | solution.py:234
  41.4 2.2 %shard_map.58 = (bf16[384,1024]{1,0:T(8,128)(2,1)S(1)}, bf16[384,512]{1,0:T(8,128)(2,1)S(1)}) custom-call(s32[1]{0:T(128)} %bitcast.5.columns_ref, f32[1040,384]{1,0:T(8,128)S(1)} %get-tuple-element.30.here_ref, bf16[1072,384]{1,0:T(8,128)(2,1)S(1)} %collective-permute-done.3.there_ref, bf16[512,8192]{1,0:T(8,128)(2,1)} %wm_ref.5, ...), custom_call_target="tpu_custom_call" | custom-call | flops 400000000 | bytes 5000000 | tf_op jit(solution)/shard_map/pallas_call | solution.py:245
  43.6 3.5 %collective-permute-start.5 = (bf16[384,512]{1,0:T(8,128)(2,1)S(1)}, bf16[384,512]{1,0:T(8,128)(2,1)S(1)}, u32[]{:S(2)}, u32[]{:S(2)}) collective-permute-start(bf16[384,512]{1,0:T(8,128)(2,1)S(1)} %get-tuple-element.39), channel_id=1, source_target_pairs={{0,2},{1,15},{2,4},{3,1},{4,6},{5,3},{6,8},{7,5},{8,10},{9,7},{10,... | collective-permute-start | bytes 1179656 | tf_op jit(solution)/shard_map/ppermute | solution.py:280
  47.1 3.0 %shard_map.60 = (bf16[384,512]{1,0:T(8,128)(2,1)S(1)}, bf16[384,512]{1,0:T(8,128)(2,1)S(1)}) custom-call(s32[2]{0:T(128)S(1)} %pad_add_fusion.1.columns_ref, bf16[384,1024]{1,0:T(8,128)(2,1)S(1)} %get-tuple-element.32.att_ref, bf16[512,8192]{1,0:T(8,128)(2,1)} %wm_ref.5, bf16[512,8192]{1,0:T(8,128)(2,1)} %collective-permute-done.4.wo_ref), custom_call_target="tpu_custom_call" | custom-call | flops 60000002048 | bytes 10000000 | tf_op jit(solution)/shard_map/pallas_call | solution.py:260
  50.0 3.5 %collective-permute-start.6 = (bf16[384,512]{1,0:T(8,128)(2,1)S(1)}, bf16[384,512]{1,0:T(8,128)(2,1)S(1)}, u32[]{:S(2)}, u32[]{:S(2)}) collective-permute-start(bf16[384,512]{1,0:T(8,128)(2,1)S(1)} %get-tuple-element.45), channel_id=1, source_target_pairs={{0,2},{1,15},{2,4},{3,1},{4,6},{5,3},{6,8},{7,5},{8,10},{9,7},{10,... | collective-permute-start | bytes 1179656 | tf_op jit(solution)/shard_map/ppermute | solution.py:282
  54.8 2.3 %collective-permute-start.7 = (bf16[384,512]{1,0:T(8,128)(2,1)S(1)}, bf16[384,512]{1,0:T(8,128)(2,1)S(1)}, u32[]{:S(2)}, u32[]{:S(2)}) collective-permute-start(bf16[384,512]{1,0:T(8,128)(2,1)S(1)} %add_convert_fusion.5), channel_id=1, source_target_pairs={{0,2},{1,15},{2,4},{3,1},{4,6},{5,3},{6,8},{7,5},{8,10},{9,7},{10,... | collective-permute-start | bytes 1179656 | tf_op jit(solution)/shard_map/ppermute | solution.py:286
  57.1 4.8 %shard_map.59 = (bf16[384,512]{1,0:T(8,128)(2,1)S(1)}, bf16[384,512]{1,0:T(8,128)(2,1)S(1)}, bf16[384,512]{1,0:T(8,128)(2,1)S(1)}, bf16[384,512]{1,0:T(8,128)(2,1)S(1)}, bf16[384,512]{1,0:T(8,128)(2,1)S(1)}) custom-call(s32[5]{0:T(128)S(1)} %concatenate.9.columns_ref, bf16[384,1024]{1,0:T(8,128)(2,1)S(1)} %get-tuple-element.32.att_ref, ...), custom_call_target="tpu_custom_call" | custom-call | flops 60000002048 | bytes 10000000 | tf_op jit(solution)/shard_map/pallas_call | solution.py:260
  62.0 4.7 %collective-permute-start.8 = (bf16[384,512]{1,0:T(8,128)(2,1)S(1)}, bf16[384,512]{1,0:T(8,128)(2,1)S(1)}, u32[]{:S(2)}, u32[]{:S(2)}) collective-permute-start(bf16[384,512]{1,0:T(8,128)(2,1)S(1)} %add_convert_fusion.4), channel_id=1, source_target_pairs={{0,2},{1,15},{2,4},{3,1},{4,6},{5,3},{6,8},{7,5},{8,10},{9,7},{10,... | collective-permute-start | bytes 1179656 | tf_op jit(solution)/shard_map/ppermute | solution.py:291
  66.8 2.6 %collective-permute-start.9 = (bf16[384,512]{1,0:T(8,128)(2,1)S(1)}, bf16[384,512]{1,0:T(8,128)(2,1)S(1)}, u32[]{:S(2)}, u32[]{:S(2)}) collective-permute-start(bf16[384,512]{1,0:T(8,128)(2,1)S(1)} %add_convert_fusion.3), channel_id=1, source_target_pairs={{0,2},{1,15},{2,4},{3,1},{4,6},{5,3},{6,8},{7,5},{8,10},{9,7},{10,... | collective-permute-start | bytes 1179656 | tf_op jit(solution)/shard_map/ppermute | solution.py:286
  69.4 3.5 %collective-permute-done.8 = bf16[384,512]{1,0:T(8,128)(2,1)S(1)} collective-permute-done((bf16[384,512]{1,0:T(8,128)(2,1)S(1)}, bf16[384,512]{1,0:T(8,128)(2,1)S(1)}, u32[]{:S(2)}, u32[]{:S(2)}) %collective-permute-start.8) | collective-permute-done | bytes 393248 | tf_op jit(solution)/shard_map/ppermute | solution.py:291
  73.0 1.9 %collective-permute-start.11 = (bf16[384,512]{1,0:T(8,128)(2,1)S(1)}, bf16[384,512]{1,0:T(8,128)(2,1)S(1)}, u32[]{:S(2)}, u32[]{:S(2)}) collective-permute-start(bf16[384,512]{1,0:T(8,128)(2,1)S(1)} %add_convert_fusion.2), channel_id=1, source_target_pairs={{0,3},{1,14},{2,5},{3,0},{4,7},{5,2},{6,9},{7,4},{8,11},{9,6},{10,... | collective-permute-start | bytes 1179656 | tf_op jit(solution)/shard_map/ppermute | solution.py:291
  74.9 2.8 %collective-permute-done.9 = bf16[384,512]{1,0:T(8,128)(2,1)S(1)} collective-permute-done((bf16[384,512]{1,0:T(8,128)(2,1)S(1)}, bf16[384,512]{1,0:T(8,128)(2,1)S(1)}, u32[]{:S(2)}, u32[]{:S(2)}) %collective-permute-start.9) | collective-permute-done | bytes 393248 | tf_op jit(solution)/shard_map/ppermute | solution.py:286
  77.8 2.9 %collective-permute-start.10 = (bf16[384,512]{1,0:T(8,128)(2,1)S(1)}, bf16[384,512]{1,0:T(8,128)(2,1)S(1)}, u32[]{:S(2)}, u32[]{:S(2)}) collective-permute-start(bf16[384,512]{1,0:T(8,128)(2,1)S(1)} %add_convert_fusion.1), channel_id=1, source_target_pairs={{0,2},{1,15},{2,4},{3,1},{4,6},{5,3},{6,8},{7,5},{8,10},{9,7},{10,... | collective-permute-start | bytes 1179656 | tf_op jit(solution)/shard_map/ppermute | solution.py:286
  82.1 6.6 %collective-permute-done.10 = bf16[384,512]{1,0:T(8,128)(2,1)S(1)} collective-permute-done((bf16[384,512]{1,0:T(8,128)(2,1)S(1)}, bf16[384,512]{1,0:T(8,128)(2,1)S(1)}, u32[]{:S(2)}, u32[]{:S(2)}) %collective-permute-start.10) | collective-permute-done | bytes 393248 | tf_op jit(solution)/shard_map/ppermute | solution.py:286
  (23 shorter events, 7.2 us)
Async XLA Ops:
  1.0 23.9 %collective-permute-start.1 = (bf16[384,256]{1,0:T(8,128)(2,1)S(1)}, bf16[384,256]{1,0:T(8,128)(2,1)S(1)}, u32[]{:S(2)}, u32[]{:S(2)}) collective-permute-start(bf16[384,256]{1,0:T(8,128)(2,1)S(1)} %pad_maximum_fusion.own_ref), channel_id=1, source_target_pairs={{0,16},{16,32},{32,48},{48,64},{64,80},{80,96},{96,112},{112,128},... | collective-permute-start | bytes 589832 | tf_op jit(solution)/shard_map/ppermute | solution.py:199
  5.3 21.6 %collective-permute-start = (bf16[384,512]{1,0:T(8,128)(2,1)}, bf16[384,512]{1,0:T(8,128)(2,1)S(1)}, u32[]{:S(2)}, u32[]{:S(2)}) collective-permute-start(bf16[384,512]{1,0:T(8,128)(2,1)} %qm_ref.5), channel_id=1, source_target_pairs={{0,1},{1,0},{2,3},{3,2},{4,5},{5,4},{6,7},{7,6},{8,9},{9,8},{10,11... | collective-permute-start | bytes 1179656 | tf_op jit(solution)/shard_map/ppermute | solution.py:201
  10.4 31.0 %collective-permute-start.4 = (bf16[512,8192]{1,0:T(8,128)(2,1)}, bf16[512,8192]{1,0:T(8,128)(2,1)}, u32[]{:S(2)}, u32[]{:S(2)}) collective-permute-start(bf16[512,8192]{1,0:T(8,128)(2,1)} %wm_ref.5), channel_id=1, source_target_pairs={{0,1},{1,0},{2,3},{3,2},{4,5},{5,4},{6,7},{7,6},{8,9},{9,8},{10,11... | collective-permute-start | bytes 25165832 | tf_op jit(solution)/shard_map/ppermute | solution.py:204
  24.9 9.7 %collective-permute-start.2 = (bf16[384,256]{1,0:T(8,128)(2,1)S(1)}, bf16[384,256]{1,0:T(8,128)(2,1)S(1)}, u32[]{:S(2)}, u32[]{:S(2)}) collective-permute-start(bf16[384,256]{1,0:T(8,128)(2,1)S(1)} %collective-permute-done.1.piece_ref), channel_id=1, source_target_pairs={{0,16},{16,32},{32,48},{48,64},{64,80},{80,96},{96,112},{112,128},... | collective-permute-start | bytes 589832 | tf_op jit(solution)/shard_map/ppermute | solution.py:202
  26.9 1.0 %copy-start = (bf16[384,512]{1,0:T(8,128)(2,1)S(1)}, bf16[384,512]{1,0:T(8,128)(2,1)}, u32[]{:S(2)}) copy-start(bf16[384,512]{1,0:T(8,128)(2,1)} %qm_ref.5) | copy-start | bytes 1179652
  37.1 4.2 %collective-permute-start.3 = (bf16[1072,384]{1,0:T(8,128)(2,1)S(1)}, bf16[1072,384]{1,0:T(8,128)(2,1)S(1)}, u32[]{:S(2)}, u32[]{:S(2)}) collective-permute-start(bf16[1072,384]{1,0:T(8,128)(2,1)S(1)} %get-tuple-element.31), channel_id=1, source_target_pairs={{0,1},{1,0},{2,3},{3,2},{4,5},{5,4},{6,7},{7,6},{8,9},{9,8},{10,11... | collective-permute-start | bytes 2469896 | tf_op jit(solution)/shard_map/ppermute | solution.py:234
  43.6 11.2 %collective-permute-start.5 = (bf16[384,512]{1,0:T(8,128)(2,1)S(1)}, bf16[384,512]{1,0:T(8,128)(2,1)S(1)}, u32[]{:S(2)}, u32[]{:S(2)}) collective-permute-start(bf16[384,512]{1,0:T(8,128)(2,1)S(1)} %get-tuple-element.39), channel_id=1, source_target_pairs={{0,2},{1,15},{2,4},{3,1},{4,6},{5,3},{6,8},{7,5},{8,10},{9,7},{10,... | collective-permute-start | bytes 1179656 | tf_op jit(solution)/shard_map/ppermute | solution.py:280
  50.0 11.9 %collective-permute-start.6 = (bf16[384,512]{1,0:T(8,128)(2,1)S(1)}, bf16[384,512]{1,0:T(8,128)(2,1)S(1)}, u32[]{:S(2)}, u32[]{:S(2)}) collective-permute-start(bf16[384,512]{1,0:T(8,128)(2,1)S(1)} %get-tuple-element.45), channel_id=1, source_target_pairs={{0,2},{1,15},{2,4},{3,1},{4,6},{5,3},{6,8},{7,5},{8,10},{9,7},{10,... | collective-permute-start | bytes 1179656 | tf_op jit(solution)/shard_map/ppermute | solution.py:282
  54.8 11.9 %collective-permute-start.7 = (bf16[384,512]{1,0:T(8,128)(2,1)S(1)}, bf16[384,512]{1,0:T(8,128)(2,1)S(1)}, u32[]{:S(2)}, u32[]{:S(2)}) collective-permute-start(bf16[384,512]{1,0:T(8,128)(2,1)S(1)} %add_convert_fusion.5), channel_id=1, source_target_pairs={{0,2},{1,15},{2,4},{3,1},{4,6},{5,3},{6,8},{7,5},{8,10},{9,7},{10,... | collective-permute-start | bytes 1179656 | tf_op jit(solution)/shard_map/ppermute | solution.py:286
  62.0 10.9 %collective-permute-start.8 = (bf16[384,512]{1,0:T(8,128)(2,1)S(1)}, bf16[384,512]{1,0:T(8,128)(2,1)S(1)}, u32[]{:S(2)}, u32[]{:S(2)}) collective-permute-start(bf16[384,512]{1,0:T(8,128)(2,1)S(1)} %add_convert_fusion.4), channel_id=1, source_target_pairs={{0,2},{1,15},{2,4},{3,1},{4,6},{5,3},{6,8},{7,5},{8,10},{9,7},{10,... | collective-permute-start | bytes 1179656 | tf_op jit(solution)/shard_map/ppermute | solution.py:291
  66.8 10.9 %collective-permute-start.9 = (bf16[384,512]{1,0:T(8,128)(2,1)S(1)}, bf16[384,512]{1,0:T(8,128)(2,1)S(1)}, u32[]{:S(2)}, u32[]{:S(2)}) collective-permute-start(bf16[384,512]{1,0:T(8,128)(2,1)S(1)} %add_convert_fusion.3), channel_id=1, source_target_pairs={{0,2},{1,15},{2,4},{3,1},{4,6},{5,3},{6,8},{7,5},{8,10},{9,7},{10,... | collective-permute-start | bytes 1179656 | tf_op jit(solution)/shard_map/ppermute | solution.py:286
  73.0 9.1 %collective-permute-start.11 = (bf16[384,512]{1,0:T(8,128)(2,1)S(1)}, bf16[384,512]{1,0:T(8,128)(2,1)S(1)}, u32[]{:S(2)}, u32[]{:S(2)}) collective-permute-start(bf16[384,512]{1,0:T(8,128)(2,1)S(1)} %add_convert_fusion.2), channel_id=1, source_target_pairs={{0,3},{1,14},{2,5},{3,0},{4,7},{5,2},{6,9},{7,4},{8,11},{9,6},{10,... | collective-permute-start | bytes 1179656 | tf_op jit(solution)/shard_map/ppermute | solution.py:291
  77.8 10.9 %collective-permute-start.10 = (bf16[384,512]{1,0:T(8,128)(2,1)S(1)}, bf16[384,512]{1,0:T(8,128)(2,1)S(1)}, u32[]{:S(2)}, u32[]{:S(2)}) collective-permute-start(bf16[384,512]{1,0:T(8,128)(2,1)S(1)} %add_convert_fusion.1), channel_id=1, source_target_pairs={{0,2},{1,15},{2,4},{3,1},{4,6},{5,3},{6,8},{7,5},{8,10},{9,7},{10,... | collective-permute-start | bytes 1179656 | tf_op jit(solution)/shard_map/ppermute | solution.py:286

commit v6 on v5

--- a/solution.py
+++ b/solution.py
@@ -143,10 +143,11 @@
     return jnp.dot(att_ref[...], w_buf[block], preferred_element_type=jnp.float32).astype(jnp.bfloat16)
 
 
-def combine(columns_ref, here_ref, there_ref, wm_ref, wo_ref, att_ref, out_ref, w_buf, sems):
+def combine(columns_ref, here_ref, there_ref, wm_ref, wo_ref, att_ref, *rest):
     heads = 8
-    copies = fetch(columns_ref, 0, (wm_ref, wo_ref), w_buf, sems)
-    for copy in copies:
+    out_refs, (w_buf, sems) = rest[:-2], rest[-2:]
+    copies = [fetch(columns_ref, block, (wm_ref, wo_ref), w_buf, sems) for block in range(len(out_refs))]
+    for copy in sum(copies, []):
         copy.start()
     here = here_ref[STATS:, :]
     there = sum(there_ref[pl.ds(STATS + 16 * term, 16), :].astype(jnp.float32) for term in (2, 1, 0))
@@ -160,9 +161,10 @@
         accum = here_ref[pl.ds(head * HD, HD), :] * share_a
         accum += there_ref[pl.ds(other * HD, HD), :].astype(jnp.float32) * share_b
         att_ref[:, head * HD : (head + 1) * HD] = jnp.transpose(accum / total).astype(jnp.bfloat16)
-    for copy in copies:
-        copy.wait()
-    out_ref[...] = product(att_ref, w_buf, 0)
+    for block, out_ref in enumerate(out_refs):
+        for copy in copies[block]:
+            copy.wait()
+        out_ref[...] = product(att_ref, w_buf, block)
 
 
 def project(count, columns_ref, att_ref, wm_ref, wo_ref, *rest):
@@ -242,18 +244,18 @@
     def w_scratch(count):
         return [pltpu.VMEM((count, 2 * wide, wide), jnp.bfloat16), pltpu.SemaphoreType.DMA((count, 2))]
 
-    attended, farthest = pl.pallas_call(
+    attended, farthest, near, far = pl.pallas_call(
         combine,
         out_shape=[
             jax.ShapeDtypeStruct((rows, 2 * wide), jnp.bfloat16),
-            jax.ShapeDtypeStruct((rows, wide), jnp.bfloat16),
+            *[jax.ShapeDtypeStruct((rows, wide), jnp.bfloat16)] * 3,
         ],
         in_specs=[SM, VM, VM, HBM, HBM],
-        out_specs=[VM, VM],
-        scratch_shapes=w_scratch(1),
+        out_specs=[VM] * 4,
+        scratch_shapes=w_scratch(3),
         compiler_params=WIDE_LIMIT,
         cost_estimate=pl.CostEstimate(flops=400_000_000, bytes_accessed=5_000_000, transcendentals=10_000),
-    )(columns_at(half)[:1], state, there, out_weight, w_other)
+    )(jnp.concatenate([columns_at(half)[:1], columns_at(half - 1)]), state, there, out_weight, w_other)
 
     def part(columns):
         count = columns.shape[0]
@@ -267,8 +269,14 @@
             cost_estimate=pl.CostEstimate(flops=PROJECT_FLOPS, bytes_accessed=10_000_000, transcendentals=0),
         )(columns, attended, out_weight, w_other)
 
-    straight = [(2 * i + c, 2 * ((i + 1 - 2 * c) % y_count) + c) for i in range(y_count) for c in range(2)]
-    cross = [(2 * i + c, 2 * ((i + 1 - 2 * c) % y_count) + 1 - c) for i in range(y_count) for c in range(2)]
+    def carried(hops, crossing):
+        return [
+            (2 * i + c, 2 * ((i + (1 - 2 * c) * hops) % y_count) + (1 - c if crossing else c))
+            for i in range(y_count)
+            for c in range(2)
+        ]
+
+    straight = carried(1, False)
     axes = ("y", "core")
 
     def add(a, *others):
@@ -277,19 +285,18 @@
             total = total + b.astype(jnp.float32)
         return total.astype(jnp.bfloat16)
 
-    near = lax.ppermute(farthest, axes, straight)
-    now = part(columns_at(half - 1))
-    far = lax.ppermute(now[1], axes, straight)
+    joining = [lax.ppermute(farthest, axes, carried(2, False))]
+    near = lax.ppermute(near, axes, straight)
+    far = lax.ppermute(far, axes, straight)
     rest = part(jnp.concatenate([*(columns_at(distance) for distance in range(half - 2, 0, -1)), columns_at(0)[:1]]))
-    for distance in range(half - 1, 0, -1):
-        send = add(now[0], near)
+    for distance in range(half - 2, 0, -1):
+        send = add(rest[0], near, *joining)
+        joining = []
         near = lax.ppermute(send, axes, straight)
-        if distance > 1:
-            rest, send = lax.optimization_barrier((rest, send))
-            now, rest = rest[:2], rest[2:]
-            send = add(now[1], far)
-            far = lax.ppermute(send, axes, straight if distance > 2 else cross)
-            now, send = lax.optimization_barrier((now, send))
+        rest, send = lax.optimization_barrier((rest, send))
+        send = add(rest[1], far)
+        far = lax.ppermute(send, axes, straight if distance > 1 else carried(1, True))
+        rest, send = lax.optimization_barrier((rest[2:], send))
     return add(rest[0], near, far)
 
 

time: 90.1 us -> 92 us (1.021)
  the two profiles are of different devices: /device:TPU:6 before, /device:TPU:7 now
where the time goes in v6:
time: 92 us; the launch traced here: 91.5 us
  starting transfers between devices  52.7 us (57%)
  waiting for transfers between devices  18.3 us (20%)
  Pallas kernels  15.7 us (17%)
  other arithmetic  2.51 us (3%)
  local copies, waits for them, and re-layouts  2.03 us (2%)
    ppermute x2, starting transfers between devices, on_device(): lax.ppermute(send, axes, straight if distance > 1 else carried(1, True))  10.4 us
    ppermute x1, starting transfers between devices, on_device(): lax.ppermute(first, 'dp', [(i, i + 1) for i in range(dp_count - 1)])  8.54 us
    ppermute x1, starting transfers between devices, on_device(): first = lax.ppermute(own, ('dp', 'core'), first_pairs)  7.62 us
    ppermute x2, waiting for transfers between devices, on_device(): lax.ppermute(send, axes, straight if distance > 1 else carried(1, True))  7.13 us
    ppermute x2, starting transfers between devices, on_device(): near = lax.ppermute(send, axes, straight)  5.79 us
    ppermute x1, starting transfers between devices, on_device(): near = lax.ppermute(near, axes, straight)  5.1 us
    pallas_call x2, Pallas kernels, on_device(): pl.pallas_call(functools.partial(attend_piece, which), out_shape=[state_s...  4.88 us
    ppermute x1, waiting for transfers between devices, on_device(): first = lax.ppermute(own, ('dp', 'core'), first_pairs)  4.72 us
  transfers between devices with their start and end apart: 12, of which 7 were waited for; matrix products, arithmetic and copies ran while one was open for 2% of the time, Pallas kernels for 13%

profile of v6, /device:TPU:7, one launch (start us, length us, event | category | flops | bytes accessed | tf_op | source)
XLA Modules:
  0.0 91.5 jit_solution(5874324349642682719)
XLA Ops:
  0.0 1.0 %constant_dynamic-slice_fusion = (bf16[384,128]{1,0:T(8,128)(2,1)S(1)}, bf16[384,128]{1,0:T(8,128)(2,1)S(1)}) fusion(bf16[384,1024]{1,0:T(8,128)(2,1)} %param.8, s32[]{:T(128)S(6)} %select_n.48, bf16[384,1024]{1,0:T(8,128)(2,1)} %param.7), kind=kLoop, calls=%fused_computation.17 | loop fusion | bytes 393220 | tf_op jit(solution)/shard_map/dynamic_slice | solution.py:196
  1.0 7.6 %collective-permute-start.1 = (bf16[384,256]{1,0:T(8,128)(2,1)S(1)}, bf16[384,256]{1,0:T(8,128)(2,1)S(1)}, u32[]{:S(2)}, u32[]{:S(2)}) collective-permute-start(bf16[384,256]{1,0:T(8,128)(2,1)S(1)} %pad_maximum_fusion.own_ref), channel_id=1, source_target_pairs={{0,16},{16,32},{32,48},{48,64},{64,80},{80,96},{96,112},{112,128},... | collective-permute-start | bytes 589832 | tf_op jit(solution)/shard_map/ppermute | solution.py:201
  8.6 1.9 %collective-permute-start = (bf16[384,512]{1,0:T(8,128)(2,1)}, bf16[384,512]{1,0:T(8,128)(2,1)S(1)}, u32[]{:S(2)}, u32[]{:S(2)}) collective-permute-start(bf16[384,512]{1,0:T(8,128)(2,1)} %qm_ref.5), channel_id=1, source_target_pairs={{0,1},{1,0},{2,3},{3,2},{4,5},{5,4},{6,7},{7,6},{8,9},{9,8},{10,11... | collective-permute-start | bytes 1179656 | tf_op jit(solution)/shard_map/ppermute | solution.py:203
  10.5 2.4 %collective-permute-start.4 = (bf16[512,8192]{1,0:T(8,128)(2,1)}, bf16[512,8192]{1,0:T(8,128)(2,1)}, u32[]{:S(2)}, u32[]{:S(2)}) collective-permute-start(bf16[512,8192]{1,0:T(8,128)(2,1)} %wm_ref.3), channel_id=1, source_target_pairs={{0,1},{1,0},{2,3},{3,2},{4,5},{5,4},{6,7},{7,6},{8,9},{9,8},{10,11... | collective-permute-start | bytes 25165832 | tf_op jit(solution)/shard_map/ppermute | solution.py:206
  14.1 4.7 %collective-permute-done.1.piece_ref = bf16[384,256]{1,0:T(8,128)(2,1)S(1)} collective-permute-done((bf16[384,256]{1,0:T(8,128)(2,1)S(1)}, bf16[384,256]{1,0:T(8,128)(2,1)S(1)}, u32[]{:S(2)}, u32[]{:S(2)}) %collective-permute-start.1) | collective-permute-done | bytes 196640 | tf_op jit(solution)/shard_map/ppermute | solution.py:201
  18.8 8.5 %collective-permute-start.2 = (bf16[384,256]{1,0:T(8,128)(2,1)S(1)}, bf16[384,256]{1,0:T(8,128)(2,1)S(1)}, u32[]{:S(2)}, u32[]{:S(2)}) collective-permute-start(bf16[384,256]{1,0:T(8,128)(2,1)S(1)} %collective-permute-done.1.piece_ref), channel_id=1, source_target_pairs={{0,16},{16,32},{32,48},{48,64},{64,80},{80,96},{96,112},{112,128},... | collective-permute-start | bytes 589832 | tf_op jit(solution)/shard_map/ppermute | solution.py:204
  27.4 1.0 %copy-done = bf16[384,512]{1,0:T(8,128)(2,1)S(1)} copy-done((bf16[384,512]{1,0:T(8,128)(2,1)S(1)}, bf16[384,512]{1,0:T(8,128)(2,1)}, u32[]{:S(2)}) %copy-start) | copy-done | bytes 393240
  28.4 2.2 %shard_map.55.state_ref = f32[1040,384]{1,0:T(8,128)S(1)} custom-call(s32[6]{0:T(128)S(1)} %pad_add_fusion.1.info_ref, bf16[384,512]{1,0:T(8,128)(2,1)S(1)} %copy-done, bf16[384,512]{1,0:T(8,128)(2,1)S(1)} %collective-permute-done.qo_ref, bf16[384,256]{1,0:T(8,128)(2,1)S(1)} %pad_maximum_fusion.own_ref), custom_call_target="tpu_custom_call" | custom-call | flops 60000002048 | bytes 4000000 | tf_op jit(solution)/shard_map/pallas_call | solution.py:217
  30.5 2.4 %shard_map.56.state_ref = f32[1040,384]{1,0:T(8,128)S(1)} custom-call(s32[6]{0:T(128)S(1)} %pad_add_fusion.1.info_ref, bf16[384,512]{1,0:T(8,128)(2,1)S(1)} %copy-done, bf16[384,512]{1,0:T(8,128)(2,1)S(1)} %collective-permute-done.qo_ref, bf16[384,256]{1,0:T(8,128)(2,1)S(1)} %collective-permute-done.1.piece_ref, f32[1040,384]{1,0:T(8,128)S(1)} %shard_map.55.state_ref), custom_call_target="tpu_custom_call" | custom-call | flops 60000002048 | bytes 6000000 | tf_op jit(solution)/shard_map/pallas_call | solution.py:227
  33.0 2.4 %shard_map.57 = (f32[1040,384]{1,0:T(8,128)S(1)}, bf16[1072,384]{1,0:T(8,128)(2,1)S(1)}) custom-call(s32[6]{0:T(128)S(1)} %pad_add_fusion.1.info_ref, bf16[384,512]{1,0:T(8,128)(2,1)S(1)} %copy-done, bf16[384,512]{1,0:T(8,128)(2,1)S(1)} %collective-permute-done.qo_ref, bf16[384,256]{1,0:T(8,128)(2,1)S(1)} %collective-permute-done.2.piece_ref, ...), custom_call_target="tpu_custom_call" | custom-call | flops 60000002048 | bytes 6000000 | tf_op jit(solution)/shard_map/pallas_call | solution.py:227
  35.4 4.2 %collective-permute-start.3 = (bf16[1072,384]{1,0:T(8,128)(2,1)S(1)}, bf16[1072,384]{1,0:T(8,128)(2,1)S(1)}, u32[]{:S(2)}, u32[]{:S(2)}) collective-permute-start(bf16[1072,384]{1,0:T(8,128)(2,1)S(1)} %get-tuple-element.31), channel_id=1, source_target_pairs={{0,1},{1,0},{2,3},{3,2},{4,5},{5,4},{6,7},{7,6},{8,9},{9,8},{10,11... | collective-permute-start | bytes 2469896 | tf_op jit(solution)/shard_map/ppermute | solution.py:236
  39.9 1.7 %collective-permute-done.3.there_ref = bf16[1072,384]{1,0:T(8,128)(2,1)S(1)} collective-permute-done((bf16[1072,384]{1,0:T(8,128)(2,1)S(1)}, bf16[1072,384]{1,0:T(8,128)(2,1)S(1)}, u32[]{:S(2)}, u32[]{:S(2)}) %collective-permute-start.3) | collective-permute-done | bytes 823328 | tf_op jit(solution)/shard_map/ppermute | solution.py:236
  41.6 3.9 %shard_map.58 = (bf16[384,1024]{1,0:T(8,128)(2,1)S(1)}, bf16[384,512]{1,0:T(8,128)(2,1)S(1)}, bf16[384,512]{1,0:T(8,128)(2,1)S(1)}, bf16[384,512]{1,0:T(8,128)(2,1)S(1)}) custom-call(s32[3]{0:T(128)S(1)} %pad_add_fusion.columns_ref, f32[1040,384]{1,0:T(8,128)S(1)} %get-tuple-element.30.here_ref, bf16[1072,384]{1,0:T(8,128)(2,1)S(1)} %collective-permute-done.3.there_ref, ...), custom_call_target="tpu_custom_call" | custom-call | flops 400000000 | bytes 5000000 | tf_op jit(solution)/shard_map/pallas_call | solution.py:247
  45.5 5.1 %collective-permute-start.5 = (bf16[384,512]{1,0:T(8,128)(2,1)S(1)}, bf16[384,512]{1,0:T(8,128)(2,1)S(1)}, u32[]{:S(2)}, u32[]{:S(2)}) collective-permute-start(bf16[384,512]{1,0:T(8,128)(2,1)S(1)} %get-tuple-element.38), channel_id=1, source_target_pairs={{0,2},{1,15},{2,4},{3,1},{4,6},{5,3},{6,8},{7,5},{8,10},{9,7},{10,... | collective-permute-start | bytes 1179656 | tf_op jit(solution)/shard_map/ppermute | solution.py:289
  50.6 3.8 %collective-permute-start.6 = (bf16[384,512]{1,0:T(8,128)(2,1)S(1)}, bf16[384,512]{1,0:T(8,128)(2,1)S(1)}, u32[]{:S(2)}, u32[]{:S(2)}) collective-permute-start(bf16[384,512]{1,0:T(8,128)(2,1)S(1)} %get-tuple-element.39), channel_id=1, source_target_pairs={{0,4},{1,13},{2,6},{3,15},{4,8},{5,1},{6,10},{7,3},{8,12},{9,5},{1... | collective-permute-start | bytes 1179656 | tf_op jit(solution)/shard_map/ppermute | solution.py:288
  54.4 3.0 %collective-permute-start.7 = (bf16[384,512]{1,0:T(8,128)(2,1)S(1)}, bf16[384,512]{1,0:T(8,128)(2,1)S(1)}, u32[]{:S(2)}, u32[]{:S(2)}) collective-permute-start(bf16[384,512]{1,0:T(8,128)(2,1)S(1)} %get-tuple-element.44), channel_id=1, source_target_pairs={{0,2},{1,15},{2,4},{3,1},{4,6},{5,3},{6,8},{7,5},{8,10},{9,7},{10,... | collective-permute-start | bytes 1179656 | tf_op jit(solution)/shard_map/ppermute | solution.py:290
  57.4 4.7 %shard_map.59 = (bf16[384,512]{1,0:T(8,128)(2,1)S(1)}, bf16[384,512]{1,0:T(8,128)(2,1)S(1)}, bf16[384,512]{1,0:T(8,128)(2,1)S(1)}, bf16[384,512]{1,0:T(8,128)(2,1)S(1)}, bf16[384,512]{1,0:T(8,128)(2,1)S(1)}) custom-call(s32[5]{0:T(128)S(1)} %concatenate.12.columns_ref, bf16[384,1024]{1,0:T(8,128)(2,1)S(1)} %get-tuple-element.32.att_ref, ...), custom_call_target="tpu_custom_call" | custom-call | flops 60000002048 | bytes 10000000 | tf_op jit(solution)/shard_map/pallas_call | solution.py:262
  62.1 2.3 %collective-permute-done.6 = bf16[384,512]{1,0:T(8,128)(2,1)S(1)} collective-permute-done((bf16[384,512]{1,0:T(8,128)(2,1)S(1)}, bf16[384,512]{1,0:T(8,128)(2,1)S(1)}, u32[]{:S(2)}, u32[]{:S(2)}) %collective-permute-start.6) | collective-permute-done | bytes 393248 | tf_op jit(solution)/shard_map/ppermute | solution.py:288
  64.5 1.9 %collective-permute-start.8 = (bf16[384,512]{1,0:T(8,128)(2,1)S(1)}, bf16[384,512]{1,0:T(8,128)(2,1)S(1)}, u32[]{:S(2)}, u32[]{:S(2)}) collective-permute-start(bf16[384,512]{1,0:T(8,128)(2,1)S(1)} %add_convert_fusion.4), channel_id=1, source_target_pairs={{0,2},{1,15},{2,4},{3,1},{4,6},{5,3},{6,8},{7,5},{8,10},{9,7},{10,... | collective-permute-start | bytes 1179656 | tf_op jit(solution)/shard_map/ppermute | solution.py:295
  66.5 2.2 %collective-permute-done.7 = bf16[384,512]{1,0:T(8,128)(2,1)S(1)} collective-permute-done((bf16[384,512]{1,0:T(8,128)(2,1)S(1)}, bf16[384,512]{1,0:T(8,128)(2,1)S(1)}, u32[]{:S(2)}, u32[]{:S(2)}) %collective-permute-start.7) | collective-permute-done | bytes 393248 | tf_op jit(solution)/shard_map/ppermute | solution.py:290
  68.8 4.3 %collective-permute-start.9 = (bf16[384,512]{1,0:T(8,128)(2,1)S(1)}, bf16[384,512]{1,0:T(8,128)(2,1)S(1)}, u32[]{:S(2)}, u32[]{:S(2)}) collective-permute-start(bf16[384,512]{1,0:T(8,128)(2,1)S(1)} %add_convert_fusion.3), channel_id=1, source_target_pairs={{0,2},{1,15},{2,4},{3,1},{4,6},{5,3},{6,8},{7,5},{8,10},{9,7},{10,... | collective-permute-start | bytes 1179656 | tf_op jit(solution)/shard_map/ppermute | solution.py:298
  73.4 3.9 %collective-permute-start.10 = (bf16[384,512]{1,0:T(8,128)(2,1)S(1)}, bf16[384,512]{1,0:T(8,128)(2,1)S(1)}, u32[]{:S(2)}, u32[]{:S(2)}) collective-permute-start(bf16[384,512]{1,0:T(8,128)(2,1)S(1)} %add_convert_fusion.2), channel_id=1, source_target_pairs={{0,2},{1,15},{2,4},{3,1},{4,6},{5,3},{6,8},{7,5},{8,10},{9,7},{10,... | collective-permute-start | bytes 1179656 | tf_op jit(solution)/shard_map/ppermute | solution.py:295
  77.9 6.0 %collective-permute-start.11 = (bf16[384,512]{1,0:T(8,128)(2,1)S(1)}, bf16[384,512]{1,0:T(8,128)(2,1)S(1)}, u32[]{:S(2)}, u32[]{:S(2)}) collective-permute-start(bf16[384,512]{1,0:T(8,128)(2,1)S(1)} %add_convert_fusion.1), channel_id=1, source_target_pairs={{0,3},{1,14},{2,5},{3,0},{4,7},{5,2},{6,9},{7,4},{8,11},{9,6},{10,... | collective-permute-start | bytes 1179656 | tf_op jit(solution)/shard_map/ppermute | solution.py:298
  84.0 6.6 %collective-permute-done.11 = bf16[384,512]{1,0:T(8,128)(2,1)S(1)} collective-permute-done((bf16[384,512]{1,0:T(8,128)(2,1)S(1)}, bf16[384,512]{1,0:T(8,128)(2,1)S(1)}, u32[]{:S(2)}, u32[]{:S(2)}) %collective-permute-start.11) | collective-permute-done | bytes 393248 | tf_op jit(solution)/shard_map/ppermute | solution.py:298
  (21 shorter events, 3.3 us)
Async XLA Ops:
  1.0 17.8 %collective-permute-start.1 = (bf16[384,256]{1,0:T(8,128)(2,1)S(1)}, bf16[384,256]{1,0:T(8,128)(2,1)S(1)}, u32[]{:S(2)}, u32[]{:S(2)}) collective-permute-start(bf16[384,256]{1,0:T(8,128)(2,1)S(1)} %pad_maximum_fusion.own_ref), channel_id=1, source_target_pairs={{0,16},{16,32},{32,48},{48,64},{64,80},{80,96},{96,112},{112,128},... | collective-permute-start | bytes 589832 | tf_op jit(solution)/shard_map/ppermute | solution.py:201
  8.6 18.7 %collective-permute-start = (bf16[384,512]{1,0:T(8,128)(2,1)}, bf16[384,512]{1,0:T(8,128)(2,1)S(1)}, u32[]{:S(2)}, u32[]{:S(2)}) collective-permute-start(bf16[384,512]{1,0:T(8,128)(2,1)} %qm_ref.5), channel_id=1, source_target_pairs={{0,1},{1,0},{2,3},{3,2},{4,5},{5,4},{6,7},{7,6},{8,9},{9,8},{10,11... | collective-permute-start | bytes 1179656 | tf_op jit(solution)/shard_map/ppermute | solution.py:203
  10.5 31.0 %collective-permute-start.4 = (bf16[512,8192]{1,0:T(8,128)(2,1)}, bf16[512,8192]{1,0:T(8,128)(2,1)}, u32[]{:S(2)}, u32[]{:S(2)}) collective-permute-start(bf16[512,8192]{1,0:T(8,128)(2,1)} %wm_ref.3), channel_id=1, source_target_pairs={{0,1},{1,0},{2,3},{3,2},{4,5},{5,4},{6,7},{7,6},{8,9},{9,8},{10,11... | collective-permute-start | bytes 25165832 | tf_op jit(solution)/shard_map/ppermute | solution.py:206
  18.8 14.2 %collective-permute-start.2 = (bf16[384,256]{1,0:T(8,128)(2,1)S(1)}, bf16[384,256]{1,0:T(8,128)(2,1)S(1)}, u32[]{:S(2)}, u32[]{:S(2)}) collective-permute-start(bf16[384,256]{1,0:T(8,128)(2,1)S(1)} %collective-permute-done.1.piece_ref), channel_id=1, source_target_pairs={{0,16},{16,32},{32,48},{48,64},{64,80},{80,96},{96,112},{112,128},... | collective-permute-start | bytes 589832 | tf_op jit(solution)/shard_map/ppermute | solution.py:204
  27.4 1.0 %copy-start = (bf16[384,512]{1,0:T(8,128)(2,1)S(1)}, bf16[384,512]{1,0:T(8,128)(2,1)}, u32[]{:S(2)}) copy-start(bf16[384,512]{1,0:T(8,128)(2,1)} %qm_ref.5) | copy-start | bytes 1179652
  35.4 6.1 %collective-permute-start.3 = (bf16[1072,384]{1,0:T(8,128)(2,1)S(1)}, bf16[1072,384]{1,0:T(8,128)(2,1)S(1)}, u32[]{:S(2)}, u32[]{:S(2)}) collective-permute-start(bf16[1072,384]{1,0:T(8,128)(2,1)S(1)} %get-tuple-element.31), channel_id=1, source_target_pairs={{0,1},{1,0},{2,3},{3,2},{4,5},{5,4},{6,7},{7,6},{8,9},{9,8},{10,11... | collective-permute-start | bytes 2469896 | tf_op jit(solution)/shard_map/ppermute | solution.py:236
  45.5 16.6 %collective-permute-start.5 = (bf16[384,512]{1,0:T(8,128)(2,1)S(1)}, bf16[384,512]{1,0:T(8,128)(2,1)S(1)}, u32[]{:S(2)}, u32[]{:S(2)}) collective-permute-start(bf16[384,512]{1,0:T(8,128)(2,1)S(1)} %get-tuple-element.38), channel_id=1, source_target_pairs={{0,2},{1,15},{2,4},{3,1},{4,6},{5,3},{6,8},{7,5},{8,10},{9,7},{10,... | collective-permute-start | bytes 1179656 | tf_op jit(solution)/shard_map/ppermute | solution.py:289
  50.6 13.8 %collective-permute-start.6 = (bf16[384,512]{1,0:T(8,128)(2,1)S(1)}, bf16[384,512]{1,0:T(8,128)(2,1)S(1)}, u32[]{:S(2)}, u32[]{:S(2)}) collective-permute-start(bf16[384,512]{1,0:T(8,128)(2,1)S(1)} %get-tuple-element.39), channel_id=1, source_target_pairs={{0,4},{1,13},{2,6},{3,15},{4,8},{5,1},{6,10},{7,3},{8,12},{9,5},{1... | collective-permute-start | bytes 1179656 | tf_op jit(solution)/shard_map/ppermute | solution.py:288
  54.4 14.3 %collective-permute-start.7 = (bf16[384,512]{1,0:T(8,128)(2,1)S(1)}, bf16[384,512]{1,0:T(8,128)(2,1)S(1)}, u32[]{:S(2)}, u32[]{:S(2)}) collective-permute-start(bf16[384,512]{1,0:T(8,128)(2,1)S(1)} %get-tuple-element.44), channel_id=1, source_target_pairs={{0,2},{1,15},{2,4},{3,1},{4,6},{5,3},{6,8},{7,5},{8,10},{9,7},{10,... | collective-permute-start | bytes 1179656 | tf_op jit(solution)/shard_map/ppermute | solution.py:290
  64.5 8.8 %collective-permute-start.8 = (bf16[384,512]{1,0:T(8,128)(2,1)S(1)}, bf16[384,512]{1,0:T(8,128)(2,1)S(1)}, u32[]{:S(2)}, u32[]{:S(2)}) collective-permute-start(bf16[384,512]{1,0:T(8,128)(2,1)S(1)} %add_convert_fusion.4), channel_id=1, source_target_pairs={{0,2},{1,15},{2,4},{3,1},{4,6},{5,3},{6,8},{7,5},{8,10},{9,7},{10,... | collective-permute-start | bytes 1179656 | tf_op jit(solution)/shard_map/ppermute | solution.py:295
  68.8 9.1 %collective-permute-start.9 = (bf16[384,512]{1,0:T(8,128)(2,1)S(1)}, bf16[384,512]{1,0:T(8,128)(2,1)S(1)}, u32[]{:S(2)}, u32[]{:S(2)}) collective-permute-start(bf16[384,512]{1,0:T(8,128)(2,1)S(1)} %add_convert_fusion.3), channel_id=1, source_target_pairs={{0,2},{1,15},{2,4},{3,1},{4,6},{5,3},{6,8},{7,5},{8,10},{9,7},{10,... | collective-permute-start | bytes 1179656 | tf_op jit(solution)/shard_map/ppermute | solution.py:298
  73.4 10.5 %collective-permute-start.10 = (bf16[384,512]{1,0:T(8,128)(2,1)S(1)}, bf16[384,512]{1,0:T(8,128)(2,1)S(1)}, u32[]{:S(2)}, u32[]{:S(2)}) collective-permute-start(bf16[384,512]{1,0:T(8,128)(2,1)S(1)} %add_convert_fusion.2), channel_id=1, source_target_pairs={{0,2},{1,15},{2,4},{3,1},{4,6},{5,3},{6,8},{7,5},{8,10},{9,7},{10,... | collective-permute-start | bytes 1179656 | tf_op jit(solution)/shard_map/ppermute | solution.py:295
  77.9 12.7 %collective-permute-start.11 = (bf16[384,512]{1,0:T(8,128)(2,1)S(1)}, bf16[384,512]{1,0:T(8,128)(2,1)S(1)}, u32[]{:S(2)}, u32[]{:S(2)}) collective-permute-start(bf16[384,512]{1,0:T(8,128)(2,1)S(1)} %add_convert_fusion.1), channel_id=1, source_target_pairs={{0,3},{1,14},{2,5},{3,0},{4,7},{5,2},{6,9},{7,4},{8,11},{9,6},{10,... | collective-permute-start | bytes 1179656 | tf_op jit(solution)/shard_map/ppermute | solution.py:298

commit v7 on v5

--- a/solution.py
+++ b/solution.py
@@ -280,17 +280,18 @@
     near = lax.ppermute(farthest, axes, straight)
     now = part(columns_at(half - 1))
     far = lax.ppermute(now[1], axes, straight)
-    rest = part(jnp.concatenate([*(columns_at(distance) for distance in range(half - 2, 0, -1)), columns_at(0)[:1]]))
     for distance in range(half - 1, 0, -1):
         send = add(now[0], near)
         near = lax.ppermute(send, axes, straight)
         if distance > 1:
-            rest, send = lax.optimization_barrier((rest, send))
-            now, rest = rest[:2], rest[2:]
+            columns = columns_at(distance - 1)
+            if distance == 2:
+                columns = jnp.concatenate([columns, columns_at(0)[:1]])
+            now, send = lax.optimization_barrier((part(columns), send))
             send = add(now[1], far)
             far = lax.ppermute(send, axes, straight if distance > 2 else cross)
             now, send = lax.optimization_barrier((now, send))
-    return add(rest[0], near, far)
+    return add(now[2], near, far)
 
 
 def solution(mesh):

time: 90.1 us -> 89.8 us (level)
  the two profiles are of different devices: /device:TPU:6 before, /device:TPU:31 now
where the time goes in v7:
time: 89.8 us; the launch traced here: 89.3 us
  starting transfers between devices  43.9 us (49%)
  waiting for transfers between devices  21.6 us (24%)
  Pallas kernels  18.7 us (21%)
  other arithmetic  2.7 us (3%)
  local copies, waits for them, and re-layouts  1.95 us (2%)
    ppermute x3, waiting for transfers between devices, on_device(): near = lax.ppermute(send, axes, straight)  9.75 us
    pallas_call x3, Pallas kernels, part(): pl.pallas_call(functools.partial(project, count), out_shape=[jax.ShapeDty...  9.39 us
    ppermute x1, starting transfers between devices, on_device(): lax.ppermute(first, 'dp', [(i, i + 1) for i in range(dp_count - 1)])  8.54 us
    ppermute x2, starting transfers between devices, on_device(): far = lax.ppermute(send, axes, straight if distance > 2 else cross)  8.46 us
    ppermute x1, starting transfers between devices, on_device(): first = lax.ppermute(own, ('dp', 'core'), first_pairs)  7.62 us
    ppermute x3, starting transfers between devices, on_device(): near = lax.ppermute(send, axes, straight)  6.64 us
    pallas_call x2, Pallas kernels, on_device(): pl.pallas_call(functools.partial(attend_piece, which), out_shape=[state_s...  4.98 us
    ppermute x1, waiting for transfers between devices, on_device(): first = lax.ppermute(own, ('dp', 'core'), first_pairs)  4.72 us
  transfers between devices with their start and end apart: 12, of which 7 were waited for; matrix products, arithmetic and copies ran while one was open for 2% of the time, Pallas kernels for 19%

profile of v7, /device:TPU:31, one launch (start us, length us, event | category | flops | bytes accessed | tf_op | source)
XLA Modules:
  0.0 89.3 jit_solution(13722471823537447356)
XLA Ops:
  1.0 7.6 %collective-permute-start.1 = (bf16[384,256]{1,0:T(8,128)(2,1)S(1)}, bf16[384,256]{1,0:T(8,128)(2,1)S(1)}, u32[]{:S(2)}, u32[]{:S(2)}) collective-permute-start(bf16[384,256]{1,0:T(8,128)(2,1)S(1)} %pad_maximum_fusion.own_ref), channel_id=1, source_target_pairs={{0,16},{16,32},{32,48},{48,64},{64,80},{80,96},{96,112},{112,128},... | collective-permute-start | bytes 589832 | tf_op jit(solution)/shard_map/ppermute | solution.py:199
  8.6 1.9 %collective-permute-start = (bf16[384,512]{1,0:T(8,128)(2,1)}, bf16[384,512]{1,0:T(8,128)(2,1)S(1)}, u32[]{:S(2)}, u32[]{:S(2)}) collective-permute-start(bf16[384,512]{1,0:T(8,128)(2,1)} %qm_ref.5), channel_id=1, source_target_pairs={{0,1},{1,0},{2,3},{3,2},{4,5},{5,4},{6,7},{7,6},{8,9},{9,8},{10,11... | collective-permute-start | bytes 1179656 | tf_op jit(solution)/shard_map/ppermute | solution.py:201
  10.5 2.4 %collective-permute-start.4 = (bf16[512,8192]{1,0:T(8,128)(2,1)}, bf16[512,8192]{1,0:T(8,128)(2,1)}, u32[]{:S(2)}, u32[]{:S(2)}) collective-permute-start(bf16[512,8192]{1,0:T(8,128)(2,1)} %wm_ref.7), channel_id=1, source_target_pairs={{0,1},{1,0},{2,3},{3,2},{4,5},{5,4},{6,7},{7,6},{8,9},{9,8},{10,11... | collective-permute-start | bytes 25165832 | tf_op jit(solution)/shard_map/ppermute | solution.py:204
  14.1 4.7 %collective-permute-done.1.piece_ref = bf16[384,256]{1,0:T(8,128)(2,1)S(1)} collective-permute-done((bf16[384,256]{1,0:T(8,128)(2,1)S(1)}, bf16[384,256]{1,0:T(8,128)(2,1)S(1)}, u32[]{:S(2)}, u32[]{:S(2)}) %collective-permute-start.1) | collective-permute-done | bytes 196640 | tf_op jit(solution)/shard_map/ppermute | solution.py:199
  18.8 8.5 %collective-permute-start.2 = (bf16[384,256]{1,0:T(8,128)(2,1)S(1)}, bf16[384,256]{1,0:T(8,128)(2,1)S(1)}, u32[]{:S(2)}, u32[]{:S(2)}) collective-permute-start(bf16[384,256]{1,0:T(8,128)(2,1)S(1)} %collective-permute-done.1.piece_ref), channel_id=1, source_target_pairs={{0,16},{16,32},{32,48},{48,64},{64,80},{80,96},{96,112},{112,128},... | collective-permute-start | bytes 589832 | tf_op jit(solution)/shard_map/ppermute | solution.py:202
  28.4 2.2 %shard_map.55.state_ref = f32[1040,384]{1,0:T(8,128)S(1)} custom-call(s32[6]{0:T(128)S(1)} %pad_add_fusion.1.info_ref, bf16[384,512]{1,0:T(8,128)(2,1)S(1)} %copy-done, bf16[384,512]{1,0:T(8,128)(2,1)S(1)} %collective-permute-done.qo_ref, bf16[384,256]{1,0:T(8,128)(2,1)S(1)} %pad_maximum_fusion.own_ref), custom_call_target="tpu_custom_call" | custom-call | flops 60000002048 | bytes 4000000 | tf_op jit(solution)/shard_map/pallas_call | solution.py:215
  30.5 2.5 %shard_map.56.state_ref = f32[1040,384]{1,0:T(8,128)S(1)} custom-call(s32[6]{0:T(128)S(1)} %pad_add_fusion.1.info_ref, bf16[384,512]{1,0:T(8,128)(2,1)S(1)} %copy-done, bf16[384,512]{1,0:T(8,128)(2,1)S(1)} %collective-permute-done.qo_ref, bf16[384,256]{1,0:T(8,128)(2,1)S(1)} %collective-permute-done.1.piece_ref, f32[1040,384]{1,0:T(8,128)S(1)} %shard_map.55.state_ref), custom_call_target="tpu_custom_call" | custom-call | flops 60000002048 | bytes 6000000 | tf_op jit(solution)/shard_map/pallas_call | solution.py:225
  33.0 2.5 %shard_map.57 = (f32[1040,384]{1,0:T(8,128)S(1)}, bf16[1072,384]{1,0:T(8,128)(2,1)S(1)}) custom-call(s32[6]{0:T(128)S(1)} %pad_add_fusion.1.info_ref, bf16[384,512]{1,0:T(8,128)(2,1)S(1)} %copy-done, bf16[384,512]{1,0:T(8,128)(2,1)S(1)} %collective-permute-done.qo_ref, bf16[384,256]{1,0:T(8,128)(2,1)S(1)} %collective-permute-done.2.piece_ref, ...), custom_call_target="tpu_custom_call" | custom-call | flops 60000002048 | bytes 6000000 | tf_op jit(solution)/shard_map/pallas_call | solution.py:225
  35.5 4.2 %collective-permute-start.3 = (bf16[1072,384]{1,0:T(8,128)(2,1)S(1)}, bf16[1072,384]{1,0:T(8,128)(2,1)S(1)}, u32[]{:S(2)}, u32[]{:S(2)}) collective-permute-start(bf16[1072,384]{1,0:T(8,128)(2,1)S(1)} %get-tuple-element.29), channel_id=1, source_target_pairs={{0,1},{1,0},{2,3},{3,2},{4,5},{5,4},{6,7},{7,6},{8,9},{9,8},{10,11... | collective-permute-start | bytes 2469896 | tf_op jit(solution)/shard_map/ppermute | solution.py:234
  41.7 2.2 %shard_map.58 = (bf16[384,1024]{1,0:T(8,128)(2,1)S(1)}, bf16[384,512]{1,0:T(8,128)(2,1)S(1)}) custom-call(s32[1]{0:T(128)} %bitcast.3.columns_ref, f32[1040,384]{1,0:T(8,128)S(1)} %get-tuple-element.28.here_ref, bf16[1072,384]{1,0:T(8,128)(2,1)S(1)} %collective-permute-done.3.there_ref, bf16[512,8192]{1,0:T(8,128)(2,1)} %wm_ref.7, ...), custom_call_target="tpu_custom_call" | custom-call | flops 400000000 | bytes 5000000 | tf_op jit(solution)/shard_map/pallas_call | solution.py:245
  43.8 2.1 %collective-permute-start.5 = (bf16[384,512]{1,0:T(8,128)(2,1)S(1)}, bf16[384,512]{1,0:T(8,128)(2,1)S(1)}, u32[]{:S(2)}, u32[]{:S(2)}) collective-permute-start(bf16[384,512]{1,0:T(8,128)(2,1)S(1)} %get-tuple-element.37), channel_id=1, source_target_pairs={{0,2},{1,15},{2,4},{3,1},{4,6},{5,3},{6,8},{7,5},{8,10},{9,7},{10,... | collective-permute-start | bytes 1179656 | tf_op jit(solution)/shard_map/ppermute | solution.py:280
  45.9 2.9 %shard_map.61 = (bf16[384,512]{1,0:T(8,128)(2,1)S(1)}, bf16[384,512]{1,0:T(8,128)(2,1)S(1)}) custom-call(s32[2]{0:T(128)S(1)} %pad_add_fusion.3.columns_ref, bf16[384,1024]{1,0:T(8,128)(2,1)S(1)} %get-tuple-element.30.att_ref, bf16[512,8192]{1,0:T(8,128)(2,1)} %wm_ref.7, bf16[512,8192]{1,0:T(8,128)(2,1)} %collective-permute-done.4.wo_ref), custom_call_target="tpu_custom_call" | custom-call | flops 60000002048 | bytes 10000000 | tf_op jit(solution)/shard_map/pallas_call | solution.py:260
  48.9 2.1 %collective-permute-start.6 = (bf16[384,512]{1,0:T(8,128)(2,1)S(1)}, bf16[384,512]{1,0:T(8,128)(2,1)S(1)}, u32[]{:S(2)}, u32[]{:S(2)}) collective-permute-start(bf16[384,512]{1,0:T(8,128)(2,1)S(1)} %get-tuple-element.40), channel_id=1, source_target_pairs={{0,2},{1,15},{2,4},{3,1},{4,6},{5,3},{6,8},{7,5},{8,10},{9,7},{10,... | collective-permute-start | bytes 1179656 | tf_op jit(solution)/shard_map/ppermute | solution.py:282
  51.0 2.6 %collective-permute-done.5 = bf16[384,512]{1,0:T(8,128)(2,1)S(1)} collective-permute-done((bf16[384,512]{1,0:T(8,128)(2,1)S(1)}, bf16[384,512]{1,0:T(8,128)(2,1)S(1)}, u32[]{:S(2)}, u32[]{:S(2)}) %collective-permute-start.5) | collective-permute-done | bytes 393248 | tf_op jit(solution)/shard_map/ppermute | solution.py:280
  53.7 1.9 %collective-permute-start.7 = (bf16[384,512]{1,0:T(8,128)(2,1)S(1)}, bf16[384,512]{1,0:T(8,128)(2,1)S(1)}, u32[]{:S(2)}, u32[]{:S(2)}) collective-permute-start(bf16[384,512]{1,0:T(8,128)(2,1)S(1)} %add_convert_fusion.5), channel_id=1, source_target_pairs={{0,2},{1,15},{2,4},{3,1},{4,6},{5,3},{6,8},{7,5},{8,10},{9,7},{10,... | collective-permute-start | bytes 1179656 | tf_op jit(solution)/shard_map/ppermute | solution.py:285
  55.6 2.9 %shard_map.60 = (bf16[384,512]{1,0:T(8,128)(2,1)S(1)}, bf16[384,512]{1,0:T(8,128)(2,1)S(1)}) custom-call(s32[2]{0:T(128)S(1)} %pad_add_fusion.2.columns_ref, bf16[384,1024]{1,0:T(8,128)(2,1)S(1)} %get-tuple-element.30.att_ref, bf16[512,8192]{1,0:T(8,128)(2,1)} %wm_ref.7, bf16[512,8192]{1,0:T(8,128)(2,1)} %collective-permute-done.4.wo_ref), custom_call_target="tpu_custom_call" | custom-call | flops 60000002048 | bytes 10000000 | tf_op jit(solution)/shard_map/pallas_call | solution.py:260
  58.7 2.6 %collective-permute-start.8 = (bf16[384,512]{1,0:T(8,128)(2,1)S(1)}, bf16[384,512]{1,0:T(8,128)(2,1)S(1)}, u32[]{:S(2)}, u32[]{:S(2)}) collective-permute-start(bf16[384,512]{1,0:T(8,128)(2,1)S(1)} %add_convert_fusion.4), channel_id=1, source_target_pairs={{0,2},{1,15},{2,4},{3,1},{4,6},{5,3},{6,8},{7,5},{8,10},{9,7},{10,... | collective-permute-start | bytes 1179656 | tf_op jit(solution)/shard_map/ppermute | solution.py:292
  61.3 2.1 %collective-permute-done.7 = bf16[384,512]{1,0:T(8,128)(2,1)S(1)} collective-permute-done((bf16[384,512]{1,0:T(8,128)(2,1)S(1)}, bf16[384,512]{1,0:T(8,128)(2,1)S(1)}, u32[]{:S(2)}, u32[]{:S(2)}) %collective-permute-start.7) | collective-permute-done | bytes 393248 | tf_op jit(solution)/shard_map/ppermute | solution.py:285
  63.5 1.9 %collective-permute-start.9 = (bf16[384,512]{1,0:T(8,128)(2,1)S(1)}, bf16[384,512]{1,0:T(8,128)(2,1)S(1)}, u32[]{:S(2)}, u32[]{:S(2)}) collective-permute-start(bf16[384,512]{1,0:T(8,128)(2,1)S(1)} %add_convert_fusion.3), channel_id=1, source_target_pairs={{0,2},{1,15},{2,4},{3,1},{4,6},{5,3},{6,8},{7,5},{8,10},{9,7},{10,... | collective-permute-start | bytes 1179656 | tf_op jit(solution)/shard_map/ppermute | solution.py:285
  65.4 3.5 %shard_map.59 = (bf16[384,512]{1,0:T(8,128)(2,1)S(1)}, bf16[384,512]{1,0:T(8,128)(2,1)S(1)}, bf16[384,512]{1,0:T(8,128)(2,1)S(1)}) custom-call(s32[3]{0:T(128)S(1)} %pad_add_fusion.columns_ref, bf16[384,1024]{1,0:T(8,128)(2,1)S(1)} %get-tuple-element.30.att_ref, bf16[512,8192]{1,0:T(8,128)(2,1)} %wm_ref.7, bf16[512,8192]{1,0:T(8,128)(2,1)} %collective-permute-done.4.wo_ref), custom_call_target="tpu_custom_call" | custom-call | flops 60000002048 | bytes 10000000 | tf_op jit(solution)/shard_map/pallas_call | solution.py:260
  69.1 5.9 %collective-permute-start.11 = (bf16[384,512]{1,0:T(8,128)(2,1)S(1)}, bf16[384,512]{1,0:T(8,128)(2,1)S(1)}, u32[]{:S(2)}, u32[]{:S(2)}) collective-permute-start(bf16[384,512]{1,0:T(8,128)(2,1)S(1)} %add_convert_fusion.2), channel_id=1, source_target_pairs={{0,3},{1,14},{2,5},{3,0},{4,7},{5,2},{6,9},{7,4},{8,11},{9,6},{10,... | collective-permute-start | bytes 1179656 | tf_op jit(solution)/shard_map/ppermute | solution.py:292
  75.1 2.8 %collective-permute-start.10 = (bf16[384,512]{1,0:T(8,128)(2,1)S(1)}, bf16[384,512]{1,0:T(8,128)(2,1)S(1)}, u32[]{:S(2)}, u32[]{:S(2)}) collective-permute-start(bf16[384,512]{1,0:T(8,128)(2,1)S(1)} %add_convert_fusion.1), channel_id=1, source_target_pairs={{0,2},{1,15},{2,4},{3,1},{4,6},{5,3},{6,8},{7,5},{8,10},{9,7},{10,... | collective-permute-start | bytes 1179656 | tf_op jit(solution)/shard_map/ppermute | solution.py:285
  77.9 2.8 %collective-permute-done.11 = bf16[384,512]{1,0:T(8,128)(2,1)S(1)} collective-permute-done((bf16[384,512]{1,0:T(8,128)(2,1)S(1)}, bf16[384,512]{1,0:T(8,128)(2,1)S(1)}, u32[]{:S(2)}, u32[]{:S(2)}) %collective-permute-start.11) | collective-permute-done | bytes 393248 | tf_op jit(solution)/shard_map/ppermute | solution.py:292
  80.7 7.7 %collective-permute-done.10 = bf16[384,512]{1,0:T(8,128)(2,1)S(1)} collective-permute-done((bf16[384,512]{1,0:T(8,128)(2,1)S(1)}, bf16[384,512]{1,0:T(8,128)(2,1)S(1)}, u32[]{:S(2)}, u32[]{:S(2)}) %collective-permute-start.10) | collective-permute-done | bytes 393248 | tf_op jit(solution)/shard_map/ppermute | solution.py:285
  (25 shorter events, 6.4 us)
Async XLA Ops:
  1.0 17.8 %collective-permute-start.1 = (bf16[384,256]{1,0:T(8,128)(2,1)S(1)}, bf16[384,256]{1,0:T(8,128)(2,1)S(1)}, u32[]{:S(2)}, u32[]{:S(2)}) collective-permute-start(bf16[384,256]{1,0:T(8,128)(2,1)S(1)} %pad_maximum_fusion.own_ref), channel_id=1, source_target_pairs={{0,16},{16,32},{32,48},{48,64},{64,80},{80,96},{96,112},{112,128},... | collective-permute-start | bytes 589832 | tf_op jit(solution)/shard_map/ppermute | solution.py:199
  8.6 18.7 %collective-permute-start = (bf16[384,512]{1,0:T(8,128)(2,1)}, bf16[384,512]{1,0:T(8,128)(2,1)S(1)}, u32[]{:S(2)}, u32[]{:S(2)}) collective-permute-start(bf16[384,512]{1,0:T(8,128)(2,1)} %qm_ref.5), channel_id=1, source_target_pairs={{0,1},{1,0},{2,3},{3,2},{4,5},{5,4},{6,7},{7,6},{8,9},{9,8},{10,11... | collective-permute-start | bytes 1179656 | tf_op jit(solution)/shard_map/ppermute | solution.py:201
  10.5 31.1 %collective-permute-start.4 = (bf16[512,8192]{1,0:T(8,128)(2,1)}, bf16[512,8192]{1,0:T(8,128)(2,1)}, u32[]{:S(2)}, u32[]{:S(2)}) collective-permute-start(bf16[512,8192]{1,0:T(8,128)(2,1)} %wm_ref.7), channel_id=1, source_target_pairs={{0,1},{1,0},{2,3},{3,2},{4,5},{5,4},{6,7},{7,6},{8,9},{9,8},{10,11... | collective-permute-start | bytes 25165832 | tf_op jit(solution)/shard_map/ppermute | solution.py:204
  18.8 14.2 %collective-permute-start.2 = (bf16[384,256]{1,0:T(8,128)(2,1)S(1)}, bf16[384,256]{1,0:T(8,128)(2,1)S(1)}, u32[]{:S(2)}, u32[]{:S(2)}) collective-permute-start(bf16[384,256]{1,0:T(8,128)(2,1)S(1)} %collective-permute-done.1.piece_ref), channel_id=1, source_target_pairs={{0,16},{16,32},{32,48},{48,64},{64,80},{80,96},{96,112},{112,128},... | collective-permute-start | bytes 589832 | tf_op jit(solution)/shard_map/ppermute | solution.py:202
  27.4 1.0 %copy-start = (bf16[384,512]{1,0:T(8,128)(2,1)S(1)}, bf16[384,512]{1,0:T(8,128)(2,1)}, u32[]{:S(2)}) copy-start(bf16[384,512]{1,0:T(8,128)(2,1)} %qm_ref.5) | copy-start | bytes 1179652
  35.5 6.1 %collective-permute-start.3 = (bf16[1072,384]{1,0:T(8,128)(2,1)S(1)}, bf16[1072,384]{1,0:T(8,128)(2,1)S(1)}, u32[]{:S(2)}, u32[]{:S(2)}) collective-permute-start(bf16[1072,384]{1,0:T(8,128)(2,1)S(1)} %get-tuple-element.29), channel_id=1, source_target_pairs={{0,1},{1,0},{2,3},{3,2},{4,5},{5,4},{6,7},{7,6},{8,9},{9,8},{10,11... | collective-permute-start | bytes 2469896 | tf_op jit(solution)/shard_map/ppermute | solution.py:234
  43.8 9.7 %collective-permute-start.5 = (bf16[384,512]{1,0:T(8,128)(2,1)S(1)}, bf16[384,512]{1,0:T(8,128)(2,1)S(1)}, u32[]{:S(2)}, u32[]{:S(2)}) collective-permute-start(bf16[384,512]{1,0:T(8,128)(2,1)S(1)} %get-tuple-element.37), channel_id=1, source_target_pairs={{0,2},{1,15},{2,4},{3,1},{4,6},{5,3},{6,8},{7,5},{8,10},{9,7},{10,... | collective-permute-start | bytes 1179656 | tf_op jit(solution)/shard_map/ppermute | solution.py:280
  48.9 9.7 %collective-permute-start.6 = (bf16[384,512]{1,0:T(8,128)(2,1)S(1)}, bf16[384,512]{1,0:T(8,128)(2,1)S(1)}, u32[]{:S(2)}, u32[]{:S(2)}) collective-permute-start(bf16[384,512]{1,0:T(8,128)(2,1)S(1)} %get-tuple-element.40), channel_id=1, source_target_pairs={{0,2},{1,15},{2,4},{3,1},{4,6},{5,3},{6,8},{7,5},{8,10},{9,7},{10,... | collective-permute-start | bytes 1179656 | tf_op jit(solution)/shard_map/ppermute | solution.py:282
  53.7 9.7 %collective-permute-start.7 = (bf16[384,512]{1,0:T(8,128)(2,1)S(1)}, bf16[384,512]{1,0:T(8,128)(2,1)S(1)}, u32[]{:S(2)}, u32[]{:S(2)}) collective-permute-start(bf16[384,512]{1,0:T(8,128)(2,1)S(1)} %add_convert_fusion.5), channel_id=1, source_target_pairs={{0,2},{1,15},{2,4},{3,1},{4,6},{5,3},{6,8},{7,5},{8,10},{9,7},{10,... | collective-permute-start | bytes 1179656 | tf_op jit(solution)/shard_map/ppermute | solution.py:285
  58.7 10.3 %collective-permute-start.8 = (bf16[384,512]{1,0:T(8,128)(2,1)S(1)}, bf16[384,512]{1,0:T(8,128)(2,1)S(1)}, u32[]{:S(2)}, u32[]{:S(2)}) collective-permute-start(bf16[384,512]{1,0:T(8,128)(2,1)S(1)} %add_convert_fusion.4), channel_id=1, source_target_pairs={{0,2},{1,15},{2,4},{3,1},{4,6},{5,3},{6,8},{7,5},{8,10},{9,7},{10,... | collective-permute-start | bytes 1179656 | tf_op jit(solution)/shard_map/ppermute | solution.py:292
  63.5 11.4 %collective-permute-start.9 = (bf16[384,512]{1,0:T(8,128)(2,1)S(1)}, bf16[384,512]{1,0:T(8,128)(2,1)S(1)}, u32[]{:S(2)}, u32[]{:S(2)}) collective-permute-start(bf16[384,512]{1,0:T(8,128)(2,1)S(1)} %add_convert_fusion.3), channel_id=1, source_target_pairs={{0,2},{1,15},{2,4},{3,1},{4,6},{5,3},{6,8},{7,5},{8,10},{9,7},{10,... | collective-permute-start | bytes 1179656 | tf_op jit(solution)/shard_map/ppermute | solution.py:285
  69.1 11.6 %collective-permute-start.11 = (bf16[384,512]{1,0:T(8,128)(2,1)S(1)}, bf16[384,512]{1,0:T(8,128)(2,1)S(1)}, u32[]{:S(2)}, u32[]{:S(2)}) collective-permute-start(bf16[384,512]{1,0:T(8,128)(2,1)S(1)} %add_convert_fusion.2), channel_id=1, source_target_pairs={{0,3},{1,14},{2,5},{3,0},{4,7},{5,2},{6,9},{7,4},{8,11},{9,6},{10,... | collective-permute-start | bytes 1179656 | tf_op jit(solution)/shard_map/ppermute | solution.py:292
  75.1 13.3 %collective-permute-start.10 = (bf16[384,512]{1,0:T(8,128)(2,1)S(1)}, bf16[384,512]{1,0:T(8,128)(2,1)S(1)}, u32[]{:S(2)}, u32[]{:S(2)}) collective-permute-start(bf16[384,512]{1,0:T(8,128)(2,1)S(1)} %add_convert_fusion.1), channel_id=1, source_target_pairs={{0,2},{1,15},{2,4},{3,1},{4,6},{5,3},{6,8},{7,5},{8,10},{9,7},{10,... | collective-permute-start | bytes 1179656 | tf_op jit(solution)/shard_map/ppermute | solution.py:285

commit v8 on v6

--- a/solution.py
+++ b/solution.py
@@ -285,8 +285,8 @@
             total = total + b.astype(jnp.float32)
         return total.astype(jnp.bfloat16)
 
+    near = lax.ppermute(near, axes, straight)
     joining = [lax.ppermute(farthest, axes, carried(2, False))]
-    near = lax.ppermute(near, axes, straight)
     far = lax.ppermute(far, axes, straight)
     rest = part(jnp.concatenate([*(columns_at(distance) for distance in range(half - 2, 0, -1)), columns_at(0)[:1]]))
     for distance in range(half - 2, 0, -1):

time: 92 us -> 92 us (level)
  no operation moved by 1% of the time
where the time goes in v8:
time: 92 us; the launch traced here: 91.5 us
  starting transfers between devices  52.7 us (57%)
  waiting for transfers between devices  18.3 us (20%)
  Pallas kernels  15.7 us (17%)
  other arithmetic  2.51 us (3%)
  local copies, waits for them, and re-layouts  2.03 us (2%)
    ppermute x2, starting transfers between devices, on_device(): lax.ppermute(send, axes, straight if distance > 1 else carried(1, True))  10.4 us
    ppermute x1, starting transfers between devices, on_device(): lax.ppermute(first, 'dp', [(i, i + 1) for i in range(dp_count - 1)])  8.54 us
    ppermute x1, starting transfers between devices, on_device(): first = lax.ppermute(own, ('dp', 'core'), first_pairs)  7.62 us
    ppermute x2, waiting for transfers between devices, on_device(): lax.ppermute(send, axes, straight if distance > 1 else carried(1, True))  7.13 us
    ppermute x2, starting transfers between devices, on_device(): near = lax.ppermute(send, axes, straight)  5.79 us
    ppermute x1, starting transfers between devices, on_device(): near = lax.ppermute(near, axes, straight)  5.1 us
    pallas_call x2, Pallas kernels, on_device(): pl.pallas_call(functools.partial(attend_piece, which), out_shape=[state_s...  4.88 us
    ppermute x1, waiting for transfers between devices, on_device(): first = lax.ppermute(own, ('dp', 'core'), first_pairs)  4.72 us
  transfers between devices with their start and end apart: 12, of which 7 were waited for; matrix products, arithmetic and copies ran while one was open for 2% of the time, Pallas kernels for 13%

profile of v8, /device:TPU:7, one launch (start us, length us, event | category | flops | bytes accessed | tf_op | source)
XLA Modules:
  0.0 91.5 jit_solution(5874324349642682719)
XLA Ops:
  0.0 1.0 %constant_dynamic-slice_fusion = (bf16[384,128]{1,0:T(8,128)(2,1)S(1)}, bf16[384,128]{1,0:T(8,128)(2,1)S(1)}) fusion(bf16[384,1024]{1,0:T(8,128)(2,1)} %param.8, s32[]{:T(128)S(6)} %select_n.48, bf16[384,1024]{1,0:T(8,128)(2,1)} %param.7), kind=kLoop, calls=%fused_computation.17 | loop fusion | bytes 393220 | tf_op jit(solution)/shard_map/dynamic_slice | solution.py:196
  1.0 7.6 %collective-permute-start.1 = (bf16[384,256]{1,0:T(8,128)(2,1)S(1)}, bf16[384,256]{1,0:T(8,128)(2,1)S(1)}, u32[]{:S(2)}, u32[]{:S(2)}) collective-permute-start(bf16[384,256]{1,0:T(8,128)(2,1)S(1)} %pad_maximum_fusion.own_ref), channel_id=1, source_target_pairs={{0,16},{16,32},{32,48},{48,64},{64,80},{80,96},{96,112},{112,128},... | collective-permute-start | bytes 589832 | tf_op jit(solution)/shard_map/ppermute | solution.py:201
  8.6 1.9 %collective-permute-start = (bf16[384,512]{1,0:T(8,128)(2,1)}, bf16[384,512]{1,0:T(8,128)(2,1)S(1)}, u32[]{:S(2)}, u32[]{:S(2)}) collective-permute-start(bf16[384,512]{1,0:T(8,128)(2,1)} %qm_ref.5), channel_id=1, source_target_pairs={{0,1},{1,0},{2,3},{3,2},{4,5},{5,4},{6,7},{7,6},{8,9},{9,8},{10,11... | collective-permute-start | bytes 1179656 | tf_op jit(solution)/shard_map/ppermute | solution.py:203
  10.5 2.4 %collective-permute-start.4 = (bf16[512,8192]{1,0:T(8,128)(2,1)}, bf16[512,8192]{1,0:T(8,128)(2,1)}, u32[]{:S(2)}, u32[]{:S(2)}) collective-permute-start(bf16[512,8192]{1,0:T(8,128)(2,1)} %wm_ref.3), channel_id=1, source_target_pairs={{0,1},{1,0},{2,3},{3,2},{4,5},{5,4},{6,7},{7,6},{8,9},{9,8},{10,11... | collective-permute-start | bytes 25165832 | tf_op jit(solution)/shard_map/ppermute | solution.py:206
  14.1 4.7 %collective-permute-done.1.piece_ref = bf16[384,256]{1,0:T(8,128)(2,1)S(1)} collective-permute-done((bf16[384,256]{1,0:T(8,128)(2,1)S(1)}, bf16[384,256]{1,0:T(8,128)(2,1)S(1)}, u32[]{:S(2)}, u32[]{:S(2)}) %collective-permute-start.1) | collective-permute-done | bytes 196640 | tf_op jit(solution)/shard_map/ppermute | solution.py:201
  18.8 8.5 %collective-permute-start.2 = (bf16[384,256]{1,0:T(8,128)(2,1)S(1)}, bf16[384,256]{1,0:T(8,128)(2,1)S(1)}, u32[]{:S(2)}, u32[]{:S(2)}) collective-permute-start(bf16[384,256]{1,0:T(8,128)(2,1)S(1)} %collective-permute-done.1.piece_ref), channel_id=1, source_target_pairs={{0,16},{16,32},{32,48},{48,64},{64,80},{80,96},{96,112},{112,128},... | collective-permute-start | bytes 589832 | tf_op jit(solution)/shard_map/ppermute | solution.py:204
  27.4 1.0 %copy-done = bf16[384,512]{1,0:T(8,128)(2,1)S(1)} copy-done((bf16[384,512]{1,0:T(8,128)(2,1)S(1)}, bf16[384,512]{1,0:T(8,128)(2,1)}, u32[]{:S(2)}) %copy-start) | copy-done | bytes 393240
  28.4 2.2 %shard_map.55.state_ref = f32[1040,384]{1,0:T(8,128)S(1)} custom-call(s32[6]{0:T(128)S(1)} %pad_add_fusion.1.info_ref, bf16[384,512]{1,0:T(8,128)(2,1)S(1)} %copy-done, bf16[384,512]{1,0:T(8,128)(2,1)S(1)} %collective-permute-done.qo_ref, bf16[384,256]{1,0:T(8,128)(2,1)S(1)} %pad_maximum_fusion.own_ref), custom_call_target="tpu_custom_call" | custom-call | flops 60000002048 | bytes 4000000 | tf_op jit(solution)/shard_map/pallas_call | solution.py:217
  30.5 2.4 %shard_map.56.state_ref = f32[1040,384]{1,0:T(8,128)S(1)} custom-call(s32[6]{0:T(128)S(1)} %pad_add_fusion.1.info_ref, bf16[384,512]{1,0:T(8,128)(2,1)S(1)} %copy-done, bf16[384,512]{1,0:T(8,128)(2,1)S(1)} %collective-permute-done.qo_ref, bf16[384,256]{1,0:T(8,128)(2,1)S(1)} %collective-permute-done.1.piece_ref, f32[1040,384]{1,0:T(8,128)S(1)} %shard_map.55.state_ref), custom_call_target="tpu_custom_call" | custom-call | flops 60000002048 | bytes 6000000 | tf_op jit(solution)/shard_map/pallas_call | solution.py:227
  33.0 2.4 %shard_map.57 = (f32[1040,384]{1,0:T(8,128)S(1)}, bf16[1072,384]{1,0:T(8,128)(2,1)S(1)}) custom-call(s32[6]{0:T(128)S(1)} %pad_add_fusion.1.info_ref, bf16[384,512]{1,0:T(8,128)(2,1)S(1)} %copy-done, bf16[384,512]{1,0:T(8,128)(2,1)S(1)} %collective-permute-done.qo_ref, bf16[384,256]{1,0:T(8,128)(2,1)S(1)} %collective-permute-done.2.piece_ref, ...), custom_call_target="tpu_custom_call" | custom-call | flops 60000002048 | bytes 6000000 | tf_op jit(solution)/shard_map/pallas_call | solution.py:227
  35.4 4.2 %collective-permute-start.3 = (bf16[1072,384]{1,0:T(8,128)(2,1)S(1)}, bf16[1072,384]{1,0:T(8,128)(2,1)S(1)}, u32[]{:S(2)}, u32[]{:S(2)}) collective-permute-start(bf16[1072,384]{1,0:T(8,128)(2,1)S(1)} %get-tuple-element.31), channel_id=1, source_target_pairs={{0,1},{1,0},{2,3},{3,2},{4,5},{5,4},{6,7},{7,6},{8,9},{9,8},{10,11... | collective-permute-start | bytes 2469896 | tf_op jit(solution)/shard_map/ppermute | solution.py:236
  39.9 1.7 %collective-permute-done.3.there_ref = bf16[1072,384]{1,0:T(8,128)(2,1)S(1)} collective-permute-done((bf16[1072,384]{1,0:T(8,128)(2,1)S(1)}, bf16[1072,384]{1,0:T(8,128)(2,1)S(1)}, u32[]{:S(2)}, u32[]{:S(2)}) %collective-permute-start.3) | collective-permute-done | bytes 823328 | tf_op jit(solution)/shard_map/ppermute | solution.py:236
  41.6 3.9 %shard_map.58 = (bf16[384,1024]{1,0:T(8,128)(2,1)S(1)}, bf16[384,512]{1,0:T(8,128)(2,1)S(1)}, bf16[384,512]{1,0:T(8,128)(2,1)S(1)}, bf16[384,512]{1,0:T(8,128)(2,1)S(1)}) custom-call(s32[3]{0:T(128)S(1)} %pad_add_fusion.columns_ref, f32[1040,384]{1,0:T(8,128)S(1)} %get-tuple-element.30.here_ref, bf16[1072,384]{1,0:T(8,128)(2,1)S(1)} %collective-permute-done.3.there_ref, ...), custom_call_target="tpu_custom_call" | custom-call | flops 400000000 | bytes 5000000 | tf_op jit(solution)/shard_map/pallas_call | solution.py:247
  45.5 5.1 %collective-permute-start.5 = (bf16[384,512]{1,0:T(8,128)(2,1)S(1)}, bf16[384,512]{1,0:T(8,128)(2,1)S(1)}, u32[]{:S(2)}, u32[]{:S(2)}) collective-permute-start(bf16[384,512]{1,0:T(8,128)(2,1)S(1)} %get-tuple-element.38), channel_id=1, source_target_pairs={{0,2},{1,15},{2,4},{3,1},{4,6},{5,3},{6,8},{7,5},{8,10},{9,7},{10,... | collective-permute-start | bytes 1179656 | tf_op jit(solution)/shard_map/ppermute | solution.py:288
  50.6 3.8 %collective-permute-start.6 = (bf16[384,512]{1,0:T(8,128)(2,1)S(1)}, bf16[384,512]{1,0:T(8,128)(2,1)S(1)}, u32[]{:S(2)}, u32[]{:S(2)}) collective-permute-start(bf16[384,512]{1,0:T(8,128)(2,1)S(1)} %get-tuple-element.39), channel_id=1, source_target_pairs={{0,4},{1,13},{2,6},{3,15},{4,8},{5,1},{6,10},{7,3},{8,12},{9,5},{1... | collective-permute-start | bytes 1179656 | tf_op jit(solution)/shard_map/ppermute | solution.py:289
  54.4 3.0 %collective-permute-start.7 = (bf16[384,512]{1,0:T(8,128)(2,1)S(1)}, bf16[384,512]{1,0:T(8,128)(2,1)S(1)}, u32[]{:S(2)}, u32[]{:S(2)}) collective-permute-start(bf16[384,512]{1,0:T(8,128)(2,1)S(1)} %get-tuple-element.44), channel_id=1, source_target_pairs={{0,2},{1,15},{2,4},{3,1},{4,6},{5,3},{6,8},{7,5},{8,10},{9,7},{10,... | collective-permute-start | bytes 1179656 | tf_op jit(solution)/shard_map/ppermute | solution.py:290
  57.4 4.7 %shard_map.59 = (bf16[384,512]{1,0:T(8,128)(2,1)S(1)}, bf16[384,512]{1,0:T(8,128)(2,1)S(1)}, bf16[384,512]{1,0:T(8,128)(2,1)S(1)}, bf16[384,512]{1,0:T(8,128)(2,1)S(1)}, bf16[384,512]{1,0:T(8,128)(2,1)S(1)}) custom-call(s32[5]{0:T(128)S(1)} %concatenate.12.columns_ref, bf16[384,1024]{1,0:T(8,128)(2,1)S(1)} %get-tuple-element.32.att_ref, ...), custom_call_target="tpu_custom_call" | custom-call | flops 60000002048 | bytes 10000000 | tf_op jit(solution)/shard_map/pallas_call | solution.py:262
  62.1 2.3 %collective-permute-done.6 = bf16[384,512]{1,0:T(8,128)(2,1)S(1)} collective-permute-done((bf16[384,512]{1,0:T(8,128)(2,1)S(1)}, bf16[384,512]{1,0:T(8,128)(2,1)S(1)}, u32[]{:S(2)}, u32[]{:S(2)}) %collective-permute-start.6) | collective-permute-done | bytes 393248 | tf_op jit(solution)/shard_map/ppermute | solution.py:289
  64.5 1.9 %collective-permute-start.8 = (bf16[384,512]{1,0:T(8,128)(2,1)S(1)}, bf16[384,512]{1,0:T(8,128)(2,1)S(1)}, u32[]{:S(2)}, u32[]{:S(2)}) collective-permute-start(bf16[384,512]{1,0:T(8,128)(2,1)S(1)} %add_convert_fusion.4), channel_id=1, source_target_pairs={{0,2},{1,15},{2,4},{3,1},{4,6},{5,3},{6,8},{7,5},{8,10},{9,7},{10,... | collective-permute-start | bytes 1179656 | tf_op jit(solution)/shard_map/ppermute | solution.py:295
  66.5 2.2 %collective-permute-done.7 = bf16[384,512]{1,0:T(8,128)(2,1)S(1)} collective-permute-done((bf16[384,512]{1,0:T(8,128)(2,1)S(1)}, bf16[384,512]{1,0:T(8,128)(2,1)S(1)}, u32[]{:S(2)}, u32[]{:S(2)}) %collective-permute-start.7) | collective-permute-done | bytes 393248 | tf_op jit(solution)/shard_map/ppermute | solution.py:290
  68.8 4.3 %collective-permute-start.9 = (bf16[384,512]{1,0:T(8,128)(2,1)S(1)}, bf16[384,512]{1,0:T(8,128)(2,1)S(1)}, u32[]{:S(2)}, u32[]{:S(2)}) collective-permute-start(bf16[384,512]{1,0:T(8,128)(2,1)S(1)} %add_convert_fusion.3), channel_id=1, source_target_pairs={{0,2},{1,15},{2,4},{3,1},{4,6},{5,3},{6,8},{7,5},{8,10},{9,7},{10,... | collective-permute-start | bytes 1179656 | tf_op jit(solution)/shard_map/ppermute | solution.py:298
  73.4 3.9 %collective-permute-start.10 = (bf16[384,512]{1,0:T(8,128)(2,1)S(1)}, bf16[384,512]{1,0:T(8,128)(2,1)S(1)}, u32[]{:S(2)}, u32[]{:S(2)}) collective-permute-start(bf16[384,512]{1,0:T(8,128)(2,1)S(1)} %add_convert_fusion.2), channel_id=1, source_target_pairs={{0,2},{1,15},{2,4},{3,1},{4,6},{5,3},{6,8},{7,5},{8,10},{9,7},{10,... | collective-permute-start | bytes 1179656 | tf_op jit(solution)/shard_map/ppermute | solution.py:295
  77.9 6.0 %collective-permute-start.11 = (bf16[384,512]{1,0:T(8,128)(2,1)S(1)}, bf16[384,512]{1,0:T(8,128)(2,1)S(1)}, u32[]{:S(2)}, u32[]{:S(2)}) collective-permute-start(bf16[384,512]{1,0:T(8,128)(2,1)S(1)} %add_convert_fusion.1), channel_id=1, source_target_pairs={{0,3},{1,14},{2,5},{3,0},{4,7},{5,2},{6,9},{7,4},{8,11},{9,6},{10,... | collective-permute-start | bytes 1179656 | tf_op jit(solution)/shard_map/ppermute | solution.py:298
  84.0 6.6 %collective-permute-done.11 = bf16[384,512]{1,0:T(8,128)(2,1)S(1)} collective-permute-done((bf16[384,512]{1,0:T(8,128)(2,1)S(1)}, bf16[384,512]{1,0:T(8,128)(2,1)S(1)}, u32[]{:S(2)}, u32[]{:S(2)}) %collective-permute-start.11) | collective-permute-done | bytes 393248 | tf_op jit(solution)/shard_map/ppermute | solution.py:298
  (21 shorter events, 3.3 us)
Async XLA Ops:
  1.0 17.8 %collective-permute-start.1 = (bf16[384,256]{1,0:T(8,128)(2,1)S(1)}, bf16[384,256]{1,0:T(8,128)(2,1)S(1)}, u32[]{:S(2)}, u32[]{:S(2)}) collective-permute-start(bf16[384,256]{1,0:T(8,128)(2,1)S(1)} %pad_maximum_fusion.own_ref), channel_id=1, source_target_pairs={{0,16},{16,32},{32,48},{48,64},{64,80},{80,96},{96,112},{112,128},... | collective-permute-start | bytes 589832 | tf_op jit(solution)/shard_map/ppermute | solution.py:201
  8.6 18.7 %collective-permute-start = (bf16[384,512]{1,0:T(8,128)(2,1)}, bf16[384,512]{1,0:T(8,128)(2,1)S(1)}, u32[]{:S(2)}, u32[]{:S(2)}) collective-permute-start(bf16[384,512]{1,0:T(8,128)(2,1)} %qm_ref.5), channel_id=1, source_target_pairs={{0,1},{1,0},{2,3},{3,2},{4,5},{5,4},{6,7},{7,6},{8,9},{9,8},{10,11... | collective-permute-start | bytes 1179656 | tf_op jit(solution)/shard_map/ppermute | solution.py:203
  10.5 31.0 %collective-permute-start.4 = (bf16[512,8192]{1,0:T(8,128)(2,1)}, bf16[512,8192]{1,0:T(8,128)(2,1)}, u32[]{:S(2)}, u32[]{:S(2)}) collective-permute-start(bf16[512,8192]{1,0:T(8,128)(2,1)} %wm_ref.3), channel_id=1, source_target_pairs={{0,1},{1,0},{2,3},{3,2},{4,5},{5,4},{6,7},{7,6},{8,9},{9,8},{10,11... | collective-permute-start | bytes 25165832 | tf_op jit(solution)/shard_map/ppermute | solution.py:206
  18.8 14.2 %collective-permute-start.2 = (bf16[384,256]{1,0:T(8,128)(2,1)S(1)}, bf16[384,256]{1,0:T(8,128)(2,1)S(1)}, u32[]{:S(2)}, u32[]{:S(2)}) collective-permute-start(bf16[384,256]{1,0:T(8,128)(2,1)S(1)} %collective-permute-done.1.piece_ref), channel_id=1, source_target_pairs={{0,16},{16,32},{32,48},{48,64},{64,80},{80,96},{96,112},{112,128},... | collective-permute-start | bytes 589832 | tf_op jit(solution)/shard_map/ppermute | solution.py:204
  27.4 1.0 %copy-start = (bf16[384,512]{1,0:T(8,128)(2,1)S(1)}, bf16[384,512]{1,0:T(8,128)(2,1)}, u32[]{:S(2)}) copy-start(bf16[384,512]{1,0:T(8,128)(2,1)} %qm_ref.5) | copy-start | bytes 1179652
  35.4 6.1 %collective-permute-start.3 = (bf16[1072,384]{1,0:T(8,128)(2,1)S(1)}, bf16[1072,384]{1,0:T(8,128)(2,1)S(1)}, u32[]{:S(2)}, u32[]{:S(2)}) collective-permute-start(bf16[1072,384]{1,0:T(8,128)(2,1)S(1)} %get-tuple-element.31), channel_id=1, source_target_pairs={{0,1},{1,0},{2,3},{3,2},{4,5},{5,4},{6,7},{7,6},{8,9},{9,8},{10,11... | collective-permute-start | bytes 2469896 | tf_op jit(solution)/shard_map/ppermute | solution.py:236
  45.5 16.6 %collective-permute-start.5 = (bf16[384,512]{1,0:T(8,128)(2,1)S(1)}, bf16[384,512]{1,0:T(8,128)(2,1)S(1)}, u32[]{:S(2)}, u32[]{:S(2)}) collective-permute-start(bf16[384,512]{1,0:T(8,128)(2,1)S(1)} %get-tuple-element.38), channel_id=1, source_target_pairs={{0,2},{1,15},{2,4},{3,1},{4,6},{5,3},{6,8},{7,5},{8,10},{9,7},{10,... | collective-permute-start | bytes 1179656 | tf_op jit(solution)/shard_map/ppermute | solution.py:288
  50.6 13.8 %collective-permute-start.6 = (bf16[384,512]{1,0:T(8,128)(2,1)S(1)}, bf16[384,512]{1,0:T(8,128)(2,1)S(1)}, u32[]{:S(2)}, u32[]{:S(2)}) collective-permute-start(bf16[384,512]{1,0:T(8,128)(2,1)S(1)} %get-tuple-element.39), channel_id=1, source_target_pairs={{0,4},{1,13},{2,6},{3,15},{4,8},{5,1},{6,10},{7,3},{8,12},{9,5},{1... | collective-permute-start | bytes 1179656 | tf_op jit(solution)/shard_map/ppermute | solution.py:289
  54.4 14.3 %collective-permute-start.7 = (bf16[384,512]{1,0:T(8,128)(2,1)S(1)}, bf16[384,512]{1,0:T(8,128)(2,1)S(1)}, u32[]{:S(2)}, u32[]{:S(2)}) collective-permute-start(bf16[384,512]{1,0:T(8,128)(2,1)S(1)} %get-tuple-element.44), channel_id=1, source_target_pairs={{0,2},{1,15},{2,4},{3,1},{4,6},{5,3},{6,8},{7,5},{8,10},{9,7},{10,... | collective-permute-start | bytes 1179656 | tf_op jit(solution)/shard_map/ppermute | solution.py:290
  64.5 8.8 %collective-permute-start.8 = (bf16[384,512]{1,0:T(8,128)(2,1)S(1)}, bf16[384,512]{1,0:T(8,128)(2,1)S(1)}, u32[]{:S(2)}, u32[]{:S(2)}) collective-permute-start(bf16[384,512]{1,0:T(8,128)(2,1)S(1)} %add_convert_fusion.4), channel_id=1, source_target_pairs={{0,2},{1,15},{2,4},{3,1},{4,6},{5,3},{6,8},{7,5},{8,10},{9,7},{10,... | collective-permute-start | bytes 1179656 | tf_op jit(solution)/shard_map/ppermute | solution.py:295
  68.8 9.1 %collective-permute-start.9 = (bf16[384,512]{1,0:T(8,128)(2,1)S(1)}, bf16[384,512]{1,0:T(8,128)(2,1)S(1)}, u32[]{:S(2)}, u32[]{:S(2)}) collective-permute-start(bf16[384,512]{1,0:T(8,128)(2,1)S(1)} %add_convert_fusion.3), channel_id=1, source_target_pairs={{0,2},{1,15},{2,4},{3,1},{4,6},{5,3},{6,8},{7,5},{8,10},{9,7},{10,... | collective-permute-start | bytes 1179656 | tf_op jit(solution)/shard_map/ppermute | solution.py:298
  73.4 10.5 %collective-permute-start.10 = (bf16[384,512]{1,0:T(8,128)(2,1)S(1)}, bf16[384,512]{1,0:T(8,128)(2,1)S(1)}, u32[]{:S(2)}, u32[]{:S(2)}) collective-permute-start(bf16[384,512]{1,0:T(8,128)(2,1)S(1)} %add_convert_fusion.2), channel_id=1, source_target_pairs={{0,2},{1,15},{2,4},{3,1},{4,6},{5,3},{6,8},{7,5},{8,10},{9,7},{10,... | collective-permute-start | bytes 1179656 | tf_op jit(solution)/shard_map/ppermute | solution.py:295
  77.9 12.7 %collective-permute-start.11 = (bf16[384,512]{1,0:T(8,128)(2,1)S(1)}, bf16[384,512]{1,0:T(8,128)(2,1)S(1)}, u32[]{:S(2)}, u32[]{:S(2)}) collective-permute-start(bf16[384,512]{1,0:T(8,128)(2,1)S(1)} %add_convert_fusion.1), channel_id=1, source_target_pairs={{0,3},{1,14},{2,5},{3,0},{4,7},{5,2},{6,9},{7,4},{8,11},{9,6},{10,... | collective-permute-start | bytes 1179656 | tf_op jit(solution)/shard_map/ppermute | solution.py:298

commit v9 on v7

--- a/solution.py
+++ b/solution.py
@@ -117,13 +117,17 @@
         factor = jnp.exp2((old_top - top) * EXP_SCALE)
         total = old_total * factor + jnp.sum(weights, axis=0, keepdims=True)
         accum = old_accum * factor + weighted(v_piece, weights)
-        store_state(out_ref, pair, unit, top, total, accum)
-        if message_ref is not None:
+        if message_ref is None:
+            store_state(out_ref, pair, unit, top, total, accum)
+        else:
             for side in range(2):
                 at = pl.ds((2 * pair + side) * HD, HD), pl.ds(unit * UNIT, UNIT)
-                message_ref[at] = accum[:, side * UNIT : (side + 1) * UNIT].astype(jnp.bfloat16)
+                part = slice(side * UNIT, (side + 1) * UNIT)
+                message_ref[at] = accum[:, part].astype(jnp.bfloat16)
+                out_ref[pl.ds(2 * pair + side, 1), at[1]] = top[:, part]
+                out_ref[pl.ds(8 + 2 * pair + side, 1), at[1]] = total[:, part]
     if message_ref is not None:
-        rest = out_ref[STATS:, :]
+        rest = out_ref[...]
         for term in range(3):
             rounded = rest.astype(jnp.bfloat16)
             message_ref[pl.ds(STATS + 16 * term, 16), :] = rounded
@@ -143,12 +147,12 @@
     return jnp.dot(att_ref[...], w_buf[block], preferred_element_type=jnp.float32).astype(jnp.bfloat16)
 
 
-def combine(columns_ref, here_ref, there_ref, wm_ref, wo_ref, att_ref, out_ref, w_buf, sems):
+def combine(columns_ref, stats_ref, here_ref, there_ref, wm_ref, wo_ref, att_ref, out_ref, w_buf, sems):
     heads = 8
     copies = fetch(columns_ref, 0, (wm_ref, wo_ref), w_buf, sems)
     for copy in copies:
         copy.start()
-    here = here_ref[STATS:, :]
+    here = stats_ref[...]
     there = sum(there_ref[pl.ds(STATS + 16 * term, 16), :].astype(jnp.float32) for term in (2, 1, 0))
     for head in range(heads):
         other = (head + heads // 2) % heads
@@ -157,7 +161,7 @@
         share_a = jnp.exp2((top_a - top) * EXP_SCALE)
         share_b = jnp.exp2((top_b - top) * EXP_SCALE)
         total = here[heads + head : heads + head + 1] * share_a + there[heads + other : heads + other + 1] * share_b
-        accum = here_ref[pl.ds(head * HD, HD), :] * share_a
+        accum = here_ref[pl.ds(head * HD, HD), :].astype(jnp.float32) * share_a
         accum += there_ref[pl.ds(other * HD, HD), :].astype(jnp.float32) * share_b
         att_ref[:, head * HD : (head + 1) * HD] = jnp.transpose(accum / total).astype(jnp.bfloat16)
     for copy in copies:
@@ -220,17 +224,18 @@
         compiler_params=LIMIT,
         cost_estimate=pl.CostEstimate(flops=OWN_FLOPS, bytes_accessed=4_000_000, transcendentals=1_000_000),
     )(info, queries, q_other, own)
+    stats_shape = jax.ShapeDtypeStruct((16, rows), jnp.float32)
     message_shape = jax.ShapeDtypeStruct((2 * wide + 48, rows), jnp.bfloat16)
     for which, piece in enumerate((first, second)):
         state = pl.pallas_call(
             functools.partial(attend_piece, which),
-            out_shape=[state_shape, message_shape][: which + 1],
+            out_shape=[state_shape] if which == 0 else [stats_shape, message_shape],
             in_specs=[SM, VM, VM, VM, VM],
             out_specs=[VM, VM][: which + 1],
             compiler_params=LIMIT,
             cost_estimate=pl.CostEstimate(flops=PIECE_FLOPS[which], bytes_accessed=6_000_000, transcendentals=1_000_000),
         )(info, queries, q_other, piece, state[0])
-    state, message = state
+    stats, message = state
     there = lax.ppermute(message, "core", swap)
     half = y_count // 2
     way = 1 - 2 * core
@@ -248,12 +253,12 @@
             jax.ShapeDtypeStruct((rows, 2 * wide), jnp.bfloat16),
             jax.ShapeDtypeStruct((rows, wide), jnp.bfloat16),
         ],
-        in_specs=[SM, VM, VM, HBM, HBM],
+        in_specs=[SM, VM, VM, VM, HBM, HBM],
         out_specs=[VM, VM],
         scratch_shapes=w_scratch(1),
         compiler_params=WIDE_LIMIT,
         cost_estimate=pl.CostEstimate(flops=400_000_000, bytes_accessed=5_000_000, transcendentals=10_000),
-    )(columns_at(half)[:1], state, there, out_weight, w_other)
+    )(columns_at(half)[:1], stats, message, there, out_weight, w_other)
 
     def part(columns):
         count = columns.shape[0]

time: 89.8 us -> 89.4 us (level)
  no operation moved by 1% of the time
where the time goes in v9:
time: 89.4 us; the launch traced here: 88.9 us
  starting transfers between devices  43.9 us (49%)
  waiting for transfers between devices  21.5 us (24%)
  Pallas kernels  18.4 us (21%)
  other arithmetic  2.71 us (3%)
  local copies, waits for them, and re-layouts  1.95 us (2%)
    ppermute x3, waiting for transfers between devices, on_device(): near = lax.ppermute(send, axes, straight)  9.7 us
    pallas_call x3, Pallas kernels, part(): pl.pallas_call(functools.partial(project, count), out_shape=[jax.ShapeDty...  9.45 us
    ppermute x1, starting transfers between devices, on_device(): lax.ppermute(first, 'dp', [(i, i + 1) for i in range(dp_count - 1)])  8.54 us
    ppermute x2, starting transfers between devices, on_device(): far = lax.ppermute(send, axes, straight if distance > 2 else cross)  8.5 us
    ppermute x1, starting transfers between devices, on_device(): first = lax.ppermute(own, ('dp', 'core'), first_pairs)  7.62 us
    ppermute x3, starting transfers between devices, on_device(): near = lax.ppermute(send, axes, straight)  6.64 us
    pallas_call x2, Pallas kernels, on_device(): pl.pallas_call(functools.partial(attend_piece, which), out_shape=[state_s...  4.96 us
    ppermute x1, waiting for transfers between devices, on_device(): first = lax.ppermute(own, ('dp', 'core'), first_pairs)  4.72 us
  transfers between devices with their start and end apart: 12, of which 7 were waited for; matrix products, arithmetic and copies ran while one was open for 2% of the time, Pallas kernels for 19%

profile of v9, /device:TPU:31, one launch (start us, length us, event | category | flops | bytes accessed | tf_op | source)
XLA Modules:
  0.0 88.9 jit_solution(2769434231362727155)
XLA Ops:
  1.0 7.6 %collective-permute-start.1 = (bf16[384,256]{1,0:T(8,128)(2,1)S(1)}, bf16[384,256]{1,0:T(8,128)(2,1)S(1)}, u32[]{:S(2)}, u32[]{:S(2)}) collective-permute-start(bf16[384,256]{1,0:T(8,128)(2,1)S(1)} %pad_maximum_fusion.own_ref), channel_id=1, source_target_pairs={{0,16},{16,32},{32,48},{48,64},{64,80},{80,96},{96,112},{112,128},... | collective-permute-start | bytes 589832 | tf_op jit(solution)/shard_map/ppermute | solution.py:203
  8.6 1.9 %collective-permute-start = (bf16[384,512]{1,0:T(8,128)(2,1)}, bf16[384,512]{1,0:T(8,128)(2,1)S(1)}, u32[]{:S(2)}, u32[]{:S(2)}) collective-permute-start(bf16[384,512]{1,0:T(8,128)(2,1)} %qm_ref.5), channel_id=1, source_target_pairs={{0,1},{1,0},{2,3},{3,2},{4,5},{5,4},{6,7},{7,6},{8,9},{9,8},{10,11... | collective-permute-start | bytes 1179656 | tf_op jit(solution)/shard_map/ppermute | solution.py:205
  10.5 2.4 %collective-permute-start.4 = (bf16[512,8192]{1,0:T(8,128)(2,1)}, bf16[512,8192]{1,0:T(8,128)(2,1)}, u32[]{:S(2)}, u32[]{:S(2)}) collective-permute-start(bf16[512,8192]{1,0:T(8,128)(2,1)} %wm_ref.7), channel_id=1, source_target_pairs={{0,1},{1,0},{2,3},{3,2},{4,5},{5,4},{6,7},{7,6},{8,9},{9,8},{10,11... | collective-permute-start | bytes 25165832 | tf_op jit(solution)/shard_map/ppermute | solution.py:208
  14.1 4.7 %collective-permute-done.1.piece_ref = bf16[384,256]{1,0:T(8,128)(2,1)S(1)} collective-permute-done((bf16[384,256]{1,0:T(8,128)(2,1)S(1)}, bf16[384,256]{1,0:T(8,128)(2,1)S(1)}, u32[]{:S(2)}, u32[]{:S(2)}) %collective-permute-start.1) | collective-permute-done | bytes 196640 | tf_op jit(solution)/shard_map/ppermute | solution.py:203
  18.8 8.5 %collective-permute-start.2 = (bf16[384,256]{1,0:T(8,128)(2,1)S(1)}, bf16[384,256]{1,0:T(8,128)(2,1)S(1)}, u32[]{:S(2)}, u32[]{:S(2)}) collective-permute-start(bf16[384,256]{1,0:T(8,128)(2,1)S(1)} %collective-permute-done.1.piece_ref), channel_id=1, source_target_pairs={{0,16},{16,32},{32,48},{48,64},{64,80},{80,96},{96,112},{112,128},... | collective-permute-start | bytes 589832 | tf_op jit(solution)/shard_map/ppermute | solution.py:206
  28.4 2.2 %shard_map.55.state_ref = f32[1040,384]{1,0:T(8,128)S(1)} custom-call(s32[6]{0:T(128)S(1)} %pad_add_fusion.1.info_ref, bf16[384,512]{1,0:T(8,128)(2,1)S(1)} %copy-done, bf16[384,512]{1,0:T(8,128)(2,1)S(1)} %collective-permute-done.qo_ref, bf16[384,256]{1,0:T(8,128)(2,1)S(1)} %pad_maximum_fusion.own_ref), custom_call_target="tpu_custom_call" | custom-call | flops 60000002048 | bytes 4000000 | tf_op jit(solution)/shard_map/pallas_call | solution.py:219
  30.5 2.5 %shard_map.56.state_ref = f32[1040,384]{1,0:T(8,128)S(1)} custom-call(s32[6]{0:T(128)S(1)} %pad_add_fusion.1.info_ref, bf16[384,512]{1,0:T(8,128)(2,1)S(1)} %copy-done, bf16[384,512]{1,0:T(8,128)(2,1)S(1)} %collective-permute-done.qo_ref, bf16[384,256]{1,0:T(8,128)(2,1)S(1)} %collective-permute-done.1.piece_ref, f32[1040,384]{1,0:T(8,128)S(1)} %shard_map.55.state_ref), custom_call_target="tpu_custom_call" | custom-call | flops 60000002048 | bytes 6000000 | tf_op jit(solution)/shard_map/pallas_call | solution.py:230
  33.0 2.5 %shard_map.57 = (f32[16,384]{1,0:T(8,128)S(1)}, bf16[1072,384]{1,0:T(8,128)(2,1)S(1)}) custom-call(s32[6]{0:T(128)S(1)} %pad_add_fusion.1.info_ref, bf16[384,512]{1,0:T(8,128)(2,1)S(1)} %copy-done, bf16[384,512]{1,0:T(8,128)(2,1)S(1)} %collective-permute-done.qo_ref, bf16[384,256]{1,0:T(8,128)(2,1)S(1)} %collective-permute-done.2.piece_ref, ...), custom_call_target="tpu_custom_call" | custom-call | flops 60000002048 | bytes 6000000 | tf_op jit(solution)/shard_map/pallas_call | solution.py:230
  35.5 4.1 %collective-permute-start.3 = (bf16[1072,384]{1,0:T(8,128)(2,1)S(1)}, bf16[1072,384]{1,0:T(8,128)(2,1)S(1)}, u32[]{:S(2)}, u32[]{:S(2)}) collective-permute-start(bf16[1072,384]{1,0:T(8,128)(2,1)S(1)} %get-tuple-element.29.here_ref), channel_id=1, source_target_pairs={{0,1},{1,0},{2,3},{3,2},{4,5},{5,4},{6,7},{7,6},{8,9},{9,8},{10,11... | collective-permute-start | bytes 2469896 | tf_op jit(solution)/shard_map/ppermute | solution.py:239
  41.6 1.8 %shard_map.58 = (bf16[384,1024]{1,0:T(8,128)(2,1)S(1)}, bf16[384,512]{1,0:T(8,128)(2,1)S(1)}) custom-call(s32[1]{0:T(128)} %bitcast.3.columns_ref, f32[16,384]{1,0:T(8,128)S(1)} %get-tuple-element.28.stats_ref, bf16[1072,384]{1,0:T(8,128)(2,1)S(1)} %get-tuple-element.29.here_ref, bf16[1072,384]{1,0:T(8,128)(2,1)S(1)} %collective-permute-done.3.there_ref, ...), custom_call_target="tpu_custom_call" | custom-call | flops 400000000 | bytes 5000000 | tf_op jit(solution)/shard_map/pallas_call | solution.py:250
  43.4 2.1 %collective-permute-start.5 = (bf16[384,512]{1,0:T(8,128)(2,1)S(1)}, bf16[384,512]{1,0:T(8,128)(2,1)S(1)}, u32[]{:S(2)}, u32[]{:S(2)}) collective-permute-start(bf16[384,512]{1,0:T(8,128)(2,1)S(1)} %get-tuple-element.37), channel_id=1, source_target_pairs={{0,2},{1,15},{2,4},{3,1},{4,6},{5,3},{6,8},{7,5},{8,10},{9,7},{10,... | collective-permute-start | bytes 1179656 | tf_op jit(solution)/shard_map/ppermute | solution.py:285
  45.5 3.0 %shard_map.61 = (bf16[384,512]{1,0:T(8,128)(2,1)S(1)}, bf16[384,512]{1,0:T(8,128)(2,1)S(1)}) custom-call(s32[2]{0:T(128)S(1)} %pad_add_fusion.3.columns_ref, bf16[384,1024]{1,0:T(8,128)(2,1)S(1)} %get-tuple-element.30.att_ref, bf16[512,8192]{1,0:T(8,128)(2,1)} %wm_ref.7, bf16[512,8192]{1,0:T(8,128)(2,1)} %collective-permute-done.4.wo_ref), custom_call_target="tpu_custom_call" | custom-call | flops 60000002048 | bytes 10000000 | tf_op jit(solution)/shard_map/pallas_call | solution.py:265
  48.5 2.1 %collective-permute-start.6 = (bf16[384,512]{1,0:T(8,128)(2,1)S(1)}, bf16[384,512]{1,0:T(8,128)(2,1)S(1)}, u32[]{:S(2)}, u32[]{:S(2)}) collective-permute-start(bf16[384,512]{1,0:T(8,128)(2,1)S(1)} %get-tuple-element.40), channel_id=1, source_target_pairs={{0,2},{1,15},{2,4},{3,1},{4,6},{5,3},{6,8},{7,5},{8,10},{9,7},{10,... | collective-permute-start | bytes 1179656 | tf_op jit(solution)/shard_map/ppermute | solution.py:287
  50.6 2.6 %collective-permute-done.5 = bf16[384,512]{1,0:T(8,128)(2,1)S(1)} collective-permute-done((bf16[384,512]{1,0:T(8,128)(2,1)S(1)}, bf16[384,512]{1,0:T(8,128)(2,1)S(1)}, u32[]{:S(2)}, u32[]{:S(2)}) %collective-permute-start.5) | collective-permute-done | bytes 393248 | tf_op jit(solution)/shard_map/ppermute | solution.py:285
  53.3 1.9 %collective-permute-start.7 = (bf16[384,512]{1,0:T(8,128)(2,1)S(1)}, bf16[384,512]{1,0:T(8,128)(2,1)S(1)}, u32[]{:S(2)}, u32[]{:S(2)}) collective-permute-start(bf16[384,512]{1,0:T(8,128)(2,1)S(1)} %add_convert_fusion.5), channel_id=1, source_target_pairs={{0,2},{1,15},{2,4},{3,1},{4,6},{5,3},{6,8},{7,5},{8,10},{9,7},{10,... | collective-permute-start | bytes 1179656 | tf_op jit(solution)/shard_map/ppermute | solution.py:290
  55.2 3.0 %shard_map.60 = (bf16[384,512]{1,0:T(8,128)(2,1)S(1)}, bf16[384,512]{1,0:T(8,128)(2,1)S(1)}) custom-call(s32[2]{0:T(128)S(1)} %pad_add_fusion.2.columns_ref, bf16[384,1024]{1,0:T(8,128)(2,1)S(1)} %get-tuple-element.30.att_ref, bf16[512,8192]{1,0:T(8,128)(2,1)} %wm_ref.7, bf16[512,8192]{1,0:T(8,128)(2,1)} %collective-permute-done.4.wo_ref), custom_call_target="tpu_custom_call" | custom-call | flops 60000002048 | bytes 10000000 | tf_op jit(solution)/shard_map/pallas_call | solution.py:265
  58.3 2.6 %collective-permute-start.8 = (bf16[384,512]{1,0:T(8,128)(2,1)S(1)}, bf16[384,512]{1,0:T(8,128)(2,1)S(1)}, u32[]{:S(2)}, u32[]{:S(2)}) collective-permute-start(bf16[384,512]{1,0:T(8,128)(2,1)S(1)} %add_convert_fusion.4), channel_id=1, source_target_pairs={{0,2},{1,15},{2,4},{3,1},{4,6},{5,3},{6,8},{7,5},{8,10},{9,7},{10,... | collective-permute-start | bytes 1179656 | tf_op jit(solution)/shard_map/ppermute | solution.py:297
  60.9 2.0 %collective-permute-done.7 = bf16[384,512]{1,0:T(8,128)(2,1)S(1)} collective-permute-done((bf16[384,512]{1,0:T(8,128)(2,1)S(1)}, bf16[384,512]{1,0:T(8,128)(2,1)S(1)}, u32[]{:S(2)}, u32[]{:S(2)}) %collective-permute-start.7) | collective-permute-done | bytes 393248 | tf_op jit(solution)/shard_map/ppermute | solution.py:290
  63.1 1.9 %collective-permute-start.9 = (bf16[384,512]{1,0:T(8,128)(2,1)S(1)}, bf16[384,512]{1,0:T(8,128)(2,1)S(1)}, u32[]{:S(2)}, u32[]{:S(2)}) collective-permute-start(bf16[384,512]{1,0:T(8,128)(2,1)S(1)} %add_convert_fusion.3), channel_id=1, source_target_pairs={{0,2},{1,15},{2,4},{3,1},{4,6},{5,3},{6,8},{7,5},{8,10},{9,7},{10,... | collective-permute-start | bytes 1179656 | tf_op jit(solution)/shard_map/ppermute | solution.py:290
  65.0 3.5 %shard_map.59 = (bf16[384,512]{1,0:T(8,128)(2,1)S(1)}, bf16[384,512]{1,0:T(8,128)(2,1)S(1)}, bf16[384,512]{1,0:T(8,128)(2,1)S(1)}) custom-call(s32[3]{0:T(128)S(1)} %pad_add_fusion.columns_ref, bf16[384,1024]{1,0:T(8,128)(2,1)S(1)} %get-tuple-element.30.att_ref, bf16[512,8192]{1,0:T(8,128)(2,1)} %wm_ref.7, bf16[512,8192]{1,0:T(8,128)(2,1)} %collective-permute-done.4.wo_ref), custom_call_target="tpu_custom_call" | custom-call | flops 60000002048 | bytes 10000000 | tf_op jit(solution)/shard_map/pallas_call | solution.py:265
  68.7 5.9 %collective-permute-start.11 = (bf16[384,512]{1,0:T(8,128)(2,1)S(1)}, bf16[384,512]{1,0:T(8,128)(2,1)S(1)}, u32[]{:S(2)}, u32[]{:S(2)}) collective-permute-start(bf16[384,512]{1,0:T(8,128)(2,1)S(1)} %add_convert_fusion.2), channel_id=1, source_target_pairs={{0,3},{1,14},{2,5},{3,0},{4,7},{5,2},{6,9},{7,4},{8,11},{9,6},{10,... | collective-permute-start | bytes 1179656 | tf_op jit(solution)/shard_map/ppermute | solution.py:297
  74.7 2.8 %collective-permute-start.10 = (bf16[384,512]{1,0:T(8,128)(2,1)S(1)}, bf16[384,512]{1,0:T(8,128)(2,1)S(1)}, u32[]{:S(2)}, u32[]{:S(2)}) collective-permute-start(bf16[384,512]{1,0:T(8,128)(2,1)S(1)} %add_convert_fusion.1), channel_id=1, source_target_pairs={{0,2},{1,15},{2,4},{3,1},{4,6},{5,3},{6,8},{7,5},{8,10},{9,7},{10,... | collective-permute-start | bytes 1179656 | tf_op jit(solution)/shard_map/ppermute | solution.py:290
  77.5 2.8 %collective-permute-done.11 = bf16[384,512]{1,0:T(8,128)(2,1)S(1)} collective-permute-done((bf16[384,512]{1,0:T(8,128)(2,1)S(1)}, bf16[384,512]{1,0:T(8,128)(2,1)S(1)}, u32[]{:S(2)}, u32[]{:S(2)}) %collective-permute-start.11) | collective-permute-done | bytes 393248 | tf_op jit(solution)/shard_map/ppermute | solution.py:297
  80.3 7.7 %collective-permute-done.10 = bf16[384,512]{1,0:T(8,128)(2,1)S(1)} collective-permute-done((bf16[384,512]{1,0:T(8,128)(2,1)S(1)}, bf16[384,512]{1,0:T(8,128)(2,1)S(1)}, u32[]{:S(2)}, u32[]{:S(2)}) %collective-permute-start.10) | collective-permute-done | bytes 393248 | tf_op jit(solution)/shard_map/ppermute | solution.py:290
  (25 shorter events, 6.4 us)
Async XLA Ops:
  1.0 17.8 %collective-permute-start.1 = (bf16[384,256]{1,0:T(8,128)(2,1)S(1)}, bf16[384,256]{1,0:T(8,128)(2,1)S(1)}, u32[]{:S(2)}, u32[]{:S(2)}) collective-permute-start(bf16[384,256]{1,0:T(8,128)(2,1)S(1)} %pad_maximum_fusion.own_ref), channel_id=1, source_target_pairs={{0,16},{16,32},{32,48},{48,64},{64,80},{80,96},{96,112},{112,128},... | collective-permute-start | bytes 589832 | tf_op jit(solution)/shard_map/ppermute | solution.py:203
  8.6 18.7 %collective-permute-start = (bf16[384,512]{1,0:T(8,128)(2,1)}, bf16[384,512]{1,0:T(8,128)(2,1)S(1)}, u32[]{:S(2)}, u32[]{:S(2)}) collective-permute-start(bf16[384,512]{1,0:T(8,128)(2,1)} %qm_ref.5), channel_id=1, source_target_pairs={{0,1},{1,0},{2,3},{3,2},{4,5},{5,4},{6,7},{7,6},{8,9},{9,8},{10,11... | collective-permute-start | bytes 1179656 | tf_op jit(solution)/shard_map/ppermute | solution.py:205
  10.5 31.1 %collective-permute-start.4 = (bf16[512,8192]{1,0:T(8,128)(2,1)}, bf16[512,8192]{1,0:T(8,128)(2,1)}, u32[]{:S(2)}, u32[]{:S(2)}) collective-permute-start(bf16[512,8192]{1,0:T(8,128)(2,1)} %wm_ref.7), channel_id=1, source_target_pairs={{0,1},{1,0},{2,3},{3,2},{4,5},{5,4},{6,7},{7,6},{8,9},{9,8},{10,11... | collective-permute-start | bytes 25165832 | tf_op jit(solution)/shard_map/ppermute | solution.py:208
  18.8 14.2 %collective-permute-start.2 = (bf16[384,256]{1,0:T(8,128)(2,1)S(1)}, bf16[384,256]{1,0:T(8,128)(2,1)S(1)}, u32[]{:S(2)}, u32[]{:S(2)}) collective-permute-start(bf16[384,256]{1,0:T(8,128)(2,1)S(1)} %collective-permute-done.1.piece_ref), channel_id=1, source_target_pairs={{0,16},{16,32},{32,48},{48,64},{64,80},{80,96},{96,112},{112,128},... | collective-permute-start | bytes 589832 | tf_op jit(solution)/shard_map/ppermute | solution.py:206
  27.4 1.0 %copy-start = (bf16[384,512]{1,0:T(8,128)(2,1)S(1)}, bf16[384,512]{1,0:T(8,128)(2,1)}, u32[]{:S(2)}) copy-start(bf16[384,512]{1,0:T(8,128)(2,1)} %qm_ref.5) | copy-start | bytes 1179652
  35.5 6.1 %collective-permute-start.3 = (bf16[1072,384]{1,0:T(8,128)(2,1)S(1)}, bf16[1072,384]{1,0:T(8,128)(2,1)S(1)}, u32[]{:S(2)}, u32[]{:S(2)}) collective-permute-start(bf16[1072,384]{1,0:T(8,128)(2,1)S(1)} %get-tuple-element.29.here_ref), channel_id=1, source_target_pairs={{0,1},{1,0},{2,3},{3,2},{4,5},{5,4},{6,7},{7,6},{8,9},{9,8},{10,11... | collective-permute-start | bytes 2469896 | tf_op jit(solution)/shard_map/ppermute | solution.py:239
  43.4 9.7 %collective-permute-start.5 = (bf16[384,512]{1,0:T(8,128)(2,1)S(1)}, bf16[384,512]{1,0:T(8,128)(2,1)S(1)}, u32[]{:S(2)}, u32[]{:S(2)}) collective-permute-start(bf16[384,512]{1,0:T(8,128)(2,1)S(1)} %get-tuple-element.37), channel_id=1, source_target_pairs={{0,2},{1,15},{2,4},{3,1},{4,6},{5,3},{6,8},{7,5},{8,10},{9,7},{10,... | collective-permute-start | bytes 1179656 | tf_op jit(solution)/shard_map/ppermute | solution.py:285
  48.5 9.7 %collective-permute-start.6 = (bf16[384,512]{1,0:T(8,128)(2,1)S(1)}, bf16[384,512]{1,0:T(8,128)(2,1)S(1)}, u32[]{:S(2)}, u32[]{:S(2)}) collective-permute-start(bf16[384,512]{1,0:T(8,128)(2,1)S(1)} %get-tuple-element.40), channel_id=1, source_target_pairs={{0,2},{1,15},{2,4},{3,1},{4,6},{5,3},{6,8},{7,5},{8,10},{9,7},{10,... | collective-permute-start | bytes 1179656 | tf_op jit(solution)/shard_map/ppermute | solution.py:287
  53.3 9.7 %collective-permute-start.7 = (bf16[384,512]{1,0:T(8,128)(2,1)S(1)}, bf16[384,512]{1,0:T(8,128)(2,1)S(1)}, u32[]{:S(2)}, u32[]{:S(2)}) collective-permute-start(bf16[384,512]{1,0:T(8,128)(2,1)S(1)} %add_convert_fusion.5), channel_id=1, source_target_pairs={{0,2},{1,15},{2,4},{3,1},{4,6},{5,3},{6,8},{7,5},{8,10},{9,7},{10,... | collective-permute-start | bytes 1179656 | tf_op jit(solution)/shard_map/ppermute | solution.py:290
  58.3 10.3 %collective-permute-start.8 = (bf16[384,512]{1,0:T(8,128)(2,1)S(1)}, bf16[384,512]{1,0:T(8,128)(2,1)S(1)}, u32[]{:S(2)}, u32[]{:S(2)}) collective-permute-start(bf16[384,512]{1,0:T(8,128)(2,1)S(1)} %add_convert_fusion.4), channel_id=1, source_target_pairs={{0,2},{1,15},{2,4},{3,1},{4,6},{5,3},{6,8},{7,5},{8,10},{9,7},{10,... | collective-permute-start | bytes 1179656 | tf_op jit(solution)/shard_map/ppermute | solution.py:297
  63.1 11.5 %collective-permute-start.9 = (bf16[384,512]{1,0:T(8,128)(2,1)S(1)}, bf16[384,512]{1,0:T(8,128)(2,1)S(1)}, u32[]{:S(2)}, u32[]{:S(2)}) collective-permute-start(bf16[384,512]{1,0:T(8,128)(2,1)S(1)} %add_convert_fusion.3), channel_id=1, source_target_pairs={{0,2},{1,15},{2,4},{3,1},{4,6},{5,3},{6,8},{7,5},{8,10},{9,7},{10,... | collective-permute-start | bytes 1179656 | tf_op jit(solution)/shard_map/ppermute | solution.py:290
  68.7 11.6 %collective-permute-start.11 = (bf16[384,512]{1,0:T(8,128)(2,1)S(1)}, bf16[384,512]{1,0:T(8,128)(2,1)S(1)}, u32[]{:S(2)}, u32[]{:S(2)}) collective-permute-start(bf16[384,512]{1,0:T(8,128)(2,1)S(1)} %add_convert_fusion.2), channel_id=1, source_target_pairs={{0,3},{1,14},{2,5},{3,0},{4,7},{5,2},{6,9},{7,4},{8,11},{9,6},{10,... | collective-permute-start | bytes 1179656 | tf_op jit(solution)/shard_map/ppermute | solution.py:297
  74.7 13.3 %collective-permute-start.10 = (bf16[384,512]{1,0:T(8,128)(2,1)S(1)}, bf16[384,512]{1,0:T(8,128)(2,1)S(1)}, u32[]{:S(2)}, u32[]{:S(2)}) collective-permute-start(bf16[384,512]{1,0:T(8,128)(2,1)S(1)} %add_convert_fusion.1), channel_id=1, source_target_pairs={{0,2},{1,15},{2,4},{3,1},{4,6},{5,3},{6,8},{7,5},{8,10},{9,7},{10,... | collective-permute-start | bytes 1179656 | tf_op jit(solution)/shard_map/ppermute | solution.py:290
